TPU v7x, 32 devices: a whole 2x2x4 slice. The times are simulated.
32 devices in a mesh: dp: 8 (over y, x, core), head: 4 (over z).
Axes of the slice: x: 2, y: 2, z: 4, core: 2. Of those that a mesh axis runs over, the one named last changes fastest.
Arguments:
- tokens: bfloat16 [16384, 1024], P(('dp', 'head')), may hold values from -6 to 6
- attn_query: bfloat16 [1024, 1024], P(None, 'head'), may hold values from -0.1875 to 0.1875
- attn_key: bfloat16 [1024, 1024], P(None, 'head'), may hold values from -0.1875 to 0.1875
- attn_value: bfloat16 [1024, 1024], P(None, 'head'), may hold values from -0.1875 to 0.1875
- attn_gate: bfloat16 [1024, 1024], P(None, 'head'), may hold values from -0.1875 to 0.1875
- attn_out: bfloat16 [1024, 1024], P('head'), may hold values from -0.1875 to 0.1875
- rotation_rates: float32 [1024], P('head'), may hold values from 0.0005 to 1
- ffn_left: bfloat16 [1024, 2816], P(None, 'head'), may hold values from -0.1875 to 0.1875
- ffn_right: bfloat16 [1024, 2816], P(None, 'head'), may hold values from -0.1875 to 0.1875
- ffn_down: bfloat16 [2816, 1024], P('head'), may hold values from -0.109375 to 0.109375
- out_grad: bfloat16 [16384, 1024], P(('dp', 'head')), may hold values from -6 to 6
Outputs:
- block_out: bfloat16 [16384, 1024], P(('dp', 'head'))
- input_grad: float32 [16384, 1024], P(('dp', 'head'))
- query_grad: float32 [1024, 1024], P(None, 'head')
- key_grad: float32 [1024, 1024], P(None, 'head')
- value_grad: float32 [1024, 1024], P(None, 'head')
- gate_grad: float32 [1024, 1024], P(None, 'head')
- out_proj_grad: float32 [1024, 1024], P('head')
- rates_grad: float32 [1024], P('head')
- left_grad: float32 [1024, 2816], P(None, 'head')
- right_grad: float32 [1024, 2816], P(None, 'head')
- down_grad: float32 [2816, 1024], P('head')
All inputs are finite; a program needn't handle non-finite values.
Results may differ from a plain program's by a relative error of at most 0.025.
The roundings to bfloat16 on the way count: a program that leaves them out, or rounds other values in their place, can miss the bound.
Values may be sent and summed in bfloat16 or wider, within the bound.
A program may use at most 192 MiB of HBM per device.

v0:
```python
import jax
import jax.numpy as jnp
from jax import lax
from jax.sharding import PartitionSpec as P

D = 1024
HEADS = 8
HEAD_DIM = 128
SPAN = 256


EPSILON = 1e-06
HIGHEST = lax.Precision.HIGHEST


def norm_parts(values):
    scale = lax.rsqrt(jnp.mean(values * values, axis=-1, keepdims=True) + EPSILON)
    return (values * scale, scale)


def norm_back(normed, scale, grad):
    return scale * (grad - normed * jnp.mean(grad * normed, axis=-1, keepdims=True))


def plain_dot(left, right):
    return jnp.dot(left, right, preferred_element_type=jnp.float32)


def first_dot(left, right):
    return lax.dot_general(
        left, right, (((0,), (0,)), ((), ())), preferred_element_type=jnp.float32
    )


def second_dot(left, right):
    return lax.dot_general(
        left, right, (((1,), (1,)), ((), ())), preferred_element_type=jnp.float32
    )


def on_device(
    tokens,
    attn_query,
    attn_key,
    attn_value,
    attn_gate,
    attn_out,
    rotation_rates,
    ffn_left,
    ffn_right,
    ffn_down,
    out_grad,
):
    inputs = tokens.astype(jnp.float32)
    normed_one, scale_one = norm_parts(inputs)
    gathered_in = lax.all_gather(normed_one.astype(jnp.bfloat16), "head", axis=0, tiled=True)
    length = gathered_in.shape[0]
    local_width = attn_query.shape[1]
    heads_here = local_width // HEAD_DIM
    query_pre = plain_dot(gathered_in, attn_query)
    key_pre = plain_dot(gathered_in, attn_key)
    value_pre = plain_dot(gathered_in, attn_value)
    gate_pre = plain_dot(gathered_in, attn_gate)
    positions = jnp.arange(length, dtype=jnp.float32)
    angles = (positions[:, None] * rotation_rates[None, :]).reshape(length, heads_here, HEAD_DIM)
    cosines = jnp.cos(angles)
    sines = jnp.sin(angles)

    def rotate(values):
        activated = jax.nn.silu(values).reshape(length, heads_here, HEAD_DIM)
        return jnp.concatenate([activated * cosines, activated * sines], axis=-1).astype(
            jnp.bfloat16
        )

    spans = length // SPAN

    def blocks(array):
        return array.reshape(spans, SPAN, heads_here, array.shape[-1])

    query_blocks = blocks(rotate(query_pre))
    key_blocks = blocks(rotate(key_pre))
    value_blocks = blocks(value_pre.astype(jnp.bfloat16).reshape(length, heads_here, HEAD_DIM))
    first_head = lax.axis_index("head") * heads_here
    head_ids = (first_head + jnp.arange(heads_here)).astype(jnp.float32)
    rates = jnp.exp2(-8.0 * (head_ids + 1.0) / HEADS)
    places = jnp.arange(SPAN, dtype=jnp.float32)
    offsets = places[:, None] - places[None, :]
    decay_mask = jnp.where(
        offsets[None] >= 0.0, jnp.exp(-rates[:, None, None] * jnp.maximum(offsets[None], 0.0)), 0.0
    )
    query_decay = jnp.exp(-rates[None, :] * (places[:, None] + 1.0))[None, :, :, None]
    key_decay = jnp.exp(-rates[None, :] * (SPAN - 1.0 - places[:, None]))[None, :, :, None]
    span_decay = jnp.exp(-rates * SPAN)[:, None, None]
    scores = jnp.einsum(
        "nihd,njhd->nhij", query_blocks, key_blocks, preferred_element_type=jnp.float32
    )
    weights = (scores * decay_mask[None]).astype(jnp.bfloat16)
    inner = jnp.einsum("nhij,njhe->nihe", weights, value_blocks, preferred_element_type=jnp.float32)
    query_wide = query_blocks.astype(jnp.float32) * query_decay
    key_wide = key_blocks.astype(jnp.float32) * key_decay
    value_wide = value_blocks.astype(jnp.float32)
    fresh = jnp.einsum("njhd,njhe->nhde", key_wide, value_wide, precision=HIGHEST)

    def advance(current, fresh_term):
        return (span_decay * current + fresh_term, current)

    zero_state = jnp.zeros((heads_here, 2 * HEAD_DIM, HEAD_DIM), jnp.float32)
    final_state, states = lax.scan(advance, zero_state, fresh)
    outer = jnp.einsum("nihd,nhde->nihe", query_wide, states, precision=HIGHEST)
    attn = (inner + outer).reshape(length, local_width)
    local_squares = jnp.sum(attn * attn, axis=-1)
    total_squares = lax.psum(local_squares, "head")
    scale_attn = lax.rsqrt(total_squares / D + EPSILON)[:, None]
    attn_normed = attn * scale_attn
    gated = (attn_normed * gate_pre).astype(jnp.bfloat16)
    hidden = inputs + lax.psum_scatter(
        plain_dot(gated, attn_out).astype(jnp.bfloat16), "head", scatter_dimension=0, tiled=True
    ).astype(jnp.float32)
    normed_two, scale_two = norm_parts(hidden)
    gathered_mid = lax.all_gather(normed_two.astype(jnp.bfloat16), "head", axis=0, tiled=True)
    left = plain_dot(gathered_mid, ffn_left)
    right = plain_dot(gathered_mid, ffn_right)
    product = (left * right).astype(jnp.bfloat16)
    result = hidden + lax.psum_scatter(
        plain_dot(product, ffn_down).astype(jnp.bfloat16), "head", scatter_dimension=0, tiled=True
    ).astype(jnp.float32)
    block_out = result.astype(jnp.bfloat16)
    grad_rows = lax.all_gather(out_grad, "head", axis=0, tiled=True)
    down_grad = first_dot(product, grad_rows)
    grad_product = second_dot(grad_rows, ffn_down)
    grad_left = (grad_product * right).astype(jnp.bfloat16)
    grad_right = (grad_product * left).astype(jnp.bfloat16)
    left_grad = first_dot(gathered_mid, grad_left)
    right_grad = first_dot(gathered_mid, grad_right)
    grad_mid = lax.psum_scatter(
        (second_dot(grad_left, ffn_left) + second_dot(grad_right, ffn_right)).astype(jnp.bfloat16),
        "head",
        scatter_dimension=0,
        tiled=True,
    ).astype(jnp.float32)
    grad_hidden = out_grad.astype(jnp.float32) + norm_back(normed_two, scale_two, grad_mid)
    branch_rows = lax.all_gather(grad_hidden.astype(jnp.bfloat16), "head", axis=0, tiled=True)
    out_proj_grad = first_dot(gated, branch_rows)
    grad_gated = second_dot(branch_rows, attn_out)
    grad_normed = grad_gated * gate_pre
    grad_gate_pre = (grad_gated * attn_normed).astype(jnp.bfloat16)
    local_products = jnp.sum(grad_normed * attn_normed, axis=-1)
    total_products = lax.psum(local_products, "head")
    grad_attn = (scale_attn * (grad_normed - attn_normed * (total_products / D)[:, None])).astype(
        jnp.bfloat16
    )
    grad_blocks = blocks(grad_attn.reshape(length, heads_here, HEAD_DIM))
    grad_wide = grad_blocks.astype(jnp.float32)
    grad_weights = jnp.einsum(
        "nihe,njhe->nhij", grad_blocks, value_blocks, preferred_element_type=jnp.float32
    )
    grad_scores = (grad_weights * decay_mask[None]).astype(jnp.bfloat16)
    grad_values = jnp.einsum(
        "nhij,nihe->njhe", weights, grad_blocks, preferred_element_type=jnp.float32
    )
    grad_query = jnp.einsum(
        "nhij,njhd->nihd", grad_scores, key_blocks, preferred_element_type=jnp.float32
    )
    grad_keys = jnp.einsum(
        "nhij,nihd->njhd", grad_scores, query_blocks, preferred_element_type=jnp.float32
    )
    grad_query = grad_query + query_decay * jnp.einsum(
        "nihe,nhde->nihd", grad_wide, states, precision=HIGHEST
    )
    grad_states = jnp.einsum("nihd,nihe->nhde", query_wide, grad_wide, precision=HIGHEST)

    def retreat(pending, grad_term):
        return (span_decay * pending + grad_term, pending)

    final_pending, later = lax.scan(retreat, zero_state, grad_states, reverse=True)
    grad_keys = grad_keys + key_decay * jnp.einsum(
        "njhe,nhde->njhd", value_wide, later, precision=HIGHEST
    )
    grad_values = grad_values + jnp.einsum("njhd,nhde->njhe", key_wide, later, precision=HIGHEST)

    def unrotate(grad_rotated, pre_values):
        shaped = grad_rotated.reshape(length, heads_here, 2 * HEAD_DIM)
        grad_cos = shaped[:, :, :HEAD_DIM]
        grad_sin = shaped[:, :, HEAD_DIM:]
        activated = jax.nn.silu(pre_values).reshape(length, heads_here, HEAD_DIM)
        grad_act = (grad_cos * cosines + grad_sin * sines).reshape(length, local_width)
        grad_angle = (activated * (grad_sin * cosines - grad_cos * sines)).reshape(
            length, local_width
        )
        sigmoid_pre = jax.nn.sigmoid(pre_values)
        grad_pre = grad_act * sigmoid_pre * (1.0 + pre_values * (1.0 - sigmoid_pre))
        return (grad_pre.astype(jnp.bfloat16), grad_angle)

    grad_query_pre, angle_query = unrotate(grad_query, query_pre)
    grad_key_pre, angle_key = unrotate(grad_keys, key_pre)
    grad_value_pre = grad_values.reshape(length, local_width).astype(jnp.bfloat16)
    rates_grad = jnp.sum(positions[:, None] * (angle_query + angle_key), axis=0)
    query_grad = first_dot(gathered_in, grad_query_pre)
    key_grad = first_dot(gathered_in, grad_key_pre)
    value_grad = first_dot(gathered_in, grad_value_pre)
    gate_grad = first_dot(gathered_in, grad_gate_pre)
    total = second_dot(grad_query_pre, attn_query)
    total = total + second_dot(grad_key_pre, attn_key)
    total = total + second_dot(grad_value_pre, attn_value)
    grad_in = lax.psum_scatter(
        (total + second_dot(grad_gate_pre, attn_gate)).astype(jnp.bfloat16),
        "head",
        scatter_dimension=0,
        tiled=True,
    ).astype(jnp.float32)
    input_grad = grad_hidden + norm_back(normed_one, scale_one, grad_in)
    (
        query_grad,
        key_grad,
        value_grad,
        gate_grad,
        out_proj_grad,
        rates_grad,
        left_grad,
        right_grad,
        down_grad,
    ) = lax.psum(
        (
            query_grad,
            key_grad,
            value_grad,
            gate_grad,
            out_proj_grad,
            rates_grad,
            left_grad,
            right_grad,
            down_grad,
        ),
        "dp",
    )
    return (
        block_out,
        input_grad,
        query_grad,
        key_grad,
        value_grad,
        gate_grad,
        out_proj_grad,
        rates_grad,
        left_grad,
        right_grad,
        down_grad,
    )


def solution(mesh):
    return jax.shard_map(
        on_device,
        mesh=mesh,
        in_specs=(
            P(("dp", "head"), None),
            P(None, "head"),
            P(None, "head"),
            P(None, "head"),
            P(None, "head"),
            P("head", None),
            P("head"),
            P(None, "head"),
            P(None, "head"),
            P("head", None),
            P(("dp", "head"), None),
        ),
        out_specs=(
            P(("dp", "head"), None),
            P(("dp", "head"), None),
            P(None, "head"),
            P(None, "head"),
            P(None, "head"),
            P(None, "head"),
            P("head", None),
            P("head"),
            P(None, "head"),
            P(None, "head"),
            P("head", None),
        ),
        check_vma=False,
    )
```

profile of v0, /device:TPU:1, one launch (start us, length us, event | category | flops | bytes accessed | tf_op | source)
XLA Modules:
  0.0 1090.0 jit_solution(13052763207052877043)
XLA Ops:
  8.9 2.5 fusion.16
  11.9 82.5 %all-gather.5.cloned.1.call-done = bf16[2048,1024]{1,0:T(8,128)(2,1)} async-done(((bf16[512,1024]{1,0:T(8,128)(2,1)}), bf16[2048,1024]{1,0:T(8,128)(2,1)}) %all-gather.5.cloned.1.call-update) | async-done | bytes 4194320 | tf_op jit(solution)/shard_map/all_gather | solution.py:56
  94.4 5.0 fusion.39
  99.4 2.2 copy.69
  101.7 3.1 copy.39
  104.8 5.0 fusion.38
  109.8 2.2 copy.70
  112.0 3.0 copy.41
  115.0 4.4 convolution_convert_fusion.2
  120.8 11.1 %fusion.25 = (bf16[8,256,2,128]{3,1,2,0:T(8,128)(2,1)S(1)}, bf16[8,256,2,128]{3,1,2,0:T(8,128)(2,1)S(1)}, bf16[8,256,2,128]{3,1,2,0:T(8,128)(2,1)S(1)}, bf16[8,256,2,128]{3,1,2,0:T(8,128)(2,1)S(1)}) fusion(f32[8,256,2,128]{3,1,2,0:T(8,128)} %copy.39, f32[2,128]{1,0:T(2,128)S(1)} %bitcast.163, f32[8,256]{1,0:T(8,128)S(1)} %multiply_add_fusion.2, ...), kind=kLoop, calls=%fused_computation.51 | loop fusion | flops 4718592 | bytes 8397824 | tf_op jit(solution)/shard_map/convert.2
  133.2 2.2 fusion.47
  135.4 4.9 fusion.9
  141.8 14.7 %while.30 = (s32[]{:T(128)}, f32[2,256,128]{2,1,0:T(8,128)S(1)}, f32[8,2,256,128]{3,2,1,0:T(8,128)}, f32[8,2,256,128]{3,2,1,0:T(8,128)}, s32[]{:T(128)}, /*index=5*/s32[]{:T(128)}, s32[]{:T(128)}) while((s32[]{:T(128)}, f32[2,256,128]{2,1,0:T(8,128)S(1)}, f32[8,2,256,128]{3,2,1,0:T(8,128)}, f32[8,2,256,128]{3,2,1,0:T(8,128)}, ...), condition=%wide.region_2.3_spmd.clone, body=%wide.region_1.2_spmd.clone.sunk | while | flops 262159 | bytes 1311344 | solution.py:108
  156.5 6.5 multiply_reduce_fusion.3
  164.2 2.2 copy.71
  166.5 7.3 psum.77
  173.8 5.6 multiply_convert_fusion.7
  179.4 3.3 convolution_convert_fusion.1
  182.7 77.8 %reduce-scatter.5.cloned.1.call-done = bf16[512,1024]{1,0:T(8,128)(2,1)} async-done(((bf16[2048,1024]{1,0:T(8,128)(2,1)}), bf16[512,1024]{1,0:T(8,128)(2,1)}) %reduce-scatter.5.cloned.1.call-update) | async-done | bytes 1048592 | tf_op jit(solution)/shard_map/reduce_scatter | solution.py:116
  264.7 80.3 %all-gather.7.cloned.1.call-done = bf16[2048,1024]{1,0:T(8,128)(2,1)} async-done(((bf16[512,1024]{1,0:T(8,128)(2,1)}), bf16[2048,1024]{1,0:T(8,128)(2,1)}) %all-gather.7.cloned.1.call-update) | async-done | bytes 4194320 | tf_op jit(solution)/shard_map/all_gather | solution.py:120
  345.0 8.5 fusion.57
  353.5 4.9 fusion.58
  358.4 67.4 %all-gather.9.cloned.1.call-done = bf16[2048,1024]{1,0:T(8,128)(2,1)} async-done(((bf16[512,1024]{1,0:T(8,128)(2,1)}), bf16[2048,1024]{1,0:T(8,128)(2,1)}) %all-gather.9.cloned.1.call-update) | async-done | bytes 4194320 | tf_op jit(solution)/shard_map/all_gather | solution.py:128
  425.8 8.7 multiply_convert_fusion
  434.5 3.5 fusion.59
  438.1 5.3 add_convert_fusion.1
  443.6 75.3 %reduce-scatter.9.cloned.1.call-done = bf16[512,1024]{1,0:T(8,128)(2,1)} async-done(((bf16[2048,1024]{1,0:T(8,128)(2,1)}), bf16[512,1024]{1,0:T(8,128)(2,1)}) %reduce-scatter.9.cloned.1.call-update) | async-done | bytes 1048592 | tf_op jit(solution)/shard_map/reduce_scatter | solution.py:135
  518.8 2.0 fusion.17
  521.4 1.8 fusion.56
  523.2 2.9 copy.62
  526.1 2.9 copy.63
  529.1 75.5 %all-gather.11.cloned.1.call-done = bf16[2048,1024]{1,0:T(8,128)(2,1)} async-done(((bf16[512,1024]{1,0:T(8,128)(2,1)}), bf16[2048,1024]{1,0:T(8,128)(2,1)}) %all-gather.11.cloned.1.call-update) | async-done | bytes 4194320 | tf_op jit(solution)/shard_map/all_gather | solution.py:142
  604.6 6.6 multiply_reduce_fusion.1
  611.2 7.3 psum.78
  618.5 2.7 multiply_convert_fusion.6
  625.9 2.8 fusion.55
  628.7 5.1 fusion.6
  633.8 2.3 fusion.5
  636.1 2.4 copy.51
  640.1 14.7 %while.31 = (s32[]{:T(128)}, f32[2,256,128]{2,1,0:T(8,128)S(1)}, f32[8,2,256,128]{3,2,1,0:T(8,128)}, f32[8,2,256,128]{3,2,1,0:T(8,128)}, s32[]{:T(128)}, /*index=5*/s32[]{:T(128)}, s32[]{:T(128)}, s32[]{:T(128)}) while((s32[]{:T(128)}, f32[2,256,128]{2,1,0:T(8,128)S(1)}, f32[8,2,256,128]{3,2,1,0:T(8,128)}, ...), condition=%wide.region_13.14_spmd.clone, body=%wide.region_12.13_spmd.clone.sunk | while | flops 262160 | bytes 1310856 | solution.py:175
  654.8 8.4 fusion.8
  663.1 3.3 fusion.4
  669.9 10.3 multiply_reduce_fusion
  680.3 2.9 copy.58
  683.1 3.4 copy.52
  686.5 2.8 fusion.42
  696.7 4.6 fusion.60
  701.3 4.7 fusion.62
  705.9 9.9 add_convert_fusion
  715.9 7.0 convolution_convert_fusion
  723.1 8.2 fusion.69
  731.4 4.7 fusion.70
  736.1 4.7 fusion.68
  740.9 2.3 fusion.64
  743.2 2.3 fusion.63
  746.0 2.2 fusion.67
  748.3 2.3 fusion.65
  750.6 2.5 fusion.66
  753.2 14.5 %psum.84 = f32[256]{0:T(256)} all-reduce(f32[256]{0:T(256)S(1)} %bitcast.165), channel_id=1, replica_groups=mesh['dp'=8,'head'=4] {'dp'}, use_global_device_ids=true, to_apply=%region_22.23 | all-reduce | flops 256 | bytes 2048 | tf_op jit(solution)/shard_map/psum | solution.py:222
  767.7 25.9 %reduce-scatter.11.cloned.1.call-done = bf16[512,1024]{1,0:T(8,128)(2,1)} async-done(((bf16[2048,1024]{1,0:T(8,128)(2,1)}), bf16[512,1024]{1,0:T(8,128)(2,1)}) %reduce-scatter.11.cloned.1.call-update) | async-done | bytes 1048592 | tf_op jit(solution)/shard_map/reduce_scatter | solution.py:205
  795.4 78.0 %reduce-scatter.7.cloned.1.call-done = bf16[512,1024]{1,0:T(8,128)(2,1)} async-done(((bf16[2048,1024]{1,0:T(8,128)(2,1)}), bf16[512,1024]{1,0:T(8,128)(2,1)}) %reduce-scatter.7.cloned.1.call-update) | async-done | bytes 1048592 | tf_op jit(solution)/shard_map/reduce_scatter | solution.py:124
  873.3 4.3 fusion.21
  877.6 191.3 %all-reduce.3.cloned.1.call-done = (f32[1024,256]{1,0:T(8,128)}, f32[1024,256]{1,0:T(8,128)}, f32[1024,256]{1,0:T(8,128)}, f32[1024,256]{1,0:T(8,128)}, f32[256,...) async-done(((f32[1024,256]{1,0:T(8,128)}, f32[1024,256]{1,0:T(8,128)}, f32[1024,256]{1,0:T(8,128)}, f32[1024,256]{1,0:T(8,128)}, ...) | async-done | bytes 13893648 | tf_op jit(solution)/shard_map/psum | solution.py:222
  1068.9 2.4 copy.119
  (267 shorter events, 72.7 us)
Async XLA Ops:
  7.2 418.6 %copy-start = (bf16[704,1024]{1,0:T(8,128)(2,1)S(1)}, bf16[704,1024]{1,0:T(8,128)(2,1)}, u32[]{:S(2)}) copy-start(bf16[704,1024]{1,0:T(8,128)(2,1)} %param.24) | copy-start | bytes 4325380
  7.2 87.2 %all-gather.5.cloned.1.call-start = ((), (), s32[]{:S(2)}) async-start(), calls=%async_computation.4 | async-start | bytes 5242880 | tf_op jit(solution)/shard_map/all_gather | solution.py:56
  8.9 2.6 copy-start.67
  8.9 85.5 %copy-start.63 = (bf16[1024,256]{1,0:T(8,128)(2,1)S(1)}, bf16[1024,256]{1,0:T(8,128)(2,1)}, u32[]{:S(2)}) copy-start(bf16[1024,256]{1,0:T(8,128)(2,1)} %param.16) | copy-start | bytes 1572868
  11.4 249.1 %reduce-scatter.5.cloned.1.call-start = ((), (), s32[]{:S(2)}) async-start(), calls=%async_computation.5 | async-start | bytes 5242880 | tf_op jit(solution)/shard_map/reduce_scatter | solution.py:116
  11.7 144.8 %copy-start.71 = (f32[256,2]{0,1:T(2,128)}, f32[256,2]{0,1:T(2,128)S(1)}, u32[]{:S(2)}) copy-start(f32[256,2]{0,1:T(2,128)S(1)} %get-tuple-element.230) | copy-start | bytes 6148
  11.9 120.1 %copy-start.53 = (f32[2,256,256]{2,1,0:T(8,128)}, f32[2,256,256]{2,1,0:T(8,128)S(1)}, u32[]{:S(2)}) copy-start(f32[2,256,256]{2,1,0:T(8,128)S(1)} %exponential_select_fusion) | copy-start | bytes 1572868
  101.7 3.1 copy-start.61
  112.0 3.0 copy-start.65
  120.8 14.6 %copy-start.8 = (bf16[8,256,2,128]{3,2,1,0:T(2,128)(2,1)}, bf16[8,256,2,128]{3,2,1,0:T(2,128)(2,1)S(1)}, u32[]{:S(2)}) copy-start(bf16[8,256,2,128]{3,2,1,0:T(2,128)(2,1)S(1)} %reshape_reshape.6) | copy-start | bytes 3145732
  131.9 3.5 copy-start.14
  131.9 3.5 copy-start.16
  141.8 14.7 %copy-start.21 = (bf16[8,256,2,128]{3,1,2,0:T(8,128)(2,1)S(1)}, bf16[8,256,2,128]{3,1,2,0:T(8,128)(2,1)}, u32[]{:S(2)}) copy-start(bf16[8,256,2,128]{3,1,2,0:T(8,128)(2,1)} %copy-done.20) | copy-start | bytes 3145732
  164.2 9.5 copy-start.49
  173.8 5.6 copy-start.51
  179.4 3.3 copy-start.36
  182.7 77.8 %copy-start.1 = (bf16[512,1024]{1,0:T(8,128)(2,1)S(1)}, bf16[512,1024]{1,0:T(8,128)(2,1)}, u32[]{:S(2)}) copy-start(bf16[512,1024]{1,0:T(8,128)(2,1)} %param.15) | copy-start | bytes 3145732
  182.7 162.3 %all-gather.7.cloned.1.call-start = ((), (), s32[]{:S(2)}) async-start(), calls=%async_computation.6 | async-start | bytes 5242880 | tf_op jit(solution)/shard_map/all_gather | solution.py:120
  263.6 162.2 %all-gather.9.cloned.1.call-start = ((), (), s32[]{:S(2)}) async-start(), calls=%async_computation.8 | async-start | bytes 5242880 | tf_op jit(solution)/shard_map/all_gather | solution.py:128
  264.1 254.7 %reduce-scatter.9.cloned.1.call-start = ((), (), s32[]{:S(2)}) async-start(), calls=%async_computation.9 | async-start | bytes 5242880 | tf_op jit(solution)/shard_map/reduce_scatter | solution.py:135
  345.0 8.5 copy-start.75
  345.0 8.5 copy-start.78
  425.8 8.7 copy-start.77
  434.5 3.5 copy-start.28
  434.5 3.5 copy-start.26
  434.5 3.5 copy-start.79
  443.4 161.2 %all-gather.11.cloned.1.call-start = ((), (), s32[]{:S(2)}) async-start(), calls=%async_computation.10 | async-start | bytes 5242880 | tf_op jit(solution)/shard_map/all_gather | solution.py:142
  518.8 2.6 copy-start.18
  518.8 2.6 copy-start.19
  523.2 270.4 %reduce-scatter.11.cloned.1.call-start = ((), (), s32[]{:S(2)}) async-start(), calls=%async_computation.11 | async-start | bytes 5242880 | tf_op jit(solution)/shard_map/reduce_scatter | solution.py:205
  526.1 78.4 %copy-start.52 = (bf16[256,1024]{1,0:T(8,128)(2,1)S(1)}, bf16[256,1024]{1,0:T(8,128)(2,1)}, u32[]{:S(2)}) copy-start(bf16[256,1024]{1,0:T(8,128)(2,1)} %param.20) | copy-start | bytes 1572868
  621.5 12.3 %copy-start.10 = (bf16[32,8,8,256]{3,2,1,0:T(8,128)(2,1)}, bf16[32,8,8,256]{3,2,1,0:T(8,128)(2,1)S(1)}, u32[]{:S(2)}) copy-start(bf16[32,8,8,256]{3,2,1,0:T(8,128)(2,1)S(1)} %copy.73) | copy-start | bytes 3145732
  625.9 2.8 copy-start.72
  628.7 5.1 copy-start.5
  654.7 8.4 copy-start.4
  654.7 8.4 copy-start.7
  666.5 2.9 copy-start.30
  666.5 3.5 copy-start.31
  666.5 3.5 copy-start.74
  683.1 3.4 copy-start.11
  689.4 2.6 copy-start.56
  690.3 11.0 %copy-start.43 = (bf16[32,8,8,256]{3,1,2,0:T(8,128)(2,1)}, bf16[32,8,8,256]{3,1,2,0:T(8,128)(2,1)S(1)}, u32[]{:S(2)}) copy-start(bf16[32,8,8,256]{3,1,2,0:T(8,128)(2,1)S(1)} %copy.74) | copy-start | bytes 3145732
  693.0 2.6 copy-start.55
  696.6 4.6 copy-start.41
  696.7 4.6 copy-start.66
  701.3 4.7 copy-start.38
  701.3 4.7 copy-start.50
  715.8 157.5 %reduce-scatter.7.cloned.1.call-start = ((), (), s32[]{:S(2)}) async-start(), calls=%async_computation.7 | async-start | bytes 5242880 | tf_op jit(solution)/shard_map/reduce_scatter | solution.py:124
  722.9 346.0 %all-reduce.3.cloned.1.call-start = ((), (), s32[]{:S(2)}) async-start(), calls=%async_computation.12 | async-start | bytes 27787264 | tf_op jit(solution)/shard_map/psum | solution.py:222
  723.1 8.2 copy-start.27
  723.1 8.2 copy-start.76
  731.3 4.8 copy-start.12
  731.3 4.8 copy-start.25
  736.1 4.8 copy-start.40
  736.1 4.8 copy-start.45
  743.2 2.9 copy-start.37
  753.1 40.5 %copy-start.68 = (f32[512]{0:T(512)S(1)}, f32[512]{0:T(512)}, u32[]{:S(2)}) copy-start(f32[512]{0:T(512)} %copy-done.67) | copy-start | bytes 6148
  753.1 120.2 %copy-start.3 = (bf16[512,1024]{1,0:T(8,128)(2,1)S(1)}, bf16[512,1024]{1,0:T(8,128)(2,1)}, u32[]{:S(2)}) copy-start(bf16[512,1024]{1,0:T(8,128)(2,1)} %reduce-scatter.5.cloned.1.call-done) | copy-start | bytes 3145732
  753.2 120.2 %copy-start.70 = (f32[512]{0:T(512)S(1)}, f32[512]{0:T(512)}, u32[]{:S(2)}) copy-start(f32[512]{0:T(512)} %copy-done.69) | copy-start | bytes 6148
  1068.9 2.4 copy-start.60
  1068.9 3.4 copy-start.59
  1073.3 2.7 copy-start.48
  1075.9 2.9 copy-start.47
  1078.8 2.9 copy-start.46
  (25 other events, 40.9 us)
Sparse Core Ops, SparseCore 0:
  11.5 82.8 all-gather.4
  182.8 77.6 reduce-scatter.4
  263.7 81.2 all-gather.6
  346.5 79.2 all-gather.8
  443.5 75.3 reduce-scatter.8
  523.3 81.2 all-gather.10
  715.9 77.6 reduce-scatter.10
  796.0 77.2 reduce-scatter.6
  879.3 189.5 all-reduce.2
where the time goes:
time: 1100 us; the launch traced here: 1090 us
  waiting for transfers between devices  755 us (69%)
  matrix products  158 us (14%)
  other arithmetic  71.4 us (6%)
  local copies, waits for them, and re-layouts  59.9 us (5%)
  blocking collectives  29.1 us (3%)
  between operations  14.8 us (1%)
    psum x1, waiting for transfers between devices, on_device(): lax.psum((query_grad, key_grad, value_grad, gate_grad, out_proj_grad, rat...  191 us
    all_gather x1, waiting for transfers between devices, on_device(): lax.all_gather(normed_one.astype(jnp.bfloat16), 'head', axis=0, tiled=True)  82.5 us
    all_gather x1, waiting for transfers between devices, on_device(): lax.all_gather(normed_two.astype(jnp.bfloat16), 'head', axis=0, tiled=True)  80.3 us
    reduce_scatter x1, waiting for transfers between devices, on_device(): lax.psum_scatter(plain_dot(product, ffn_down).astype(jnp.bfloat16), 'head...  78 us
    reduce_scatter x1, waiting for transfers between devices, on_device(): lax.psum_scatter(plain_dot(gated, attn_out).astype(jnp.bfloat16), 'head',...  77.8 us
    all_gather x1, waiting for transfers between devices, on_device(): lax.all_gather(grad_hidden.astype(jnp.bfloat16), 'head', axis=0, tiled=True)  75.5 us
    reduce_scatter x1, waiting for transfers between devices, on_device(): lax.psum_scatter((second_dot(grad_left, ffn_left) + second_dot(grad_right...  75.3 us
    all_gather x1, waiting for transfers between devices, on_device(): grad_rows = lax.all_gather(out_grad, 'head', axis=0, tiled=True)  67.4 us
  transfers between devices with their start and end apart: 9, of which 9 were waited for; matrix products, arithmetic and copies ran while one was open for 6% of the time, Pallas kernels for 0%

commit v1 on v0

v1 whole, which is shorter than its diff:
```python
import jax
import jax.numpy as jnp
from jax import lax
from jax.sharding import PartitionSpec as P

HEADS = 8
HEAD_DIM = 128
SPAN = 256
EPSILON = 1e-06
BF = jnp.bfloat16
F32 = jnp.float32


def norm_parts(values):
    scale = lax.rsqrt(jnp.mean(values * values, axis=-1, keepdims=True) + EPSILON)
    return (values * scale, scale)


def norm_back(normed, scale, grad):
    return scale * (grad - normed * jnp.mean(grad * normed, axis=-1, keepdims=True))


def plain_dot(left, right):
    return jnp.dot(left, right, preferred_element_type=F32)


def first_dot(left, right):
    return lax.dot_general(left, right, (((0,), (0,)), ((), ())), preferred_element_type=F32)


def second_dot(left, right):
    return lax.dot_general(left, right, (((1,), (1,)), ((), ())), preferred_element_type=F32)


def make(n_dp, n_head):
    def swap(array, bit):
        return lax.ppermute(array, "dp", [(i, i ^ bit) for i in range(n_dp)])

    def from_above(array, step):
        return lax.ppermute(array, "head", [((i + step) % n_head, i) for i in range(n_head)])

    def to_above(array, step):
        return lax.ppermute(array, "head", [(i, (i + step) % n_head) for i in range(n_head)])

    def share(pieces, axis):
        half = pieces.shape[axis] // 2
        by_x = swap(pieces, 2)
        by_y = swap(pieces, 4)
        low = swap(lax.slice_in_dim(by_x, 0, half, axis=axis), 4)
        high = swap(lax.slice_in_dim(by_y, half, 2 * half, axis=axis), 2)
        return [pieces, by_x, by_y, jnp.concatenate([low, high], axis=axis)]

    def collect(parts, axis):
        own, for_x, for_y, for_far = parts
        half = own.shape[axis] // 2

        def cut(array, which):
            return lax.slice_in_dim(array, which * half, (which + 1) * half, axis=axis)

        def add(left, right):
            return (left.astype(F32) + right.astype(F32)).astype(BF)

        low = swap(cut(for_far, 0), 4)
        high = swap(cut(for_far, 1), 2)
        by_x = swap(jnp.concatenate([add(cut(for_x, 0), low), cut(for_x, 1)], axis=axis), 2)
        by_y = swap(jnp.concatenate([cut(for_y, 0), add(cut(for_y, 1), high)], axis=axis), 4)
        plane = (own.astype(F32) + by_x.astype(F32) + by_y.astype(F32)).astype(BF)
        total = plane[0].astype(F32)
        for step in range(1, n_head):
            total = total + to_above(plane[step], step).astype(F32)
        if n_dp > 8:
            groups = [[i + 8 * j for j in range(n_dp // 8)] for i in range(8)]
            total = lax.psum(total, "dp", axis_index_groups=groups)
        return total.astype(BF)

    def on_device(
        tokens,
        attn_query,
        attn_key,
        attn_value,
        attn_gate,
        attn_out,
        rotation_rates,
        ffn_left,
        ffn_right,
        ffn_down,
        out_grad,
    ):
        width = tokens.shape[1]
        quarter = width // 4
        rows = tokens.shape[0]
        spans = rows // SPAN
        units = ffn_left.shape[1] // 2
        dp = lax.axis_index("dp")
        place = lax.axis_index("head")
        core = dp & 1
        plane = (dp >> 1) & 3

        def relative(array, axis):
            return jnp.concatenate(
                [
                    lax.dynamic_slice_in_dim(array, (plane ^ q) * quarter, quarter, axis=axis)
                    for q in range(4)
                ],
                axis=axis,
            )

        def half_of(array, axis):
            size = array.shape[axis] // 2
            return lax.dynamic_slice_in_dim(array, core * size, size, axis=axis)

        attn_own = jnp.concatenate(
            [half_of(w, 1) for w in (attn_query, attn_key, attn_value, attn_gate)]
            + [half_of(attn_out, 0).T],
            axis=1,
        )
        attn_own = relative(attn_own, 0)
        ffn_own = jnp.stack([half_of(ffn_left, 1).T, half_of(ffn_right, 1).T, half_of(ffn_down, 0)])
        ffn_own = relative(ffn_own, 2)

        attn_piece = attn_own[:quarter]
        attn_far = jnp.stack([from_above(attn_piece, r) for r in range(1, n_head)])
        attn_weights = jnp.concatenate(share(attn_far, 1), axis=1)
        attn_weights = [attn_own] + [attn_weights[r] for r in range(n_head - 1)]
        ffn_piece = ffn_own[:, :, :quarter]
        ffn_far = jnp.stack([from_above(ffn_piece, r) for r in range(1, n_head)], axis=1)
        ffn_rest = jnp.concatenate(share(ffn_far, 2), axis=3)
        ffn_all = jnp.concatenate([ffn_own[:, None], ffn_rest], axis=1)
        ffn_all = ffn_all.reshape(3, n_head * units, width)
        left_w, right_w, down_w = ffn_all[0], ffn_all[1], ffn_all[2]

        inputs = relative(tokens, 1).astype(F32)
        normed_one, scale_one = norm_parts(inputs)
        normed_low = normed_one.astype(BF)
        gathered_in = jnp.concatenate([normed_low, swap(normed_low, 1)], axis=0)
        out_grad = relative(out_grad, 1)
        grad_rows = jnp.concatenate([out_grad, swap(out_grad, 1)], axis=0)

        rates_own = half_of(rotation_rates, 0)
        rates_all = jnp.stack(
            [rates_own] + [from_above(rates_own, r) for r in range(1, n_head)]
        )
        positions = (place * rows + jnp.arange(rows)).astype(F32)
        angles = positions[None, :, None] * rates_all[:, None, :]
        cosines = jnp.cos(angles)[:, None]
        sines = jnp.sin(angles)[:, None]

        pre = jnp.stack([plain_dot(gathered_in, w[:, : 4 * HEAD_DIM]) for w in attn_weights])
        pre = pre.reshape(n_head, 2, rows, 4 * HEAD_DIM)
        query_pre, key_pre, value_pre, gate_pre = (
            pre[..., i * HEAD_DIM : (i + 1) * HEAD_DIM] for i in range(4)
        )

        def rotate(values):
            activated = jax.nn.silu(values)
            return jnp.concatenate([activated * cosines, activated * sines], axis=-1).astype(BF)

        def blocks(array):
            return array.reshape(n_head, 2, spans, SPAN, array.shape[-1])

        query = blocks(rotate(query_pre))
        keys = blocks(rotate(key_pre))
        values = blocks(value_pre.astype(BF))
        head_ids = 2 * ((place + jnp.arange(n_head)) % n_head) + core
        decay_rates = jnp.exp2(-8.0 * (head_ids.astype(F32) + 1.0) / HEADS)
        places = jnp.arange(SPAN, dtype=F32)
        offsets = places[:, None] - places[None, :]
        decay_mask = jnp.where(
            offsets[None] >= 0.0,
            jnp.exp(-decay_rates[:, None, None] * jnp.maximum(offsets[None], 0.0)),
            0.0,
        )[:, None, None]
        query_decay = jnp.exp(-decay_rates[:, None] * (places[None] + 1.0))[:, None, None, :, None]
        key_decay = jnp.exp(-decay_rates[:, None] * (SPAN - 1.0 - places[None]))[
            :, None, None, :, None
        ]
        span_decay = jnp.exp(-decay_rates * SPAN)[:, None, None, None]
        rows_decay = jnp.exp(-decay_rates * rows)[:, None, None, None]

        def ein(spec, left, right):
            return jnp.einsum(spec, left, right, preferred_element_type=F32)

        def exact(spec, left, right):
            left, right = left.astype(F32), right.astype(F32)
            return jnp.einsum(spec, left, right, precision=lax.Precision.HIGHEST)

        def roll(array, step):
            return jnp.roll(array, step, axis=0)

        scores = ein("hsnid,hsnjd->hsnij", query, keys)
        weights = (scores * decay_mask).astype(BF)
        attn = ein("hsnij,hsnje->hsnie", weights, values)
        value_late = values.astype(F32) * key_decay
        fresh = exact("hsnjd,hsnje->hsnde", keys, value_late)
        local_state = jnp.zeros(fresh.shape[:2] + fresh.shape[3:], F32)
        for n in range(spans):
            local_state = span_decay * local_state + fresh[:, :, n]
        state = jnp.zeros_like(local_state)
        for hop in range(n_head - 1):
            message = roll((local_state + rows_decay * state).astype(BF), -1)
            state = lax.ppermute(message, "head", [(i, i + 1) for i in range(n_head - 1)]).astype(
                F32
            )
        states = []
        for n in range(spans):
            states.append(state)
            state = span_decay * state + fresh[:, :, n]
        states = jnp.stack(states, axis=2)
        attn = attn + query_decay * exact("hsnid,hsnde->hsnie", query, states)
        attn = attn.reshape(n_head, 2, rows, HEAD_DIM)

        def core_sum(array):
            return array + swap(array[::-1], 1)

        squares = core_sum(jnp.sum(attn * attn, axis=(0, 3)))
        scale_attn = lax.rsqrt(squares / width + EPSILON)[None, :, :, None]
        attn_normed = attn * scale_attn
        gated = (attn_normed * gate_pre).astype(BF).reshape(n_head, 2 * rows, HEAD_DIM)
        out_w = jnp.concatenate([w[:, 4 * HEAD_DIM :] for w in attn_weights], axis=1)
        gated = gated.transpose(1, 0, 2).reshape(2 * rows, n_head * HEAD_DIM)

        def core_scatter(array):
            return array[:rows] + swap(array[rows:].astype(BF), 1).astype(F32)

        hidden = inputs + core_scatter(second_dot(gated, out_w))
        normed_two, scale_two = norm_parts(hidden)
        normed_low = normed_two.astype(BF)
        gathered_mid = jnp.concatenate([normed_low, swap(normed_low, 1)], axis=0)
        left = second_dot(gathered_mid, left_w)
        right = second_dot(gathered_mid, right_w)
        product = (left * right).astype(BF)
        down_grad = first_dot(product, grad_rows).astype(BF)
        grad_product = second_dot(grad_rows, down_w)
        grad_left = (grad_product * right).astype(BF)
        grad_right = (grad_product * left).astype(BF)
        left_grad = first_dot(grad_left, gathered_mid).astype(BF)
        right_grad = first_dot(grad_right, gathered_mid).astype(BF)
        grad_mid = core_scatter(plain_dot(grad_left, left_w) + plain_dot(grad_right, right_w))
        grad_hidden = out_grad.astype(F32) + norm_back(normed_two, scale_two, grad_mid)

        def ffn_total(grad):
            grad = grad.reshape(n_head, units, width)
            piece = collect([grad[:, :, q * quarter : (q + 1) * quarter] for q in range(4)], 1)
            return jnp.concatenate(share(piece, 0), axis=1)

        down_grad, left_grad, right_grad = (ffn_total(g) for g in (down_grad, left_grad, right_grad))
        block_out = (hidden + core_scatter(plain_dot(product, down_w))).astype(BF)

        branch_low = grad_hidden.astype(BF)
        branch_rows = jnp.concatenate([branch_low, swap(branch_low, 1)], axis=0)
        out_grads = first_dot(branch_rows, gated)
        grad_gated = plain_dot(branch_rows, out_w)
        grad_gated = grad_gated.reshape(2, rows, n_head, HEAD_DIM).transpose(2, 0, 1, 3)
        grad_normed = grad_gated * gate_pre
        grad_gate_pre = (grad_gated * attn_normed).astype(BF)
        products = core_sum(jnp.sum(grad_normed * attn_normed, axis=(0, 3)))[None, :, :, None]
        grad_attn = (scale_attn * (grad_normed - attn_normed * (products / width))).astype(BF)
        grad_blocks = blocks(grad_attn)
        grad_scores = (ein("hsnie,hsnje->hsnij", grad_blocks, values) * decay_mask).astype(BF)
        grad_values = ein("hsnij,hsnie->hsnje", weights, grad_blocks)
        grad_query = ein("hsnij,hsnjd->hsnid", grad_scores, keys)
        grad_keys = ein("hsnij,hsnid->hsnjd", grad_scores, query)
        grad_query = grad_query + query_decay * exact("hsnie,hsnde->hsnid", grad_blocks, states)
        grad_early = grad_blocks.astype(F32) * query_decay
        grad_states = exact("hsnid,hsnie->hsnde", query, grad_early)
        local_pending = jnp.zeros(grad_states.shape[:2] + grad_states.shape[3:], F32)
        for n in reversed(range(spans)):
            local_pending = span_decay * local_pending + grad_states[:, :, n]
        pending = jnp.zeros_like(local_pending)
        for hop in range(n_head - 1):
            message = roll((local_pending + rows_decay * pending).astype(BF), 1)
            pending = lax.ppermute(message, "head", [(i + 1, i) for i in range(n_head - 1)]).astype(
                F32
            )
        later = []
        for n in reversed(range(spans)):
            later.insert(0, pending)
            pending = span_decay * pending + grad_states[:, :, n]
        later = jnp.stack(later, axis=2)
        grad_keys = grad_keys + key_decay * exact("hsnje,hsnde->hsnjd", values, later)
        grad_values = grad_values + key_decay * exact("hsnjd,hsnde->hsnje", keys, later)

        def unrotate(grad_rotated, pre_values):
            shaped = grad_rotated.reshape(n_head, 2, rows, 2 * HEAD_DIM)
            grad_cos = shaped[..., :HEAD_DIM]
            grad_sin = shaped[..., HEAD_DIM:]
            grad_act = grad_cos * cosines + grad_sin * sines
            sigmoid_pre = jax.nn.sigmoid(pre_values)
            activated = pre_values * sigmoid_pre
            grad_angle = activated * (grad_sin * cosines - grad_cos * sines)
            grad_pre = grad_act * sigmoid_pre * (1.0 + pre_values * (1.0 - sigmoid_pre))
            return (grad_pre.astype(BF), grad_angle)

        grad_query_pre, angle_query = unrotate(grad_query, query_pre)
        grad_key_pre, angle_key = unrotate(grad_keys, key_pre)
        grad_value_pre = grad_values.reshape(n_head, 2, rows, HEAD_DIM).astype(BF)
        rates_grad = jnp.sum(
            positions[None, None, :, None] * (angle_query + angle_key), axis=(1, 2)
        )
        grad_pre = jnp.concatenate(
            [grad_query_pre, grad_key_pre, grad_value_pre, grad_gate_pre], axis=-1
        ).reshape(n_head, 2 * rows, 4 * HEAD_DIM)
        attn_grads = []
        grad_in = None
        for r in range(n_head):
            main = first_dot(gathered_in, grad_pre[r]).astype(BF)
            outs = out_grads[:, r * HEAD_DIM : (r + 1) * HEAD_DIM].astype(BF)
            attn_grads.append(jnp.concatenate([main, outs], axis=1))
            term = second_dot(grad_pre[r], attn_weights[r][:, : 4 * HEAD_DIM])
            grad_in = term if grad_in is None else grad_in + term
        grad_in = core_scatter(grad_in)
        input_grad = grad_hidden + norm_back(normed_one, scale_one, grad_in)

        attn_grads = jnp.stack(attn_grads).reshape(n_head, 4, quarter, 5 * HEAD_DIM)
        piece = collect([attn_grads[:, q] for q in range(4)], 1)
        attn_total = jnp.concatenate(share(piece, 0), axis=0)
        rates_piece = rates_grad[0]
        for step in range(1, n_head):
            rates_piece = rates_piece + to_above(rates_grad[step], step)
        groups = [list(range(0, n_dp, 2)), list(range(1, n_dp, 2))]
        rates_piece = lax.psum(rates_piece, "dp", axis_index_groups=groups)

        def both(array, axis):
            other = swap(array, 1)
            first = jnp.where(core == 0, array, other)
            second = jnp.where(core == 0, other, array)
            return first, second

        first, second = both(relative(attn_total, 0), 0)
        matrices = []
        for i in range(5):
            pair = [part[:, i * HEAD_DIM : (i + 1) * HEAD_DIM] for part in (first, second)]
            matrices.append(jnp.concatenate(pair, axis=1).astype(F32))
        query_grad, key_grad, value_grad, gate_grad, out_proj_grad = matrices
        out_proj_grad = out_proj_grad.T
        rates_grad = jnp.concatenate(both(rates_piece, 0), axis=0)
        ffn_grads = jnp.stack([relative(g, 1) for g in (left_grad, right_grad, down_grad)])
        ffn_grads = jnp.concatenate(both(ffn_grads, 1), axis=1).astype(F32)
        return (
            relative(block_out, 1),
            relative(input_grad, 1),
            query_grad,
            key_grad,
            value_grad,
            gate_grad,
            out_proj_grad,
            rates_grad,
            ffn_grads[0].T,
            ffn_grads[1].T,
            ffn_grads[2],
        )

    return on_device


def solution(mesh):
    weights = (P(None, "head"),) * 4 + (P("head", None), P("head")) + (P(None, "head"),) * 2
    weights = weights + (P("head", None),)
    rows = P(("dp", "head"), None)
    return jax.shard_map(
        make(mesh.shape["dp"], mesh.shape["head"]),
        mesh=mesh,
        in_specs=(rows,) + weights + (rows,),
        out_specs=(rows, rows) + weights,
        check_vma=False,
    )
```

time: 1100 us -> 683 us (0.62)
  waiting for transfers between devices: 755 us -> 241 us
  starting transfers between devices: 1.18 us -> 149 us
  matrix products: 158 us -> 115 us
  local copies, waits for them, and re-layouts: 59.9 us -> 82.7 us
  blocking collectives: 29.1 us -> 7.73 us
  between operations: 14.8 us -> 3.65 us
    all_gather x4 -> x0, waiting for transfers between devices: 306 us -> none  [the longest x1 82.5 us: on_device(): lax.all_gather(normed_one.astype(jnp.bfloat16), 'head', axis=0, tiled=True)]
    reduce_scatter x4 -> x0, waiting for transfers between devices: 257 us -> none  [the longest x1 78 us: on_device(): lax.psum_scatter(plain_dot(product, ffn_down).astype(jnp.bfloat16), 'head...]
    ppermute x0 -> x83, waiting for transfers between devices: none -> 241 us  [the longest x53 100 us: swap(): return lax.ppermute(array, 'dp', [(i, i ^ bit) for i in range(n_dp)])]
    psum x1 -> x0, waiting for transfers between devices: 191 us -> none  [on_device(): lax.psum((query_grad, key_grad, value_grad, gate_grad, out_proj_grad, rat...]
    ppermute x0 -> x83, starting transfers between devices: none -> 149 us  [the longest x53 54.7 us: swap(): return lax.ppermute(array, 'dp', [(i, i ^ bit) for i in range(n_dp)])]
    dot_general x20, matrix products: 84.5 us -> 46 us  [the longest x8 26.3 us: plain_dot(): return jnp.dot(left, right, preferred_element_type=F32)]
    concatenate x0 -> x29, other arithmetic: none -> 22.6 us  [the longest x1 8.14 us: on_device(): ffn_all = jnp.concatenate([ffn_own[:, None], ffn_rest], axis=1)]
    slice x0 -> x43, local copies, waits for them, and re-layouts: none -> 22.1 us  [the longest x3 4.99 us: on_device(): out_w = jnp.concatenate([w[:, 4 * HEAD_DIM:] for w in attn_weights], axis=1)]
  transfers between devices with their start and end apart: 9 -> 83, of which waited for: 9 -> 32; matrix products, arithmetic and copies ran while one was open for 6% -> 23% of each run, Pallas kernels for 0% -> 0%
where the time goes in v1:
time: 683 us; the launch traced here: 677 us
  waiting for transfers between devices  241 us (35%)
  starting transfers between devices  149 us (22%)
  matrix products  115 us (17%)
  local copies, waits for them, and re-layouts  82.7 us (12%)
  other arithmetic  77.5 us (11%)
  blocking collectives  7.73 us (1%)
    ppermute x53, waiting for transfers between devices, swap(): return lax.ppermute(array, 'dp', [(i, i ^ bit) for i in range(n_dp)])  100 us
    ppermute x53, starting transfers between devices, swap(): return lax.ppermute(array, 'dp', [(i, i ^ bit) for i in range(n_dp)])  54.7 us
    ppermute x15, starting transfers between devices, to_above(): lax.ppermute(array, 'head', [(i, (i + step) % n_head) for i in range(n_he...  51.1 us
    ppermute x3, waiting for transfers between devices, on_device(): lax.ppermute(message, 'head', [(i, i + 1) for i in range(n_head - 1)])  47.1 us
    ppermute x15, waiting for transfers between devices, to_above(): lax.ppermute(array, 'head', [(i, (i + step) % n_head) for i in range(n_he...  47.1 us
    dot_general x8, matrix products, second_dot(): lax.dot_general(left, right, (((1,), (1,)), ((), ())), preferred_element_...  45 us
    ppermute x3, waiting for transfers between devices, on_device(): lax.ppermute(message, 'head', [(i + 1, i) for i in range(n_head - 1)])  32.6 us
    dot_general x8, matrix products, plain_dot(): return jnp.dot(left, right, preferred_element_type=F32)  26.3 us
  transfers between devices with their start and end apart: 83, of which 32 were waited for; matrix products, arithmetic and copies ran while one was open for 23% of the time, Pallas kernels for 0%

profile of v1, /device:TPU:1, one launch (start us, length us, event | category | flops | bytes accessed | tf_op | source)
XLA Modules:
  0.0 676.7 jit_solution(15169631067833033753)
XLA Ops:
  2.1 3.1 collective-permute-start.9
  22.1 3.9 collective-permute-start
  25.9 10.7 %collective-permute-done.2 = bf16[256,640]{0,1:T(8,128)(2,1)} collective-permute-done((bf16[256,640]{0,1:T(8,128)(2,1)}, bf16[256,640]{0,1:T(8,128)(2,1)}, u32[]{:S(2)}, u32[]{:S(2)}) %collective-permute-start.2) | collective-permute-done | bytes 327712 | tf_op jit(solution)/shard_map/ppermute | solution.py:40
  41.8 7.9 %collective-permute-start.10 = (f32[128]{0:T(128)}, f32[128]{0:T(128)S(1)}, u32[]{:S(2)}, u32[]{:S(2)}) collective-permute-start(f32[128]{0:T(128)} %dynamic_slice.160), channel_id=1, source_target_pairs={{3,0},{0,1},{1,2},{2,3},{7,4},{4,5},{5,6},{6,7},{11,8},{8,9},{9,10... | collective-permute-start | bytes 1544 | tf_op jit(solution)/shard_map/ppermute | solution.py:40
  51.2 3.7 multiply_cosine_fusion
  54.9 4.7 collective-permute-done.4
  64.0 7.1 %collective-permute-done.6 = bf16[3,128,640]{1,2,0:T(8,128)(2,1)S(1)} collective-permute-done((bf16[3,128,640]{1,2,0:T(8,128)(2,1)S(1)}, bf16[3,128,640]{1,2,0:T(8,128)(2,1)S(1)}, u32[]{:S(2)}, u32[]{:S(2)}) %collective-permute-start.6) | collective-permute-done | bytes 491552 | tf_op jit(solution)/shard_map/ppermute | solution.py:37
  77.7 3.3 multiply_convert_fusion.12
  86.0 11.0 %collective-permute-start.11 = (bf16[4,2,256,128]{3,2,1,0:T(8,128)(2,1)}, bf16[4,2,256,128]{3,2,1,0:T(8,128)(2,1)}, u32[]{:S(2)}, u32[]{:S(2)}) collective-permute-start(bf16[4,2,256,128]{3,2,1,0:T(8,128)(2,1)} %pad_maximum_fusion.37), channel_id=1, source_target_pairs={{0,1},{1,2},{2,3},{4,5},{5,6},{6,7},{8,9},{9,10},{10,11},{12,13},{... | collective-permute-start | bytes 1572872 | tf_op jit(solution)/shard_map/ppermute | solution.py:201
  98.8 5.8 collective-permute-done.11
  106.0 4.1 collective-permute-start.12
  111.8 3.0 collective-permute-start.17
  117.5 4.1 collective-permute-start.13
  123.8 39.5 %collective-permute-done.13 = bf16[4,2,256,128]{3,2,1,0:T(8,128)(2,1)S(1)} collective-permute-done((bf16[4,2,256,128]{3,2,1,0:T(8,128)(2,1)S(1)}, bf16[4,2,256,128]{3,2,1,0:T(8,128)(2,1)S(1)}, u32[]{:S(2)}, u32[]{:S(2)}) %collective-permute-start.13) | collective-permute-done | bytes 524320 | tf_op jit(solution)/shard_map/ppermute | solution.py:201
  163.5 3.4 multiply_reduce_fusion.4
  167.1 5.1 collective-permute-start.14
  195.2 17.2 %collective-permute-done.21 = bf16[3,3,352,256]{3,2,0,1:T(8,128)(2,1)} collective-permute-done((bf16[3,3,352,256]{3,2,0,1:T(8,128)(2,1)}, bf16[3,3,352,256]{3,2,0,1:T(8,128)(2,1)}, u32[]{:S(2)}, u32[]{:S(2)}) %collective-permute-start.21) | collective-permute-done | bytes 1622048 | tf_op jit(solution)/shard_map/ppermute | solution.py:37
  220.1 12.4 %collective-permute-done.23 = bf16[3,3,176,256]{3,2,0,1:T(8,128)(2,1)S(1)} collective-permute-done((bf16[3,3,176,256]{3,2,0,1:T(8,128)(2,1)S(1)}, bf16[3,3,176,256]{3,2,0,1:T(8,128)(2,1)S(1)}, u32[]{:S(2)}, u32[]{:S(2)}) %collective-permute-start.23) | collective-permute-done | bytes 811040 | tf_op jit(solution)/shard_map/ppermute | solution.py:37
  234.6 8.1 %maximum_maximum_fusion = bf16[3,4,352,1024]{3,2,0,1:T(8,128)(2,1)S(1)} fusion(bf16[3,3,176,256]{3,2,0,1:T(8,128)(2,1)S(1)} %collective-permute-done.23, bf16[3,3,176,256]{3,2,0,1:T(8,128)(2,1)S(1)} %collective-permute-done.22, bf16[3,3,352,256]{3,2,0,1:T(8,128)(2,1)} %collective-permute-done.21, bf16[3,3,352,256]{3,2,0,1:T(8,128)(2,1)} %collective-permute-done.20, ...), kind=kLoop, calls=%fused_computation | loop fusion | flops 69206016 | bytes 17301504 | tf_op jit(solution)/shard_map/concatenate | solution.py:128
  244.9 5.3 fusion.84
  250.2 5.7 fusion.85
  255.9 12.6 %multiply_convert_fusion.1 = (bf16[1024,1408]{1,0:T(8,128)(2,1)}, bf16[1024,1408]{1,0:T(8,128)(2,1)}, bf16[1024,1408]{1,0:T(8,128)(2,1)}) fusion(f32[1024,1408]{1,0:T(8,128)} %fusion.84, f32[1024,1408]{1,0:T(8,128)} %fusion.85, bf16[1408,1024]{1,0:T(8,128)(2,1)} %bitcast.283, bf16[512,1024]{0,1:T(8,128)(2,1)} %collective-permute-done.25, ...), kind=kOutput, calls=%fused_computation.3 | convolution fusion | flops 2971926528 | bytes 25165824 | tf_op jit(solution)/shard_map/dot_general | solution.py:32
  268.6 6.4 fusion.106
  277.2 5.1 fusion.107
  282.3 6.2 convolution_add_fusion
  289.7 5.4 convolution_convert_fusion.2
  296.3 3.5 convolution_convert_fusion.1
  300.7 5.3 convolution_convert_fusion
  308.0 5.0 collective-permute-done.60
  316.4 4.4 collective-permute-done.71
  329.1 7.1 %collective-permute-done.52 = bf16[4,352,256]{2,1,0:T(8,128)(2,1)S(1)} collective-permute-done((bf16[4,352,256]{2,1,0:T(8,128)(2,1)S(1)}, bf16[4,352,256]{2,1,0:T(8,128)(2,1)S(1)}, u32[]{:S(2)}, u32[]{:S(2)}) %collective-permute-start.52) | collective-permute-done | bytes 720928 | tf_op jit(solution)/shard_map/ppermute | solution.py:37
  339.2 11.9 %collective-permute-start.53 = (bf16[352,256]{1,0:T(8,128)(2,1)S(1)}, bf16[352,256]{1,0:T(8,128)(2,1)S(1)}, u32[]{:S(2)}, u32[]{:S(2)}) collective-permute-start(bf16[352,256]{1,0:T(8,128)(2,1)S(1)} %get-tuple-element.151), channel_id=1, source_target_pairs={{0,1},{1,2},{2,3},{3,0},{4,5},{5,6},{6,7},{7,4},{8,9},{9,10},{10,1... | collective-permute-start | bytes 540680 | tf_op jit(solution)/shard_map/ppermute | solution.py:43
  354.3 13.7 %collective-permute-start.54 = (bf16[352,256]{1,0:T(8,128)(2,1)S(1)}, bf16[352,256]{1,0:T(8,128)(2,1)S(1)}, u32[]{:S(2)}, u32[]{:S(2)}) collective-permute-start(bf16[352,256]{1,0:T(8,128)(2,1)S(1)} %get-tuple-element.153), channel_id=1, source_target_pairs={{0,2},{1,3},{2,0},{3,1},{4,6},{5,7},{6,4},{7,5},{8,10},{9,11},{10,... | collective-permute-start | bytes 540680 | tf_op jit(solution)/shard_map/ppermute | solution.py:43
  368.4 10.5 %collective-permute-start.64 = (bf16[352,256]{1,0:T(8,128)(2,1)S(1)}, bf16[352,256]{1,0:T(8,128)(2,1)S(1)}, u32[]{:S(2)}, u32[]{:S(2)}) collective-permute-start(bf16[352,256]{1,0:T(8,128)(2,1)S(1)} %get-tuple-element.158), channel_id=1, source_target_pairs={{0,1},{1,2},{2,3},{3,0},{4,5},{5,6},{6,7},{7,4},{8,9},{9,10},{10,1... | collective-permute-start | bytes 540680 | tf_op jit(solution)/shard_map/ppermute | solution.py:43
  379.3 4.6 collective-permute-start.65
  388.2 9.6 %collective-permute-done.65 = bf16[352,256]{1,0:T(8,128)(2,1)S(1)} collective-permute-done((bf16[352,256]{1,0:T(8,128)(2,1)S(1)}, bf16[352,256]{1,0:T(8,128)(2,1)S(1)}, u32[]{:S(2)}, u32[]{:S(2)}) %collective-permute-start.65) | collective-permute-done | bytes 180256 | tf_op jit(solution)/shard_map/ppermute | solution.py:43
  400.1 10.1 %collective-permute-done.76 = bf16[352,256]{1,0:T(8,128)(2,1)S(1)} collective-permute-done((bf16[352,256]{1,0:T(8,128)(2,1)S(1)}, bf16[352,256]{1,0:T(8,128)(2,1)S(1)}, u32[]{:S(2)}, u32[]{:S(2)}) %collective-permute-start.76) | collective-permute-done | bytes 180256 | tf_op jit(solution)/shard_map/ppermute | solution.py:43
  417.7 3.2 collective-permute-start.27
  434.4 3.5 fusion.31
  440.7 3.4 multiply_reduce_fusion.1
  446.1 3.1 convolution_convert_fusion.6
  457.8 12.3 %collective-permute-done.29 = bf16[4,2,256,128]{3,2,1,0:T(8,128)(2,1)S(1)} collective-permute-done((bf16[4,2,256,128]{3,2,1,0:T(8,128)(2,1)S(1)}, bf16[4,2,256,128]{3,2,1,0:T(8,128)(2,1)S(1)}, u32[]{:S(2)}, u32[]{:S(2)}) %collective-permute-start.29) | collective-permute-done | bytes 524320 | tf_op jit(solution)/shard_map/ppermute | solution.py:272
  473.9 11.1 %collective-permute-done.30 = bf16[4,2,256,128]{3,2,1,0:T(8,128)(2,1)S(1)} collective-permute-done((bf16[4,2,256,128]{3,2,1,0:T(8,128)(2,1)S(1)}, bf16[4,2,256,128]{3,2,1,0:T(8,128)(2,1)S(1)}, u32[]{:S(2)}, u32[]{:S(2)}) %collective-permute-start.30) | collective-permute-done | bytes 524320 | tf_op jit(solution)/shard_map/ppermute | solution.py:272
  490.0 9.2 %collective-permute-done.31 = bf16[4,2,256,128]{3,2,1,0:T(8,128)(2,1)S(1)} collective-permute-done((bf16[4,2,256,128]{3,2,1,0:T(8,128)(2,1)S(1)}, bf16[4,2,256,128]{3,2,1,0:T(8,128)(2,1)S(1)}, u32[]{:S(2)}, u32[]{:S(2)}) %collective-permute-start.31) | collective-permute-done | bytes 524320 | tf_op jit(solution)/shard_map/ppermute | solution.py:272
  504.3 3.2 multiply_reduce_fusion
  516.1 3.2 convolution_convert_fusion.3
  520.5 3.8 stack.142
  524.3 5.0 fusion.53
  531.8 3.8 stack.139
  535.6 4.9 fusion.49
  543.0 4.0 stack.140
  558.5 3.3 fusion.45
  562.0 3.9 collective-permute-start.82
  565.9 7.7 %psum.7 = f32[128]{0:T(128)S(1)} all-reduce(f32[128]{0:T(128)S(1)} %fusion.80), channel_id=1, replica_groups={{0,8,16,24},{4,12,20,28},{1,9,17,25},{5,13,21,29},{2,10,18,26},{6,14,22..., use_global_device_ids=true, to_apply=%region_7.8 | all-reduce | flops 128 | bytes 1024 | tf_op jit(solution)/shard_map/psum | solution.py:321
  580.2 5.3 add_add_fusion
  588.9 18.5 %collective-permute-done.36 = bf16[4,256,640]{1,2,0:T(8,128)(2,1)S(1)} collective-permute-done((bf16[4,256,640]{1,2,0:T(8,128)(2,1)S(1)}, bf16[4,256,640]{1,2,0:T(8,128)(2,1)S(1)}, u32[]{:S(2)}, u32[]{:S(2)}) %collective-permute-start.36) | collective-permute-done | bytes 1310752 | tf_op jit(solution)/shard_map/ppermute | solution.py:37
  607.4 3.2 collective-permute-done.34
  612.6 3.5 collective-permute-start.39
  617.2 5.7 collective-permute-done.37
  622.9 5.3 collective-permute-done.39
  628.2 16.5 %collective-permute-done.38 = bf16[256,640]{0,1:T(8,128)(2,1)S(1)} collective-permute-done((bf16[256,640]{0,1:T(8,128)(2,1)S(1)}, bf16[256,640]{0,1:T(8,128)(2,1)S(1)}, u32[]{:S(2)}, u32[]{:S(2)}) %collective-permute-start.38) | collective-permute-done | bytes 327712 | tf_op jit(solution)/shard_map/ppermute | solution.py:43
  645.2 3.7 slice_bitcast_fusion
  648.9 4.6 collective-permute-done.41
  654.7 3.6 collective-permute-done.42
  (602 shorter events, 224.3 us)
Async XLA Ops:
  2.1 39.7 %collective-permute-start.9 = (f32[128]{0:T(128)}, f32[128]{0:T(128)}, u32[]{:S(2)}, u32[]{:S(2)}) collective-permute-start(f32[128]{0:T(128)} %dynamic_slice.160), channel_id=1, source_target_pairs={{2,0},{3,1},{0,2},{1,3},{6,4},{7,5},{4,6},{5,7},{10,8},{11,9},{8,1... | collective-permute-start | bytes 1544 | tf_op jit(solution)/shard_map/ppermute | solution.py:40
  5.2 44.5 %collective-permute-start.8 = (f32[128]{0:T(128)}, f32[128]{0:T(128)}, u32[]{:S(2)}, u32[]{:S(2)}) collective-permute-start(f32[128]{0:T(128)} %dynamic_slice.160), channel_id=1, source_target_pairs={{1,0},{2,1},{3,2},{0,3},{5,4},{6,5},{7,6},{4,7},{9,8},{10,9},{11,1... | collective-permute-start | bytes 1544 | tf_op jit(solution)/shard_map/ppermute | solution.py:40
  12.2 24.4 %collective-permute-start.2 = (bf16[256,640]{0,1:T(8,128)(2,1)}, bf16[256,640]{0,1:T(8,128)(2,1)}, u32[]{:S(2)}, u32[]{:S(2)}) collective-permute-start(bf16[256,640]{0,1:T(8,128)(2,1)} %get-tuple-element.128), channel_id=1, source_target_pairs={{2,0},{3,1},{0,2},{1,3},{6,4},{7,5},{4,6},{5,7},{10,8},{11,9},{8,1... | collective-permute-start | bytes 983048 | tf_op jit(solution)/shard_map/ppermute | solution.py:40
  13.3 23.3 %collective-permute-start.1 = (bf16[256,640]{0,1:T(8,128)(2,1)}, bf16[256,640]{0,1:T(8,128)(2,1)}, u32[]{:S(2)}, u32[]{:S(2)}) collective-permute-start(bf16[256,640]{0,1:T(8,128)(2,1)} %get-tuple-element.128), channel_id=1, source_target_pairs={{1,0},{2,1},{3,2},{0,3},{5,4},{6,5},{7,6},{4,7},{9,8},{10,9},{11,1... | collective-permute-start | bytes 983048 | tf_op jit(solution)/shard_map/ppermute | solution.py:40
  22.1 40.3 %collective-permute-start = (bf16[512,1024]{0,1:T(8,128)(2,1)S(1)}, bf16[512,1024]{0,1:T(8,128)(2,1)S(1)}, u32[]{:S(2)}, u32[]{:S(2)}) collective-permute-start(bf16[512,1024]{0,1:T(8,128)(2,1)S(1)} %fusion.2), channel_id=1, source_target_pairs={{0,4},{4,0},{8,12},{12,8},{16,20},{20,16},{24,28},{28,24},{1,5},{5... | collective-permute-start | bytes 3145736 | tf_op jit(solution)/shard_map/ppermute | solution.py:37
  38.0 21.6 %collective-permute-start.4 = (bf16[3,256,640]{1,2,0:T(8,128)(2,1)S(1)}, bf16[3,256,640]{1,2,0:T(8,128)(2,1)S(1)}, u32[]{:S(2)}, u32[]{:S(2)}) collective-permute-start(bf16[3,256,640]{1,2,0:T(8,128)(2,1)S(1)} %get-tuple-element.145), channel_id=1, source_target_pairs={{0,8},{4,12},{8,0},{12,4},{16,24},{20,28},{24,16},{28,20},{1,9},{5... | collective-permute-start | bytes 2949128 | tf_op jit(solution)/shard_map/ppermute | solution.py:37
  39.3 21.7 %collective-permute-start.5 = (bf16[3,256,640]{1,2,0:T(8,128)(2,1)S(1)}, bf16[3,256,640]{1,2,0:T(8,128)(2,1)S(1)}, u32[]{:S(2)}, u32[]{:S(2)}) collective-permute-start(bf16[3,256,640]{1,2,0:T(8,128)(2,1)S(1)} %get-tuple-element.145), channel_id=1, source_target_pairs={{0,16},{4,20},{8,24},{12,28},{16,0},{20,4},{24,8},{28,12},{1,17},{... | collective-permute-start | bytes 2949128 | tf_op jit(solution)/shard_map/ppermute | solution.py:37
  59.7 11.3 %collective-permute-start.6 = (bf16[3,128,640]{1,2,0:T(8,128)(2,1)S(1)}, bf16[3,128,640]{1,2,0:T(8,128)(2,1)S(1)}, u32[]{:S(2)}, u32[]{:S(2)}) collective-permute-start(bf16[3,128,640]{1,2,0:T(8,128)(2,1)S(1)} %slice.578), channel_id=1, source_target_pairs={{0,16},{4,20},{8,24},{12,28},{16,0},{20,4},{24,8},{28,12},{1,17},{... | collective-permute-start | bytes 1474568 | tf_op jit(solution)/shard_map/ppermute | solution.py:37
  86.0 18.6 %collective-permute-start.11 = (bf16[4,2,256,128]{3,2,1,0:T(8,128)(2,1)}, bf16[4,2,256,128]{3,2,1,0:T(8,128)(2,1)}, u32[]{:S(2)}, u32[]{:S(2)}) collective-permute-start(bf16[4,2,256,128]{3,2,1,0:T(8,128)(2,1)} %pad_maximum_fusion.37), channel_id=1, source_target_pairs={{0,1},{1,2},{2,3},{4,5},{5,6},{6,7},{8,9},{9,10},{10,11},{12,13},{... | collective-permute-start | bytes 1572872 | tf_op jit(solution)/shard_map/ppermute | solution.py:201
  106.0 11.2 %collective-permute-start.12 = (bf16[4,2,256,128]{3,2,1,0:T(8,128)(2,1)S(1)}, bf16[4,2,256,128]{3,2,1,0:T(8,128)(2,1)S(1)}, u32[]{:S(2)}, u32[]{:S(2)}) collective-permute-start(bf16[4,2,256,128]{3,2,1,0:T(8,128)(2,1)S(1)} %pad_maximum_fusion.38), channel_id=1, source_target_pairs={{0,1},{1,2},{2,3},{4,5},{5,6},{6,7},{8,9},{9,10},{10,11},{12,13},{... | collective-permute-start | bytes 1572872 | tf_op jit(solution)/shard_map/ppermute | solution.py:201
  111.6 60.6 %collective-permute-start.19 = (bf16[3,352,256]{2,1,0:T(8,128)(2,1)}, bf16[3,352,256]{2,1,0:T(8,128)(2,1)}, u32[]{:S(2)}, u32[]{:S(2)}) collective-permute-start(bf16[3,352,256]{2,1,0:T(8,128)(2,1)} %get-tuple-element.100), channel_id=1, source_target_pairs={{3,0},{0,1},{1,2},{2,3},{7,4},{4,5},{5,6},{6,7},{11,8},{8,9},{9,10... | collective-permute-start | bytes 1622024 | tf_op jit(solution)/shard_map/ppermute | solution.py:40
  111.8 60.4 %collective-permute-start.18 = (bf16[3,352,256]{2,1,0:T(8,128)(2,1)}, bf16[3,352,256]{2,1,0:T(8,128)(2,1)}, u32[]{:S(2)}, u32[]{:S(2)}) collective-permute-start(bf16[3,352,256]{2,1,0:T(8,128)(2,1)} %get-tuple-element.100), channel_id=1, source_target_pairs={{2,0},{3,1},{0,2},{1,3},{6,4},{7,5},{4,6},{5,7},{10,8},{11,9},{8,1... | collective-permute-start | bytes 1622024 | tf_op jit(solution)/shard_map/ppermute | solution.py:40
  111.8 60.4 %collective-permute-start.17 = (bf16[3,352,256]{2,1,0:T(8,128)(2,1)}, bf16[3,352,256]{2,1,0:T(8,128)(2,1)}, u32[]{:S(2)}, u32[]{:S(2)}) collective-permute-start(bf16[3,352,256]{2,1,0:T(8,128)(2,1)} %get-tuple-element.100), channel_id=1, source_target_pairs={{1,0},{2,1},{3,2},{0,3},{5,4},{6,5},{7,6},{4,7},{9,8},{10,9},{11,1... | collective-permute-start | bytes 1622024 | tf_op jit(solution)/shard_map/ppermute | solution.py:40
  117.5 45.8 %collective-permute-start.13 = (bf16[4,2,256,128]{3,2,1,0:T(8,128)(2,1)S(1)}, bf16[4,2,256,128]{3,2,1,0:T(8,128)(2,1)S(1)}, u32[]{:S(2)}, u32[]{:S(2)}) collective-permute-start(bf16[4,2,256,128]{3,2,1,0:T(8,128)(2,1)S(1)} %pad_maximum_fusion.39), channel_id=1, source_target_pairs={{0,1},{1,2},{2,3},{4,5},{5,6},{6,7},{8,9},{9,10},{10,11},{12,13},{... | collective-permute-start | bytes 1572872 | tf_op jit(solution)/shard_map/ppermute | solution.py:201
  167.1 14.6 %collective-permute-start.14 = (f32[2,512]{1,0:T(2,128)S(1)}, f32[2,512]{1,0:T(2,128)S(1)}, u32[]{:S(2)}, u32[]{:S(2)}) collective-permute-start(f32[2,512]{1,0:T(2,128)S(1)} %rev.6), channel_id=1, source_target_pairs={{0,4},{4,0},{8,12},{12,8},{16,20},{20,16},{24,28},{28,24},{1,5},{5... | collective-permute-start | bytes 12296 | tf_op jit(solution)/shard_map/ppermute | solution.py:37
  175.1 37.4 %collective-permute-start.21 = (bf16[3,3,352,256]{3,2,0,1:T(8,128)(2,1)}, bf16[3,3,352,256]{3,2,0,1:T(8,128)(2,1)}, u32[]{:S(2)}, u32[]{:S(2)}) collective-permute-start(bf16[3,3,352,256]{3,2,0,1:T(8,128)(2,1)} %pad_maximum_fusion.13), channel_id=1, source_target_pairs={{0,16},{4,20},{8,24},{12,28},{16,0},{20,4},{24,8},{28,12},{1,17},{... | collective-permute-start | bytes 4866056 | tf_op jit(solution)/shard_map/ppermute | solution.py:37
  175.8 39.1 %collective-permute-start.20 = (bf16[3,3,352,256]{3,2,0,1:T(8,128)(2,1)}, bf16[3,3,352,256]{3,2,0,1:T(8,128)(2,1)}, u32[]{:S(2)}, u32[]{:S(2)}) collective-permute-start(bf16[3,3,352,256]{3,2,0,1:T(8,128)(2,1)} %pad_maximum_fusion.13), channel_id=1, source_target_pairs={{0,8},{4,12},{8,0},{12,4},{16,24},{20,28},{24,16},{28,20},{1,9},{5... | collective-permute-start | bytes 4866056 | tf_op jit(solution)/shard_map/ppermute | solution.py:37
  190.8 25.7 %collective-permute-start.15 = (bf16[512,1024]{0,1:T(8,128)(2,1)}, bf16[512,1024]{0,1:T(8,128)(2,1)}, u32[]{:S(2)}, u32[]{:S(2)}) collective-permute-start(bf16[512,1024]{0,1:T(8,128)(2,1)} %slice.841), channel_id=1, source_target_pairs={{0,4},{4,0},{8,12},{12,8},{16,20},{20,16},{24,28},{28,24},{1,5},{5... | collective-permute-start | bytes 3145736 | tf_op jit(solution)/shard_map/ppermute | solution.py:37
  193.1 62.8 %collective-permute-start.25 = (bf16[512,1024]{0,1:T(8,128)(2,1)}, bf16[512,1024]{0,1:T(8,128)(2,1)}, u32[]{:S(2)}, u32[]{:S(2)}) collective-permute-start(bf16[512,1024]{0,1:T(8,128)(2,1)} %pad_maximum_fusion.29), channel_id=1, source_target_pairs={{0,4},{4,0},{8,12},{12,8},{16,20},{20,16},{24,28},{28,24},{1,5},{5... | collective-permute-start | bytes 3145736 | tf_op jit(solution)/shard_map/ppermute | solution.py:37
  213.6 18.8 %collective-permute-start.23 = (bf16[3,3,176,256]{3,2,0,1:T(8,128)(2,1)S(1)}, bf16[3,3,176,256]{3,2,0,1:T(8,128)(2,1)S(1)}, u32[]{:S(2)}, u32[]{:S(2)}) collective-permute-start(bf16[3,3,176,256]{3,2,0,1:T(8,128)(2,1)S(1)} %slice.604), channel_id=1, source_target_pairs={{0,8},{4,12},{8,0},{12,4},{16,24},{20,28},{24,16},{28,20},{1,9},{5... | collective-permute-start | bytes 2433032 | tf_op jit(solution)/shard_map/ppermute | solution.py:37
  216.1 18.5 %collective-permute-start.22 = (bf16[3,3,176,256]{3,2,0,1:T(8,128)(2,1)S(1)}, bf16[3,3,176,256]{3,2,0,1:T(8,128)(2,1)S(1)}, u32[]{:S(2)}, u32[]{:S(2)}) collective-permute-start(bf16[3,3,176,256]{3,2,0,1:T(8,128)(2,1)S(1)} %slice.603), channel_id=1, source_target_pairs={{0,16},{4,20},{8,24},{12,28},{16,0},{20,4},{24,8},{28,12},{1,17},{... | collective-permute-start | bytes 2433032 | tf_op jit(solution)/shard_map/ppermute | solution.py:37
  218.6 26.2 %collective-permute-start.16 = (bf16[512,1024]{0,1:T(8,128)(2,1)S(1)}, bf16[512,1024]{0,1:T(8,128)(2,1)S(1)}, u32[]{:S(2)}, u32[]{:S(2)}) collective-permute-start(bf16[512,1024]{0,1:T(8,128)(2,1)S(1)} %multiply_convert_fusion.13), channel_id=1, source_target_pairs={{0,4},{4,0},{8,12},{12,8},{16,20},{20,16},{24,28},{28,24},{1,5},{5... | collective-permute-start | bytes 3145736 | tf_op jit(solution)/shard_map/ppermute | solution.py:37
  275.2 50.4 %collective-permute-start.24 = (bf16[512,1024]{0,1:T(8,128)(2,1)S(1)}, bf16[512,1024]{0,1:T(8,128)(2,1)S(1)}, u32[]{:S(2)}, u32[]{:S(2)}) collective-permute-start(bf16[512,1024]{0,1:T(8,128)(2,1)S(1)} %slice.840), channel_id=1, source_target_pairs={{0,4},{4,0},{8,12},{12,8},{16,20},{20,16},{24,28},{28,24},{1,5},{5... | collective-permute-start | bytes 3145736 | tf_op jit(solution)/shard_map/ppermute | solution.py:37
  288.7 35.6 %collective-permute-start.26 = (bf16[512,1024]{0,1:T(8,128)(2,1)S(1)}, bf16[512,1024]{0,1:T(8,128)(2,1)S(1)}, u32[]{:S(2)}, u32[]{:S(2)}) collective-permute-start(bf16[512,1024]{0,1:T(8,128)(2,1)S(1)} %slice.839), channel_id=1, source_target_pairs={{0,4},{4,0},{8,12},{12,8},{16,20},{20,16},{24,28},{28,24},{1,5},{5... | collective-permute-start | bytes 3145736 | tf_op jit(solution)/shard_map/ppermute | solution.py:37
  295.3 10.8 %collective-permute-start.49 = (bf16[4,176,256]{2,1,0:T(8,128)(2,1)S(1)}, bf16[4,176,256]{2,1,0:T(8,128)(2,1)S(1)}, u32[]{:S(2)}, u32[]{:S(2)}) collective-permute-start(bf16[4,176,256]{2,1,0:T(8,128)(2,1)S(1)} %get-tuple-element.79), channel_id=1, source_target_pairs={{0,16},{4,20},{8,24},{12,28},{16,0},{20,4},{24,8},{28,12},{1,17},{... | collective-permute-start | bytes 1081352 | tf_op jit(solution)/shard_map/ppermute | solution.py:37
  295.7 11.7 %collective-permute-start.51 = (bf16[4,176,256]{2,1,0:T(8,128)(2,1)S(1)}, bf16[4,176,256]{2,1,0:T(8,128)(2,1)S(1)}, u32[]{:S(2)}, u32[]{:S(2)}) collective-permute-start(bf16[4,176,256]{2,1,0:T(8,128)(2,1)S(1)} %get-tuple-element.80), channel_id=1, source_target_pairs={{0,8},{4,12},{8,0},{12,4},{16,24},{20,28},{24,16},{28,20},{1,9},{5... | collective-permute-start | bytes 1081352 | tf_op jit(solution)/shard_map/ppermute | solution.py:37
  299.9 13.1 %collective-permute-start.60 = (bf16[4,176,256]{2,1,0:T(8,128)(2,1)S(1)}, bf16[4,176,256]{2,1,0:T(8,128)(2,1)S(1)}, u32[]{:S(2)}, u32[]{:S(2)}) collective-permute-start(bf16[4,176,256]{2,1,0:T(8,128)(2,1)S(1)} %get-tuple-element.85), channel_id=1, source_target_pairs={{0,16},{4,20},{8,24},{12,28},{16,0},{20,4},{24,8},{28,12},{1,17},{... | collective-permute-start | bytes 1081352 | tf_op jit(solution)/shard_map/ppermute | solution.py:37
  307.4 13.4 %collective-permute-start.71 = (bf16[4,176,256]{2,1,0:T(8,128)(2,1)S(1)}, bf16[4,176,256]{2,1,0:T(8,128)(2,1)S(1)}, u32[]{:S(2)}, u32[]{:S(2)}) collective-permute-start(bf16[4,176,256]{2,1,0:T(8,128)(2,1)S(1)} %get-tuple-element.91), channel_id=1, source_target_pairs={{0,16},{4,20},{8,24},{12,28},{16,0},{20,4},{24,8},{28,12},{1,17},{... | collective-permute-start | bytes 1081352 | tf_op jit(solution)/shard_map/ppermute | solution.py:37
  315.2 21.0 %collective-permute-start.52 = (bf16[4,352,256]{2,1,0:T(8,128)(2,1)S(1)}, bf16[4,352,256]{2,1,0:T(8,128)(2,1)S(1)}, u32[]{:S(2)}, u32[]{:S(2)}) collective-permute-start(bf16[4,352,256]{2,1,0:T(8,128)(2,1)S(1)} %pad_maximum_fusion.32), channel_id=1, source_target_pairs={{0,16},{4,20},{8,24},{12,28},{16,0},{20,4},{24,8},{28,12},{1,17},{... | collective-permute-start | bytes 2162696 | tf_op jit(solution)/shard_map/ppermute | solution.py:37
  320.8 18.1 %collective-permute-start.50 = (bf16[4,352,256]{2,1,0:T(8,128)(2,1)S(1)}, bf16[4,352,256]{2,1,0:T(8,128)(2,1)S(1)}, u32[]{:S(2)}, u32[]{:S(2)}) collective-permute-start(bf16[4,352,256]{2,1,0:T(8,128)(2,1)S(1)} %pad_maximum_fusion.31), channel_id=1, source_target_pairs={{0,8},{4,12},{8,0},{12,4},{16,24},{20,28},{24,16},{28,20},{1,9},{5... | collective-permute-start | bytes 2162696 | tf_op jit(solution)/shard_map/ppermute | solution.py:37
  323.4 28.3 %collective-permute-start.63 = (bf16[4,352,256]{2,1,0:T(8,128)(2,1)S(1)}, bf16[4,352,256]{2,1,0:T(8,128)(2,1)S(1)}, u32[]{:S(2)}, u32[]{:S(2)}) collective-permute-start(bf16[4,352,256]{2,1,0:T(8,128)(2,1)S(1)} %pad_maximum_fusion.34), channel_id=1, source_target_pairs={{0,16},{4,20},{8,24},{12,28},{16,0},{20,4},{24,8},{28,12},{1,17},{... | collective-permute-start | bytes 2162696 | tf_op jit(solution)/shard_map/ppermute | solution.py:37
  324.2 30.1 %collective-permute-start.61 = (bf16[4,352,256]{2,1,0:T(8,128)(2,1)S(1)}, bf16[4,352,256]{2,1,0:T(8,128)(2,1)S(1)}, u32[]{:S(2)}, u32[]{:S(2)}) collective-permute-start(bf16[4,352,256]{2,1,0:T(8,128)(2,1)S(1)} %pad_maximum_fusion.33), channel_id=1, source_target_pairs={{0,8},{4,12},{8,0},{12,4},{16,24},{20,28},{24,16},{28,20},{1,9},{5... | collective-permute-start | bytes 2162696 | tf_op jit(solution)/shard_map/ppermute | solution.py:37
  325.5 42.9 %collective-permute-start.74 = (bf16[4,352,256]{2,1,0:T(8,128)(2,1)S(1)}, bf16[4,352,256]{2,1,0:T(8,128)(2,1)S(1)}, u32[]{:S(2)}, u32[]{:S(2)}) collective-permute-start(bf16[4,352,256]{2,1,0:T(8,128)(2,1)S(1)} %pad_maximum_fusion.36), channel_id=1, source_target_pairs={{0,16},{4,20},{8,24},{12,28},{16,0},{20,4},{24,8},{28,12},{1,17},{... | collective-permute-start | bytes 2162696 | tf_op jit(solution)/shard_map/ppermute | solution.py:37
  336.2 42.7 %collective-permute-start.72 = (bf16[4,352,256]{2,1,0:T(8,128)(2,1)S(1)}, bf16[4,352,256]{2,1,0:T(8,128)(2,1)S(1)}, u32[]{:S(2)}, u32[]{:S(2)}) collective-permute-start(bf16[4,352,256]{2,1,0:T(8,128)(2,1)S(1)} %pad_maximum_fusion.35), channel_id=1, source_target_pairs={{0,8},{4,12},{8,0},{12,4},{16,24},{20,28},{24,16},{28,20},{1,9},{5... | collective-permute-start | bytes 2162696 | tf_op jit(solution)/shard_map/ppermute | solution.py:37
  339.2 40.1 %collective-permute-start.53 = (bf16[352,256]{1,0:T(8,128)(2,1)S(1)}, bf16[352,256]{1,0:T(8,128)(2,1)S(1)}, u32[]{:S(2)}, u32[]{:S(2)}) collective-permute-start(bf16[352,256]{1,0:T(8,128)(2,1)S(1)} %get-tuple-element.151), channel_id=1, source_target_pairs={{0,1},{1,2},{2,3},{3,0},{4,5},{5,6},{6,7},{7,4},{8,9},{9,10},{10,1... | collective-permute-start | bytes 540680 | tf_op jit(solution)/shard_map/ppermute | solution.py:43
  351.7 32.3 %collective-permute-start.55 = (bf16[352,256]{1,0:T(8,128)(2,1)S(1)}, bf16[352,256]{1,0:T(8,128)(2,1)S(1)}, u32[]{:S(2)}, u32[]{:S(2)}) collective-permute-start(bf16[352,256]{1,0:T(8,128)(2,1)S(1)} %get-tuple-element.152), channel_id=1, source_target_pairs={{0,3},{1,0},{2,1},{3,2},{4,7},{5,4},{6,5},{7,6},{8,11},{9,8},{10,9... | collective-permute-start | bytes 540680 | tf_op jit(solution)/shard_map/ppermute | solution.py:43
  354.3 31.1 %collective-permute-start.54 = (bf16[352,256]{1,0:T(8,128)(2,1)S(1)}, bf16[352,256]{1,0:T(8,128)(2,1)S(1)}, u32[]{:S(2)}, u32[]{:S(2)}) collective-permute-start(bf16[352,256]{1,0:T(8,128)(2,1)S(1)} %get-tuple-element.153), channel_id=1, source_target_pairs={{0,2},{1,3},{2,0},{3,1},{4,6},{5,7},{6,4},{7,5},{8,10},{9,11},{10,... | collective-permute-start | bytes 540680 | tf_op jit(solution)/shard_map/ppermute | solution.py:43
  368.4 19.1 %collective-permute-start.64 = (bf16[352,256]{1,0:T(8,128)(2,1)S(1)}, bf16[352,256]{1,0:T(8,128)(2,1)S(1)}, u32[]{:S(2)}, u32[]{:S(2)}) collective-permute-start(bf16[352,256]{1,0:T(8,128)(2,1)S(1)} %get-tuple-element.158), channel_id=1, source_target_pairs={{0,1},{1,2},{2,3},{3,0},{4,5},{5,6},{6,7},{7,4},{8,9},{9,10},{10,1... | collective-permute-start | bytes 540680 | tf_op jit(solution)/shard_map/ppermute | solution.py:43
  379.3 18.5 %collective-permute-start.65 = (bf16[352,256]{1,0:T(8,128)(2,1)S(1)}, bf16[352,256]{1,0:T(8,128)(2,1)S(1)}, u32[]{:S(2)}, u32[]{:S(2)}) collective-permute-start(bf16[352,256]{1,0:T(8,128)(2,1)S(1)} %get-tuple-element.160), channel_id=1, source_target_pairs={{0,2},{1,3},{2,0},{3,1},{4,6},{5,7},{6,4},{7,5},{8,10},{9,11},{10,... | collective-permute-start | bytes 540680 | tf_op jit(solution)/shard_map/ppermute | solution.py:43
  383.9 14.6 %collective-permute-start.75 = (bf16[352,256]{1,0:T(8,128)(2,1)S(1)}, bf16[352,256]{1,0:T(8,128)(2,1)S(1)}, u32[]{:S(2)}, u32[]{:S(2)}) collective-permute-start(bf16[352,256]{1,0:T(8,128)(2,1)S(1)} %get-tuple-element.165), channel_id=1, source_target_pairs={{0,1},{1,2},{2,3},{3,0},{4,5},{5,6},{6,7},{7,4},{8,9},{9,10},{10,1... | collective-permute-start | bytes 540680 | tf_op jit(solution)/shard_map/ppermute | solution.py:43
  385.4 13.2 %collective-permute-start.77 = (bf16[352,256]{1,0:T(8,128)(2,1)S(1)}, bf16[352,256]{1,0:T(8,128)(2,1)S(1)}, u32[]{:S(2)}, u32[]{:S(2)}) collective-permute-start(bf16[352,256]{1,0:T(8,128)(2,1)S(1)} %get-tuple-element.166), channel_id=1, source_target_pairs={{0,3},{1,0},{2,1},{3,2},{4,7},{5,4},{6,5},{7,6},{8,11},{9,8},{10,9... | collective-permute-start | bytes 540680 | tf_op jit(solution)/shard_map/ppermute | solution.py:43
  387.5 22.7 %collective-permute-start.76 = (bf16[352,256]{1,0:T(8,128)(2,1)S(1)}, bf16[352,256]{1,0:T(8,128)(2,1)S(1)}, u32[]{:S(2)}, u32[]{:S(2)}) collective-permute-start(bf16[352,256]{1,0:T(8,128)(2,1)S(1)} %get-tuple-element.167), channel_id=1, source_target_pairs={{0,2},{1,3},{2,0},{3,1},{4,6},{5,7},{6,4},{7,5},{8,10},{9,11},{10,... | collective-permute-start | bytes 540680 | tf_op jit(solution)/shard_map/ppermute | solution.py:43
  387.6 23.7 %collective-permute-start.57 = (bf16[352,256]{1,0:T(8,128)(2,1)S(1)}, bf16[352,256]{1,0:T(8,128)(2,1)S(1)}, u32[]{:S(2)}, u32[]{:S(2)}) collective-permute-start(bf16[352,256]{1,0:T(8,128)(2,1)S(1)} %fusion.68), channel_id=1, source_target_pairs={{0,16},{4,20},{8,24},{12,28},{16,0},{20,4},{24,8},{28,12},{1,17},{... | collective-permute-start | bytes 540680 | tf_op jit(solution)/shard_map/ppermute | solution.py:37
  397.8 14.3 %collective-permute-start.56 = (bf16[352,256]{1,0:T(8,128)(2,1)S(1)}, bf16[352,256]{1,0:T(8,128)(2,1)S(1)}, u32[]{:S(2)}, u32[]{:S(2)}) collective-permute-start(bf16[352,256]{1,0:T(8,128)(2,1)S(1)} %fusion.68), channel_id=1, source_target_pairs={{0,8},{4,12},{8,0},{12,4},{16,24},{20,28},{24,16},{28,20},{1,9},{5... | collective-permute-start | bytes 540680 | tf_op jit(solution)/shard_map/ppermute | solution.py:37
  398.6 15.5 %collective-permute-start.68 = (bf16[352,256]{1,0:T(8,128)(2,1)}, bf16[352,256]{1,0:T(8,128)(2,1)S(1)}, u32[]{:S(2)}, u32[]{:S(2)}) collective-permute-start(bf16[352,256]{1,0:T(8,128)(2,1)} %fusion.65), channel_id=1, source_target_pairs={{0,16},{4,20},{8,24},{12,28},{16,0},{20,4},{24,8},{28,12},{1,17},{... | collective-permute-start | bytes 540680 | tf_op jit(solution)/shard_map/ppermute | solution.py:37
  398.6 19.1 %collective-permute-start.67 = (bf16[352,256]{1,0:T(8,128)(2,1)}, bf16[352,256]{1,0:T(8,128)(2,1)}, u32[]{:S(2)}, u32[]{:S(2)}) collective-permute-start(bf16[352,256]{1,0:T(8,128)(2,1)} %fusion.65), channel_id=1, source_target_pairs={{0,8},{4,12},{8,0},{12,4},{16,24},{20,28},{24,16},{28,20},{1,9},{5... | collective-permute-start | bytes 540680 | tf_op jit(solution)/shard_map/ppermute | solution.py:37
  411.0 10.8 %collective-permute-start.79 = (bf16[352,256]{1,0:T(8,128)(2,1)}, bf16[352,256]{1,0:T(8,128)(2,1)}, u32[]{:S(2)}, u32[]{:S(2)}) collective-permute-start(bf16[352,256]{1,0:T(8,128)(2,1)} %fusion.62), channel_id=1, source_target_pairs={{0,16},{4,20},{8,24},{12,28},{16,0},{20,4},{24,8},{28,12},{1,17},{... | collective-permute-start | bytes 540680 | tf_op jit(solution)/shard_map/ppermute | solution.py:37
  411.3 12.2 %collective-permute-start.78 = (bf16[352,256]{1,0:T(8,128)(2,1)}, bf16[352,256]{1,0:T(8,128)(2,1)}, u32[]{:S(2)}, u32[]{:S(2)}) collective-permute-start(bf16[352,256]{1,0:T(8,128)(2,1)} %fusion.62), channel_id=1, source_target_pairs={{0,8},{4,12},{8,0},{12,4},{16,24},{20,28},{24,16},{28,20},{1,9},{5... | collective-permute-start | bytes 540680 | tf_op jit(solution)/shard_map/ppermute | solution.py:37
  412.1 12.8 %collective-permute-start.59 = (bf16[176,256]{1,0:T(8,128)(2,1)}, bf16[176,256]{1,0:T(8,128)(2,1)}, u32[]{:S(2)}, u32[]{:S(2)}) collective-permute-start(bf16[176,256]{1,0:T(8,128)(2,1)} %slice.672), channel_id=1, source_target_pairs={{0,8},{4,12},{8,0},{12,4},{16,24},{20,28},{24,16},{28,20},{1,9},{5... | collective-permute-start | bytes 270344 | tf_op jit(solution)/shard_map/ppermute | solution.py:37
  414.1 11.7 %collective-permute-start.58 = (bf16[176,256]{1,0:T(8,128)(2,1)}, bf16[176,256]{1,0:T(8,128)(2,1)}, u32[]{:S(2)}, u32[]{:S(2)}) collective-permute-start(bf16[176,256]{1,0:T(8,128)(2,1)} %slice.671), channel_id=1, source_target_pairs={{0,16},{4,20},{8,24},{12,28},{16,0},{20,4},{24,8},{28,12},{1,17},{... | collective-permute-start | bytes 270344 | tf_op jit(solution)/shard_map/ppermute | solution.py:37
  417.7 15.1 %collective-permute-start.27 = (bf16[512,1024]{0,1:T(8,128)(2,1)}, bf16[512,1024]{0,1:T(8,128)(2,1)S(1)}, u32[]{:S(2)}, u32[]{:S(2)}) collective-permute-start(bf16[512,1024]{0,1:T(8,128)(2,1)} %get-tuple-element.37), channel_id=1, source_target_pairs={{0,4},{4,0},{8,12},{12,8},{16,20},{20,16},{24,28},{28,24},{1,5},{5... | collective-permute-start | bytes 3145736 | tf_op jit(solution)/shard_map/ppermute | solution.py:37
  454.8 15.4 %collective-permute-start.29 = (bf16[4,2,256,128]{3,2,1,0:T(8,128)(2,1)S(1)}, bf16[4,2,256,128]{3,2,1,0:T(8,128)(2,1)S(1)}, u32[]{:S(2)}, u32[]{:S(2)}) collective-permute-start(bf16[4,2,256,128]{3,2,1,0:T(8,128)(2,1)S(1)} %pad_maximum_fusion.40), channel_id=1, source_target_pairs={{1,0},{2,1},{3,2},{5,4},{6,5},{7,6},{9,8},{10,9},{11,10},{13,12},{... | collective-permute-start | bytes 1572872 | tf_op jit(solution)/shard_map/ppermute | solution.py:272
  470.5 14.5 %collective-permute-start.30 = (bf16[4,2,256,128]{3,2,1,0:T(8,128)(2,1)S(1)}, bf16[4,2,256,128]{3,2,1,0:T(8,128)(2,1)S(1)}, u32[]{:S(2)}, u32[]{:S(2)}) collective-permute-start(bf16[4,2,256,128]{3,2,1,0:T(8,128)(2,1)S(1)} %pad_maximum_fusion.41), channel_id=1, source_target_pairs={{1,0},{2,1},{3,2},{5,4},{6,5},{7,6},{9,8},{10,9},{11,10},{13,12},{... | collective-permute-start | bytes 1572872 | tf_op jit(solution)/shard_map/ppermute | solution.py:272
  485.3 13.9 %collective-permute-start.31 = (bf16[4,2,256,128]{3,2,1,0:T(8,128)(2,1)S(1)}, bf16[4,2,256,128]{3,2,1,0:T(8,128)(2,1)S(1)}, u32[]{:S(2)}, u32[]{:S(2)}) collective-permute-start(bf16[4,2,256,128]{3,2,1,0:T(8,128)(2,1)S(1)} %pad_maximum_fusion.42), channel_id=1, source_target_pairs={{1,0},{2,1},{3,2},{5,4},{6,5},{7,6},{9,8},{10,9},{11,10},{13,12},{... | collective-permute-start | bytes 1572872 | tf_op jit(solution)/shard_map/ppermute | solution.py:272
  553.8 21.5 %collective-permute-start.35 = (bf16[4,128,640]{1,2,0:T(8,128)(2,1)}, bf16[4,128,640]{1,2,0:T(8,128)(2,1)}, u32[]{:S(2)}, u32[]{:S(2)}) collective-permute-start(bf16[4,128,640]{1,2,0:T(8,128)(2,1)} %get-tuple-element.124), channel_id=1, source_target_pairs={{0,8},{4,12},{8,0},{12,4},{16,24},{20,28},{24,16},{28,20},{1,9},{5... | collective-permute-start | bytes 1966088 | tf_op jit(solution)/shard_map/ppermute | solution.py:37
  557.6 20.6 %collective-permute-start.33 = (bf16[4,128,640]{1,2,0:T(8,128)(2,1)}, bf16[4,128,640]{1,2,0:T(8,128)(2,1)}, u32[]{:S(2)}, u32[]{:S(2)}) collective-permute-start(bf16[4,128,640]{1,2,0:T(8,128)(2,1)} %get-tuple-element.123), channel_id=1, source_target_pairs={{0,16},{4,20},{8,24},{12,28},{16,0},{20,4},{24,8},{28,12},{1,17},{... | collective-permute-start | bytes 1966088 | tf_op jit(solution)/shard_map/ppermute | solution.py:37
  562.0 24.6 %collective-permute-start.82 = (bf16[3,352,1024]{2,1,0:T(8,128)(2,1)}, bf16[3,352,1024]{2,1,0:T(8,128)(2,1)}, u32[]{:S(2)}, u32[]{:S(2)}) collective-permute-start(bf16[3,352,1024]{2,1,0:T(8,128)(2,1)} %pad_maximum_fusion.3), channel_id=1, source_target_pairs={{0,4},{4,0},{8,12},{12,8},{16,20},{20,16},{24,28},{28,24},{1,5},{5... | collective-permute-start | bytes 6488072 | tf_op jit(solution)/shard_map/ppermute | solution.py:37
  573.6 12.4 %collective-permute-start.48 = (f32[128]{0:T(128)S(1)}, f32[128]{0:T(128)S(1)}, u32[]{:S(2)}, u32[]{:S(2)}) collective-permute-start(f32[128]{0:T(128)S(1)} %psum.7), channel_id=1, source_target_pairs={{0,4},{4,0},{8,12},{12,8},{16,20},{20,16},{24,28},{28,24},{1,5},{5... | collective-permute-start | bytes 1544 | tf_op jit(solution)/shard_map/ppermute | solution.py:37
  577.0 30.5 %collective-permute-start.36 = (bf16[4,256,640]{1,2,0:T(8,128)(2,1)S(1)}, bf16[4,256,640]{1,2,0:T(8,128)(2,1)S(1)}, u32[]{:S(2)}, u32[]{:S(2)}) collective-permute-start(bf16[4,256,640]{1,2,0:T(8,128)(2,1)S(1)} %pad_maximum_fusion.22), channel_id=1, source_target_pairs={{0,16},{4,20},{8,24},{12,28},{16,0},{20,4},{24,8},{28,12},{1,17},{... | collective-permute-start | bytes 3932168 | tf_op jit(solution)/shard_map/ppermute | solution.py:37
  580.1 30.5 %collective-permute-start.34 = (bf16[4,256,640]{1,2,0:T(8,128)(2,1)S(1)}, bf16[4,256,640]{1,2,0:T(8,128)(2,1)S(1)}, u32[]{:S(2)}, u32[]{:S(2)}) collective-permute-start(bf16[4,256,640]{1,2,0:T(8,128)(2,1)S(1)} %pad_maximum_fusion.21), channel_id=1, source_target_pairs={{0,8},{4,12},{8,0},{12,4},{16,24},{20,28},{24,16},{28,20},{1,9},{5... | collective-permute-start | bytes 3932168 | tf_op jit(solution)/shard_map/ppermute | solution.py:37
  585.8 76.9 %collective-permute-start.32 = (bf16[512,1024]{0,1:T(8,128)(2,1)S(1)}, bf16[512,1024]{0,1:T(8,128)(2,1)S(1)}, u32[]{:S(2)}, u32[]{:S(2)}) collective-permute-start(bf16[512,1024]{0,1:T(8,128)(2,1)S(1)} %slice.838), channel_id=1, source_target_pairs={{0,4},{4,0},{8,12},{12,8},{16,20},{20,16},{24,28},{28,24},{1,5},{5... | collective-permute-start | bytes 3145736 | tf_op jit(solution)/shard_map/ppermute | solution.py:37
  612.5 10.4 %collective-permute-start.37 = (bf16[256,640]{0,1:T(8,128)(2,1)S(1)}, bf16[256,640]{0,1:T(8,128)(2,1)S(1)}, u32[]{:S(2)}, u32[]{:S(2)}) collective-permute-start(bf16[256,640]{0,1:T(8,128)(2,1)S(1)} %get-tuple-element.120), channel_id=1, source_target_pairs={{0,1},{1,2},{2,3},{3,0},{4,5},{5,6},{6,7},{7,4},{8,9},{9,10},{10,1... | collective-permute-start | bytes 983048 | tf_op jit(solution)/shard_map/ppermute | solution.py:43
  612.6 15.6 %collective-permute-start.39 = (bf16[256,640]{0,1:T(8,128)(2,1)S(1)}, bf16[256,640]{0,1:T(8,128)(2,1)S(1)}, u32[]{:S(2)}, u32[]{:S(2)}) collective-permute-start(bf16[256,640]{0,1:T(8,128)(2,1)S(1)} %get-tuple-element.121), channel_id=1, source_target_pairs={{0,3},{1,0},{2,1},{3,2},{4,7},{5,4},{6,5},{7,6},{8,11},{9,8},{10,9... | collective-permute-start | bytes 983048 | tf_op jit(solution)/shard_map/ppermute | solution.py:43
  616.1 28.6 %collective-permute-start.38 = (bf16[256,640]{0,1:T(8,128)(2,1)S(1)}, bf16[256,640]{0,1:T(8,128)(2,1)S(1)}, u32[]{:S(2)}, u32[]{:S(2)}) collective-permute-start(bf16[256,640]{0,1:T(8,128)(2,1)S(1)} %get-tuple-element.122), channel_id=1, source_target_pairs={{0,2},{1,3},{2,0},{3,1},{4,6},{5,7},{6,4},{7,5},{8,10},{9,11},{10,... | collective-permute-start | bytes 983048 | tf_op jit(solution)/shard_map/ppermute | solution.py:43
  (145 other events, 1149.6 us)

commit v2 on v1

--- a/solution.py
+++ b/solution.py
@@ -1,6 +1,10 @@
+import functools
+
 import jax
 import jax.numpy as jnp
 from jax import lax
+from jax.experimental import pallas as pl
+from jax.experimental.pallas import tpu as pltpu
 from jax.sharding import PartitionSpec as P
 
 HEADS = 8
@@ -30,6 +34,566 @@
 
 def second_dot(left, right):
     return lax.dot_general(left, right, (((1,), (1,)), ((), ())), preferred_element_type=F32)
+
+
+MESH = pl.DeviceIdType.MESH
+ANY = pl.BlockSpec(memory_space=pl.ANY)
+IN_VMEM = pl.BlockSpec(memory_space=pltpu.VMEM)
+
+
+def split(value):
+    high = value.astype(BF)
+    return high, (value - high.astype(F32)).astype(BF)
+
+
+class Place:
+    def __init__(self, n_head):
+        self.n_head = n_head
+        dp = lax.axis_index("dp")
+        self.z = lax.axis_index("head")
+        self.core = lax.rem(dp, 2)
+        x = lax.rem(lax.div(dp, 2), 2)
+        y = lax.rem(lax.div(dp, 4), 2)
+        self.plane = x + 2 * y
+        self.at = [self.plane, self.plane + 1 - 2 * x, self.plane + 2 - 4 * y, 3 - self.plane]
+        self.across = {"dp": dp + 1 - 2 * self.core}
+        self.by_x = {"dp": dp + 2 - 4 * x}
+        self.by_y = {"dp": dp + 4 - 8 * y}
+        self.up = {"head": lax.rem(self.z + 1, n_head)}
+        self.down = {"head": lax.rem(self.z + n_head - 1, n_head)}
+
+    def below(self, step):
+        return {"head": lax.rem(self.z + self.n_head - step, self.n_head)}
+
+    def greet(self):
+        barrier = pltpu.get_barrier_semaphore()
+        others = [self.across, self.by_x, self.by_y]
+        others += [self.below(step) for step in range(1, self.n_head)]
+        for other in others:
+            pl.semaphore_signal(barrier, inc=1, device_id=other, device_id_type=MESH)
+        pl.semaphore_wait(barrier, len(others))
+
+
+class Copies:
+    def __init__(self, sends, receives, locals_):
+        self.sends, self.receives, self.locals = sends, receives, locals_
+        self.pending = []
+        self.n_local = 0
+
+    def send(self, src, dst, out, into, device, when=None):
+        copy = pltpu.make_async_remote_copy(
+            src_ref=src,
+            dst_ref=dst,
+            send_sem=self.sends.at[out],
+            recv_sem=self.receives.at[into],
+            device_id=device,
+            device_id_type=MESH,
+        )
+        if when is None:
+            copy.start()
+            self.pending.append(copy.wait_send)
+        else:
+            pl.when(when)(copy.start)
+            self.pending.append(lambda: pl.when(when)(copy.wait_send))
+
+    def receive(self, dst, into, device):
+        pltpu.make_async_remote_copy(
+            src_ref=dst,
+            dst_ref=dst,
+            send_sem=self.sends.at[0],
+            recv_sem=self.receives.at[into],
+            device_id=device,
+            device_id_type=MESH,
+        ).wait_recv()
+
+    def move(self, src, dst, later=False):
+        copy = pltpu.make_async_copy(src, dst, self.locals.at[self.n_local])
+        self.n_local += 1
+        copy.start()
+        if later:
+            self.pending.append(copy.wait)
+        return copy
+
+    def finish(self):
+        for wait in self.pending:
+            wait()
+
+
+class Gather:
+    def __init__(self, place, copies, view, base):
+        self.place, self.copies, self.view, self.base = place, copies, view, base
+
+    def begin(self):
+        place, z = self.place, self.place.z
+        own = self.view(0, 0, None)
+        last = place.n_head - 1
+        self.copies.send(
+            own, self.view(last, 0, None), self.base, self.base + last, place.up, when=z < last
+        )
+        self.copies.send(own, self.view(1, 0, None), self.base + 1, self.base + 1, place.down, when=z > 0)
+
+    def arrived(self, slot):
+        place, copies, z, base = self.place, self.copies, self.place.z, self.base
+        last = place.n_head - 1
+        copies.receive(self.view(slot, 0, None), base + slot, place.up)
+        from_up = z + slot <= last
+        piece = self.view(slot, 0, None)
+        down = jnp.logical_and(from_up, z > 0)
+        up = jnp.logical_and(jnp.logical_not(from_up), z < last)
+        after = jnp.minimum(slot + 1, last)
+        before = jnp.maximum(slot - 1, 1)
+        copies.send(piece, self.view(after, 0, None), base + 1 + slot, base + after, place.down, when=down)
+        copies.send(piece, self.view(before, 0, None), base + 1 + slot, base + before, place.up, when=up)
+        at = base + 4 * slot + 4
+        copies.send(piece, self.view(slot, 1, None), at, at, place.by_x)
+        copies.send(piece, self.view(slot, 2, None), at + 1, at + 1, place.by_y)
+
+    def spread(self, slot):
+        place, copies = self.place, self.copies
+        at = self.base + 4 * slot + 4
+        copies.receive(self.view(slot, 1, None), at, place.by_x)
+        copies.send(self.view(slot, 1, 0), self.view(slot, 3, 0), at + 2, at + 2, place.by_y)
+        copies.receive(self.view(slot, 2, None), at + 1, place.by_y)
+        copies.send(self.view(slot, 2, 1), self.view(slot, 3, 1), at + 3, at + 3, place.by_x)
+
+    def complete(self, slot):
+        place, copies = self.place, self.copies
+        at = self.base + 4 * slot + 4
+        copies.receive(self.view(slot, 3, 0), at + 2, place.by_y)
+        copies.receive(self.view(slot, 3, 1), at + 3, place.by_x)
+
+
+PER_GATHER = 24
+
+
+def forward_kernel(
+    n_head,
+    tokens,
+    wq,
+    wk,
+    wv,
+    wg,
+    wo,
+    ffn,
+    rates,
+    wa_out,
+    wo_out,
+    wf_out,
+    nin_out,
+    pre_out,
+    q_out,
+    k_out,
+    v_out,
+    attn_out,
+    cos_out,
+    sin_out,
+    fresh_out,
+    carry_out,
+    scale_out,
+    gated_out,
+    hidden_out,
+    nm_out,
+    wa_ref,
+    wo_ref,
+    wf_ref,
+    x_ref,
+    nin_ref,
+    pre_ref,
+    q_ref,
+    k_ref,
+    v_ref,
+    attn_ref,
+    cos_ref,
+    sin_ref,
+    fresh_ref,
+    carry_ref,
+    message_ref,
+    squares_ref,
+    other_squares_ref,
+    gated_ref,
+    branch_ref,
+    other_branch_ref,
+    hidden_ref,
+    nm_ref,
+    rates_ref,
+    sends,
+    receives,
+    locals_,
+):
+    rows, width = tokens.shape
+    quarter = width // 4
+    units = ffn.shape[1] // 2
+    tiles = 2 * rows // SPAN
+    place = Place(n_head)
+    z, core = place.z, place.core
+    copies = Copies(sends, receives, locals_)
+
+    def columns(start, size):
+        return pl.ds(pl.multiple_of(start, size), size)
+
+    own_loads = []
+    for q in range(4):
+        far = columns(place.at[q] * quarter, quarter)
+        near = pl.ds(q * quarter, quarter)
+        loads = []
+        for i, w in enumerate((wq, wk, wv, wg)):
+            src = w.at[far, columns(core * HEAD_DIM, HEAD_DIM)]
+            loads.append(copies.move(src, wa_ref.at[0, near, pl.ds(i * HEAD_DIM, HEAD_DIM)]))
+        src = wo.at[columns(core * HEAD_DIM, HEAD_DIM), far]
+        loads.append(copies.move(src, wo_ref.at[pl.ds(0, HEAD_DIM), near]))
+        src = ffn.at[:, pl.ds(pl.multiple_of(core * units, 16), units), far]
+        loads.append(copies.move(src, wf_ref.at[:, pl.ds(0, units), near]))
+        own_loads.append(loads)
+    token_loads = [
+        copies.move(
+            tokens.at[:, columns(place.at[q] * quarter, quarter)],
+            x_ref.at[:, pl.ds(q * quarter, quarter)],
+        )
+        for q in range(4)
+    ]
+    place.greet()
+
+    def half_rows(half, size):
+        return pl.ds(0, size) if half is None else pl.ds(half * (size // 2), size // 2)
+
+    def wa_view(slot, q, half):
+        at = half_rows(half, quarter)
+        return wa_ref.at[slot, pl.ds(q * quarter + at.start, at.size), :]
+
+    def wo_view(slot, q, half):
+        at = half_rows(half, HEAD_DIM)
+        return wo_ref.at[
+            pl.ds(pl.multiple_of(slot * HEAD_DIM + at.start, HEAD_DIM // 2), at.size),
+            pl.ds(q * quarter, quarter),
+        ]
+
+    def wf_view(slot, q, half):
+        at = half_rows(half, units)
+        return wf_ref.at[
+            :,
+            pl.ds(pl.multiple_of(slot * units + at.start, 16), at.size),
+            pl.ds(q * quarter, quarter),
+        ]
+
+    attn_in = Gather(place, copies, wa_view, 0)
+    attn_down = Gather(place, copies, wo_view, PER_GATHER)
+    feed = Gather(place, copies, wf_view, 2 * PER_GATHER)
+    base = 3 * PER_GATHER
+    for load in own_loads[0][:4]:
+        load.wait()
+    attn_in.begin()
+    own_loads[0][4].wait()
+    attn_down.begin()
+    for step in range(1, n_head):
+        copies.send(rates, rates_ref.at[step], base + step, base + step, place.below(step))
+    rates_ref[0] = rates[...]
+
+    for load in token_loads:
+        load.wait()
+
+    def norm_rows(values):
+        mean = jnp.mean(values * values, axis=-1, keepdims=True)
+        return values * lax.rsqrt(mean + EPSILON)
+
+    @pl.loop(0, rows // 128)
+    def _(i):
+        at = pl.ds(pl.multiple_of(i * 128, 128), 128)
+        nin_ref[at, :] = norm_rows(x_ref[at, :].astype(F32)).astype(BF)
+
+    base += 4
+    nin_other = nin_ref.at[pl.ds(rows, rows)]
+    copies.send(nin_ref.at[pl.ds(0, rows)], nin_other, base, base, place.across)
+    own_loads[0][5].wait()
+    feed.begin()
+    for loads in own_loads[1:]:
+        for load in loads:
+            load.wait()
+    for step in range(1, n_head):
+        copies.receive(rates_ref.at[step], base - 4 + step, place.up)
+    copies.receive(nin_other, base, place.across)
+    copies.move(nin_ref, nin_out, later=True)
+
+    def decay_of(head):
+        exponent = jnp.full((1, 1), -8.0 / HEADS, F32) * (head + 1).astype(F32)
+        return jnp.exp2(exponent)
+
+    def tile(i):
+        return pl.ds(pl.multiple_of(i * SPAN, SPAN), SPAN)
+
+    def iota(shape, axis):
+        return lax.broadcasted_iota(jnp.int32, shape, axis).astype(F32)
+
+    def dot(left, right):
+        return jnp.dot(left, right, preferred_element_type=F32)
+
+    def slot_compute(slot):
+        head = 2 * lax.rem(z + slot, n_head) + core
+        decay = decay_of(head)
+        rate = rates_ref[slot, pl.ds(core, 1), :]
+        coarse = (z * rows).astype(F32) + 32.0 * iota((rows // 32, HEAD_DIM), 0)
+        coarse = coarse * rate
+        fine = iota((32, HEAD_DIM), 0) * rate
+        cos_a, sin_a = jnp.cos(coarse), jnp.sin(coarse)
+        cos_b, sin_b = jnp.cos(fine), jnp.sin(fine)
+        for a in range(rows // 32):
+            cos_row, sin_row = cos_a[a : a + 1], sin_a[a : a + 1]
+            cos_ref[slot, pl.ds(a * 32, 32), :] = cos_row * cos_b - sin_row * sin_b
+            sin_ref[slot, pl.ds(a * 32, 32), :] = sin_row * cos_b + cos_row * sin_b
+        offsets = iota((SPAN, SPAN), 0) - iota((SPAN, SPAN), 1)
+        mask = jnp.where(offsets >= 0.0, jnp.exp(-decay * jnp.maximum(offsets, 0.0)), 0.0)
+        late = jnp.exp(-decay * (SPAN - 1.0 - iota((SPAN, HEAD_DIM), 0)))
+
+        @pl.loop(0, tiles)
+        def _(i):
+            at = tile(i)
+            pre = dot(nin_ref[at, :], wa_ref[slot])
+            pre_ref[slot, at, :] = pre
+            here = tile(lax.rem(i, rows // SPAN))
+            cosines, sines = cos_ref[slot, here, :], sin_ref[slot, here, :]
+
+            def rotate(values):
+                activated = values / (1.0 + jnp.exp(-values))
+                turned = jnp.concatenate([activated * cosines, activated * sines], axis=1)
+                return turned.astype(BF)
+
+            query = rotate(pre[:, :HEAD_DIM])
+            keys = rotate(pre[:, HEAD_DIM : 2 * HEAD_DIM])
+            value = pre[:, 2 * HEAD_DIM : 3 * HEAD_DIM].astype(BF)
+            q_ref[slot, at, :] = query
+            k_ref[slot, at, :] = keys
+            v_ref[slot, at, :] = value
+            scores = lax.dot_general(
+                query, keys, (((1,), (1,)), ((), ())), preferred_element_type=F32
+            )
+            weights = (scores * mask).astype(BF)
+            attn_ref[slot, at, :] = dot(weights, value)
+            high, low = split(value.astype(F32) * late)
+            both = lax.dot_general(
+                keys,
+                jnp.concatenate([high, low], axis=1),
+                (((0,), (0,)), ((), ())),
+                preferred_element_type=F32,
+            )
+            fresh_ref[slot, i] = both[:, :HEAD_DIM] + both[:, HEAD_DIM:]
+
+        for ref, out in (
+            (wa_ref, wa_out),
+            (pre_ref, pre_out),
+            (q_ref, q_out),
+            (k_ref, k_out),
+            (v_ref, v_out),
+            (cos_ref, cos_out),
+            (sin_ref, sin_out),
+            (fresh_ref, fresh_out),
+        ):
+            copies.move(ref.at[slot], out.at[slot], later=True)
+
+    last = n_head - 1
+    first = 1 + 2 * lax.div(z, last)
+    second = 2 + lax.rem(lax.div(z + 1, 2), 2)
+    third = 6 - first - second
+
+    attn_in.arrived(first)
+    attn_down.arrived(first)
+    slot_compute(0)
+    attn_in.arrived(second)
+    attn_down.arrived(second)
+    attn_in.spread(first)
+    attn_down.spread(first)
+    attn_in.arrived(third)
+    attn_down.arrived(third)
+    attn_in.spread(second)
+    attn_down.spread(second)
+    attn_in.complete(first)
+    slot_compute(first)
+    feed.arrived(first)
+    attn_in.spread(third)
+    attn_down.spread(third)
+    attn_in.complete(second)
+    slot_compute(second)
+    feed.arrived(second)
+    feed.spread(first)
+    attn_in.complete(third)
+    slot_compute(third)
+    feed.arrived(third)
+    feed.spread(second)
+
+    base += 1
+    chain_base = base
+    n_chain = 2 * n_head
+
+    def chain_at(index):
+        group, seq = lax.div(index, 2), lax.rem(index, 2)
+        return lax.rem(group - z + n_head, n_head), seq, decay_of(2 * group + core)
+
+    def chain_copy(index, slot, seq):
+        after = lax.rem(slot + n_head - 1, n_head)
+        return pltpu.make_async_remote_copy(
+            src_ref=message_ref.at[slot, seq],
+            dst_ref=carry_ref.at[after, seq],
+            send_sem=sends.at[chain_base + index],
+            recv_sem=receives.at[chain_base + index],
+            device_id=place.up,
+            device_id_type=MESH,
+        )
+
+    @pl.loop(0, n_chain)
+    def _(index):
+        slot, seq, decay = chain_at(index)
+
+        @pl.when(z > 0)
+        def _():
+            copies.receive(carry_ref.at[slot, seq], chain_base + index, place.down)
+
+        @pl.when(z == 0)
+        def _():
+            carry_ref[slot, seq] = jnp.zeros(carry_ref.shape[2:], BF)
+
+        @pl.when(z < last)
+        def _():
+            total = jnp.exp(-decay * rows) * carry_ref[slot, seq].astype(F32)
+            for n in range(rows // SPAN):
+                left = rows - (n + 1) * SPAN
+                total += jnp.exp(-decay * left) * fresh_ref[slot, seq * (rows // SPAN) + n]
+            message_ref[slot, seq] = total.astype(BF)
+            chain_copy(index, slot, seq).start()
+
+    copies.move(carry_ref, carry_out, later=True)
+
+    squares_ref[...] = jnp.zeros_like(squares_ref)
+
+    @pl.loop(0, n_head)
+    def _(slot):
+        decay = decay_of(2 * lax.rem(z + slot, n_head) + core)
+        early = jnp.exp(-decay * (iota((SPAN, HEAD_DIM), 0) + 1.0))
+
+        @pl.loop(0, 2)
+        def _(seq):
+            state = carry_ref[slot, seq].astype(F32)
+            for n in range(rows // SPAN):
+                i = seq * (rows // SPAN) + n
+                at = tile(i)
+                both = dot(q_ref[slot, at, :], jnp.concatenate(split(state), axis=1))
+                attn = attn_ref[slot, at, :]
+                attn += early * (both[:, :HEAD_DIM] + both[:, HEAD_DIM:])
+                attn_ref[slot, at, :] = attn
+                squares_ref[at, :] += jnp.sum(attn * attn, axis=-1, keepdims=True)
+                if n + 1 < rows // SPAN:
+                    state = jnp.exp(-decay * SPAN) * state + fresh_ref[slot, i]
+
+    copies.move(attn_ref, attn_out, later=True)
+    base += n_chain
+    own, other = pl.ds(0, rows), pl.ds(rows, rows)
+    copies.send(squares_ref.at[own], other_squares_ref.at[other], base, base, place.across)
+    copies.send(squares_ref.at[other], other_squares_ref.at[own], base + 1, base + 1, place.across)
+    feed.spread(third)
+    for slot in (first, second, third):
+        attn_down.complete(slot)
+    copies.receive(other_squares_ref.at[other], base, place.across)
+    copies.receive(other_squares_ref.at[own], base + 1, place.across)
+
+    @pl.loop(0, tiles)
+    def _(i):
+        at = tile(i)
+        total = squares_ref[at, :] + other_squares_ref[at, :]
+        scale = lax.rsqrt(total / width + EPSILON)
+        other_squares_ref[at, :] = scale
+        for slot in range(n_head):
+            gate = pre_ref[slot, at, pl.ds(3 * HEAD_DIM, HEAD_DIM)]
+            gated = (attn_ref[slot, at, :] * scale * gate).astype(BF)
+            gated_ref[at, pl.ds(slot * HEAD_DIM, HEAD_DIM)] = gated
+
+    copies.move(other_squares_ref, scale_out, later=True)
+    copies.move(gated_ref, gated_out, later=True)
+    copies.move(wo_ref, wo_out, later=True)
+    base += 2
+
+    @pl.loop(0, rows // SPAN)
+    def _(i):
+        gated = gated_ref[pl.ds(pl.multiple_of(rows + i * SPAN, SPAN), SPAN), :]
+        branch_ref[tile(i), :] = dot(gated, wo_ref[...]).astype(BF)
+
+    copies.send(branch_ref, other_branch_ref, base, base, place.across)
+
+    @pl.loop(0, rows // SPAN)
+    def _(i):
+        at = tile(i)
+        hidden_ref[at, :] = x_ref[at, :].astype(F32) + dot(gated_ref[at, :], wo_ref[...])
+
+    copies.receive(other_branch_ref, base, place.across)
+
+    @pl.loop(0, rows // 128)
+    def _(i):
+        at = pl.ds(pl.multiple_of(i * 128, 128), 128)
+        hidden = hidden_ref[at, :] + other_branch_ref[at, :].astype(F32)
+        hidden_ref[at, :] = hidden
+        nm_ref[at, :] = norm_rows(hidden).astype(BF)
+
+    copies.send(nm_ref.at[own], nm_ref.at[other], base + 1, base + 1, place.across)
+    copies.move(hidden_ref, hidden_out, later=True)
+    for slot in (first, second, third):
+        feed.complete(slot)
+    copies.move(wf_ref, wf_out, later=True)
+    copies.receive(nm_ref.at[other], base + 1, place.across)
+    copies.move(nm_ref, nm_out, later=True)
+
+    @pl.when(z < last)
+    def _():
+        @pl.loop(0, n_chain)
+        def _(index):
+            slot, seq, _ = chain_at(index)
+            chain_copy(index, slot, seq).wait_send()
+
+    copies.finish()
+
+
+def forward(n_head, tokens, wq, wk, wv, wg, wo, ffn, rates):
+    rows, width = tokens.shape
+    units = ffn.shape[1] // 2
+    tall = 2 * rows
+    buffers = [
+        ((n_head, width, 4 * HEAD_DIM), BF),
+        ((n_head * HEAD_DIM, width), BF),
+        ((3, n_head * units, width), BF),
+        ((rows, width), BF),
+        ((tall, width), BF),
+        ((n_head, tall, 4 * HEAD_DIM), F32),
+        ((n_head, tall, 2 * HEAD_DIM), BF),
+        ((n_head, tall, 2 * HEAD_DIM), BF),
+        ((n_head, tall, HEAD_DIM), BF),
+        ((n_head, tall, HEAD_DIM), F32),
+        ((n_head, rows, HEAD_DIM), F32),
+        ((n_head, rows, HEAD_DIM), F32),
+        ((n_head, tall // SPAN, 2 * HEAD_DIM, HEAD_DIM), F32),
+        ((n_head, 2, 2 * HEAD_DIM, HEAD_DIM), BF),
+        ((n_head, 2, 2 * HEAD_DIM, HEAD_DIM), BF),
+        ((tall, HEAD_DIM), F32),
+        ((tall, HEAD_DIM), F32),
+        ((tall, n_head * HEAD_DIM), BF),
+        ((rows, width), BF),
+        ((rows, width), BF),
+        ((rows, width), F32),
+        ((tall, width), BF),
+        ((n_head, 8, HEAD_DIM), F32),
+    ]
+    out_of = [0, 1, 2, 4, 5, 6, 7, 8, 9, 10, 11, 12, 13, 16, 17, 20, 21]
+    n_sems = 3 * PER_GATHER + 4 + 1 + 2 * n_head + 2 + 2
+    return pl.pallas_call(
+        functools.partial(forward_kernel, n_head),
+        out_shape=[jax.ShapeDtypeStruct(*buffers[i]) for i in out_of],
+        in_specs=[ANY] * 7 + [IN_VMEM],
+        out_specs=[ANY] * len(out_of),
+        scratch_shapes=[pltpu.VMEM(*b) for b in buffers]
+        + [
+            pltpu.SemaphoreType.DMA((n_sems,)),
+            pltpu.SemaphoreType.DMA((n_sems,)),
+            pltpu.SemaphoreType.DMA((80,)),
+        ],
+        compiler_params=pltpu.CompilerParams(
+            collective_id=0, has_side_effects=True, vmem_limit_bytes=62 << 20
+        ),
+        name="forward",
+    )(tokens, wq, wk, wv, wg, wo, ffn, rates)
 
 
 def make(n_dp, n_head):
@@ -109,58 +673,55 @@
             size = array.shape[axis] // 2
             return lax.dynamic_slice_in_dim(array, core * size, size, axis=axis)
 
-        attn_own = jnp.concatenate(
-            [half_of(w, 1) for w in (attn_query, attn_key, attn_value, attn_gate)]
-            + [half_of(attn_out, 0).T],
-            axis=1,
+        ffn = jnp.stack([ffn_left.T, ffn_right.T, ffn_down])
+        rates_in = jnp.pad(rotation_rates.reshape(2, HEAD_DIM), ((0, 6), (0, 0)))
+        (
+            attn_weights,
+            out_w,
+            ffn_all,
+            gathered_in,
+            pre,
+            query,
+            keys,
+            values,
+            attn,
+            cosines,
+            sines,
+            fresh,
+            carry,
+            scale_attn,
+            gated,
+            hidden,
+            gathered_mid,
+        ) = forward(
+            n_head,
+            tokens,
+            attn_query,
+            attn_key,
+            attn_value,
+            attn_gate,
+            attn_out,
+            ffn,
+            rates_in,
         )
-        attn_own = relative(attn_own, 0)
-        ffn_own = jnp.stack([half_of(ffn_left, 1).T, half_of(ffn_right, 1).T, half_of(ffn_down, 0)])
-        ffn_own = relative(ffn_own, 2)
-
-        attn_piece = attn_own[:quarter]
-        attn_far = jnp.stack([from_above(attn_piece, r) for r in range(1, n_head)])
-        attn_weights = jnp.concatenate(share(attn_far, 1), axis=1)
-        attn_weights = [attn_own] + [attn_weights[r] for r in range(n_head - 1)]
-        ffn_piece = ffn_own[:, :, :quarter]
-        ffn_far = jnp.stack([from_above(ffn_piece, r) for r in range(1, n_head)], axis=1)
-        ffn_rest = jnp.concatenate(share(ffn_far, 2), axis=3)
-        ffn_all = jnp.concatenate([ffn_own[:, None], ffn_rest], axis=1)
-        ffn_all = ffn_all.reshape(3, n_head * units, width)
         left_w, right_w, down_w = ffn_all[0], ffn_all[1], ffn_all[2]
+        out_w = out_w.T
 
         inputs = relative(tokens, 1).astype(F32)
         normed_one, scale_one = norm_parts(inputs)
-        normed_low = normed_one.astype(BF)
-        gathered_in = jnp.concatenate([normed_low, swap(normed_low, 1)], axis=0)
         out_grad = relative(out_grad, 1)
         grad_rows = jnp.concatenate([out_grad, swap(out_grad, 1)], axis=0)
-
-        rates_own = half_of(rotation_rates, 0)
-        rates_all = jnp.stack(
-            [rates_own] + [from_above(rates_own, r) for r in range(1, n_head)]
-        )
         positions = (place * rows + jnp.arange(rows)).astype(F32)
-        angles = positions[None, :, None] * rates_all[:, None, :]
-        cosines = jnp.cos(angles)[:, None]
-        sines = jnp.sin(angles)[:, None]
-
-        pre = jnp.stack([plain_dot(gathered_in, w[:, : 4 * HEAD_DIM]) for w in attn_weights])
+        cosines, sines = cosines[:, None], sines[:, None]
         pre = pre.reshape(n_head, 2, rows, 4 * HEAD_DIM)
         query_pre, key_pre, value_pre, gate_pre = (
             pre[..., i * HEAD_DIM : (i + 1) * HEAD_DIM] for i in range(4)
         )
 
-        def rotate(values):
-            activated = jax.nn.silu(values)
-            return jnp.concatenate([activated * cosines, activated * sines], axis=-1).astype(BF)
-
         def blocks(array):
             return array.reshape(n_head, 2, spans, SPAN, array.shape[-1])
 
-        query = blocks(rotate(query_pre))
-        keys = blocks(rotate(key_pre))
-        values = blocks(value_pre.astype(BF))
+        query, keys, values = blocks(query), blocks(keys), blocks(values)
         head_ids = 2 * ((place + jnp.arange(n_head)) % n_head) + core
         decay_rates = jnp.exp2(-8.0 * (head_ids.astype(F32) + 1.0) / HEADS)
         places = jnp.arange(SPAN, dtype=F32)
@@ -189,43 +750,24 @@
 
         scores = ein("hsnid,hsnjd->hsnij", query, keys)
         weights = (scores * decay_mask).astype(BF)
-        attn = ein("hsnij,hsnje->hsnie", weights, values)
-        value_late = values.astype(F32) * key_decay
-        fresh = exact("hsnjd,hsnje->hsnde", keys, value_late)
-        local_state = jnp.zeros(fresh.shape[:2] + fresh.shape[3:], F32)
-        for n in range(spans):
-            local_state = span_decay * local_state + fresh[:, :, n]
-        state = jnp.zeros_like(local_state)
-        for hop in range(n_head - 1):
-            message = roll((local_state + rows_decay * state).astype(BF), -1)
-            state = lax.ppermute(message, "head", [(i, i + 1) for i in range(n_head - 1)]).astype(
-                F32
-            )
+        fresh = fresh.reshape(n_head, 2, spans, 2 * HEAD_DIM, HEAD_DIM)
+        state = carry.astype(F32)
         states = []
         for n in range(spans):
             states.append(state)
             state = span_decay * state + fresh[:, :, n]
         states = jnp.stack(states, axis=2)
-        attn = attn + query_decay * exact("hsnid,hsnde->hsnie", query, states)
         attn = attn.reshape(n_head, 2, rows, HEAD_DIM)
+        scale_attn = scale_attn[:, :1].reshape(1, 2, rows, 1)
+        attn_normed = attn * scale_attn
 
         def core_sum(array):
             return array + swap(array[::-1], 1)
 
-        squares = core_sum(jnp.sum(attn * attn, axis=(0, 3)))
-        scale_attn = lax.rsqrt(squares / width + EPSILON)[None, :, :, None]
-        attn_normed = attn * scale_attn
-        gated = (attn_normed * gate_pre).astype(BF).reshape(n_head, 2 * rows, HEAD_DIM)
-        out_w = jnp.concatenate([w[:, 4 * HEAD_DIM :] for w in attn_weights], axis=1)
-        gated = gated.transpose(1, 0, 2).reshape(2 * rows, n_head * HEAD_DIM)
-
         def core_scatter(array):
             return array[:rows] + swap(array[rows:].astype(BF), 1).astype(F32)
 
-        hidden = inputs + core_scatter(second_dot(gated, out_w))
         normed_two, scale_two = norm_parts(hidden)
-        normed_low = normed_two.astype(BF)
-        gathered_mid = jnp.concatenate([normed_low, swap(normed_low, 1)], axis=0)
         left = second_dot(gathered_mid, left_w)
         right = second_dot(gathered_mid, right_w)
         product = (left * right).astype(BF)
@@ -306,7 +848,7 @@
             main = first_dot(gathered_in, grad_pre[r]).astype(BF)
             outs = out_grads[:, r * HEAD_DIM : (r + 1) * HEAD_DIM].astype(BF)
             attn_grads.append(jnp.concatenate([main, outs], axis=1))
-            term = second_dot(grad_pre[r], attn_weights[r][:, : 4 * HEAD_DIM])
+            term = second_dot(grad_pre[r], attn_weights[r])
             grad_in = term if grad_in is None else grad_in + term
         grad_in = core_scatter(grad_in)
         input_grad = grad_hidden + norm_back(normed_one, scale_one, grad_in)

time: 683 us -> 560 us (0.82)
  Pallas kernels: 0 us -> 115 us
  waiting for transfers between devices: 241 us -> 149 us
  starting transfers between devices: 149 us -> 78.2 us
  local copies, waits for them, and re-layouts: 82.7 us -> 44.4 us
  other arithmetic: 77.5 us -> 54.4 us
  matrix products: 115 us -> 99.2 us
    pallas_call x0 -> x1, Pallas kernels: none -> 115 us  [forward(): pl.pallas_call(functools.partial(forward_kernel, n_head), out_shape=[jax....]
    ppermute x12 -> x0, waiting for transfers between devices: 60.7 us -> none  [the longest x3 47.1 us: on_device(): lax.ppermute(message, 'head', [(i, i + 1) for i in range(n_head - 1)])]
    ppermute x12 -> x0, starting transfers between devices: 38.5 us -> none  [the longest x3 19.3 us: on_device(): lax.ppermute(message, 'head', [(i, i + 1) for i in range(n_head - 1)])]
    ppermute x15, starting transfers between devices: 51.1 us -> 29.4 us  [to_above(): lax.ppermute(array, 'head', [(i, (i + step) % n_head) for i in range(n_he...]
    ppermute x15, waiting for transfers between devices: 47.1 us -> 34.6 us  [to_above(): lax.ppermute(array, 'head', [(i, (i + step) % n_head) for i in range(n_he...]
    ppermute x53 -> x41, waiting for transfers between devices: 100 us -> 88.6 us  [swap(): return lax.ppermute(array, 'dp', [(i, i ^ bit) for i in range(n_dp)])]
    dot_general x8 -> x4, matrix products: 26.3 us -> 14.9 us  [plain_dot(): return jnp.dot(left, right, preferred_element_type=F32)]
    unnamed x284 -> x150, local copies, waits for them, and re-layouts: 25.9 us -> 15.7 us
  transfers between devices with their start and end apart: 83 -> 59, of which waited for: 32 -> 22; matrix products, arithmetic and copies ran while one was open for 23% -> 16% of each run, Pallas kernels for 0% -> 21%
where the time goes in v2:
time: 560 us; the launch traced here: 551 us
  waiting for transfers between devices  149 us (27%)
  Pallas kernels  115 us (21%)
  matrix products  99.2 us (18%)
  starting transfers between devices  78.2 us (14%)
  other arithmetic  54.4 us (10%)
  local copies, waits for them, and re-layouts  44.4 us (8%)
  blocking collectives  7.2 us (1%)
    pallas_call x1, Pallas kernels, forward(): pl.pallas_call(functools.partial(forward_kernel, n_head), out_shape=[jax....  115 us
    ppermute x41, waiting for transfers between devices, swap(): return lax.ppermute(array, 'dp', [(i, i ^ bit) for i in range(n_dp)])  88.6 us
    ppermute x41, starting transfers between devices, swap(): return lax.ppermute(array, 'dp', [(i, i ^ bit) for i in range(n_dp)])  44.5 us
    dot_general x7, matrix products, second_dot(): lax.dot_general(left, right, (((1,), (1,)), ((), ())), preferred_element_...  41.7 us
    ppermute x15, waiting for transfers between devices, to_above(): lax.ppermute(array, 'head', [(i, (i + step) % n_head) for i in range(n_he...  34.6 us
    ppermute x15, starting transfers between devices, to_above(): lax.ppermute(array, 'head', [(i, (i + step) % n_head) for i in range(n_he...  29.4 us
    ppermute x3, waiting for transfers between devices, on_device(): lax.ppermute(message, 'head', [(i + 1, i) for i in range(n_head - 1)])  26.2 us
    dot_general x8, matrix products, first_dot(): lax.dot_general(left, right, (((0,), (0,)), ((), ())), preferred_element_...  23.3 us
  transfers between devices with their start and end apart: 59, of which 22 were waited for; matrix products, arithmetic and copies ran while one was open for 16% of the time, Pallas kernels for 21%

profile of v2, /device:TPU:1, one launch (start us, length us, event | category | flops | bytes accessed | tf_op | source)
XLA Modules:
  0.0 550.8 jit_solution(1214123298508186063)
XLA Ops:
  6.3 3.4 pad_maximum_fusion.ffn
  9.8 115.3 %forward.1 = (bf16[4,1024,512]{2,1,0:T(8,128)(2,1)}, bf16[512,1024]{1,0:T(8,128)(2,1)}, bf16[3,1408,1024]{2,1,0:T(8,128)(2,1)}, bf16[1024,1024]{1,0:T(8,128)(2,1...) custom-call(bf16[512,1024]{1,0:T(8,128)(2,1)} %tokens.1, ...), custom_call_target="tpu_custom_call" | custom-call | tf_op jit(solution)/shard_map/forward/pallas_call | solution.py:581
  128.2 8.9 %fusion.6 = f32[1024,1408]{1,0:T(8,128)} fusion(bf16[1024,1024]{1,0:T(8,128)(2,1)} %get-tuple-element.29, bf16[3,1408,1024]{2,1,0:T(8,128)(2,1)} %get-tuple-element.30), kind=kOutput, calls=%fused_computation.23 | convolution fusion | flops 2952790016 | bytes 10747904 | tf_op jit(solution)/shard_map/dot_general | solution.py:36
  139.5 5.5 fusion.10
  145.1 11.7 %multiply_convert_fusion.1 = (bf16[1024,1408]{1,0:T(8,128)(2,1)}, bf16[1024,1408]{1,0:T(8,128)(2,1)}, bf16[1024,1408]{1,0:T(8,128)(2,1)}) fusion(f32[1024,1408]{1,0:T(8,128)} %fusion.6, f32[1024,1408]{1,0:T(8,128)} %fusion.10, bf16[3,1408,1024]{2,1,0:T(8,128)(2,1)S(1)} %bitcast.267, bf16[512,1024]{1,0:T(8,128)(2,1)} %collective-permute-done.1, ...), kind=kOutput, calls=%fused_computation.1 | convolution fusion | flops 2971926528 | bytes 25165824 | tf_op jit(solution)/shard_map/dot_general | solution.py:36
  156.8 5.4 fusion.4
  162.1 3.4 convolution_convert_fusion.1
  165.6 3.6 convolution_convert_fusion.2
  169.3 3.5 fusion.37
  174.8 3.4 fusion.2
  178.5 5.3 convolution_convert_fusion
  186.9 6.5 %collective-permute-done.47 = bf16[4,176,256]{2,1,0:T(8,128)(2,1)S(1)} collective-permute-done((bf16[4,176,256]{2,1,0:T(8,128)(2,1)S(1)}, bf16[4,176,256]{2,1,0:T(8,128)(2,1)S(1)}, u32[]{:S(2)}, u32[]{:S(2)}) %collective-permute-start.47) | collective-permute-done | bytes 360480 | tf_op jit(solution)/shard_map/ppermute | solution.py:601
  195.1 6.0 %collective-permute-done.36 = bf16[4,176,256]{2,1,0:T(8,128)(2,1)S(1)} collective-permute-done((bf16[4,176,256]{2,1,0:T(8,128)(2,1)S(1)}, bf16[4,176,256]{2,1,0:T(8,128)(2,1)S(1)}, u32[]{:S(2)}, u32[]{:S(2)}) %collective-permute-start.36) | collective-permute-done | bytes 360480 | tf_op jit(solution)/shard_map/ppermute | solution.py:601
  203.0 5.9 %collective-permute-done.25 = bf16[4,176,256]{2,1,0:T(8,128)(2,1)S(1)} collective-permute-done((bf16[4,176,256]{2,1,0:T(8,128)(2,1)S(1)}, bf16[4,176,256]{2,1,0:T(8,128)(2,1)S(1)}, u32[]{:S(2)}, u32[]{:S(2)}) %collective-permute-start.25) | collective-permute-done | bytes 360480 | tf_op jit(solution)/shard_map/ppermute | solution.py:601
  212.8 2.2 fusion.89
  215.0 9.3 %collective-permute-done.50 = bf16[4,352,256]{2,1,0:T(8,128)(2,1)S(1)} collective-permute-done((bf16[4,352,256]{2,1,0:T(8,128)(2,1)S(1)}, bf16[4,352,256]{2,1,0:T(8,128)(2,1)S(1)}, u32[]{:S(2)}, u32[]{:S(2)}) %collective-permute-start.50) | collective-permute-done | bytes 720928 | tf_op jit(solution)/shard_map/ppermute | solution.py:601
  227.2 12.6 %collective-permute-done.39 = bf16[4,352,256]{2,1,0:T(8,128)(2,1)S(1)} collective-permute-done((bf16[4,352,256]{2,1,0:T(8,128)(2,1)S(1)}, bf16[4,352,256]{2,1,0:T(8,128)(2,1)S(1)}, u32[]{:S(2)}, u32[]{:S(2)}) %collective-permute-start.39) | collective-permute-done | bytes 720928 | tf_op jit(solution)/shard_map/ppermute | solution.py:601
  241.6 13.6 %collective-permute-done.28 = bf16[4,352,256]{2,1,0:T(8,128)(2,1)S(1)} collective-permute-done((bf16[4,352,256]{2,1,0:T(8,128)(2,1)S(1)}, bf16[4,352,256]{2,1,0:T(8,128)(2,1)S(1)}, u32[]{:S(2)}, u32[]{:S(2)}) %collective-permute-start.28) | collective-permute-done | bytes 720928 | tf_op jit(solution)/shard_map/ppermute | solution.py:601
  257.2 2.4 collective-permute-start.31
  261.1 5.9 %collective-permute-done.31 = bf16[352,256]{1,0:T(8,128)(2,1)S(1)} collective-permute-done((bf16[352,256]{1,0:T(8,128)(2,1)S(1)}, bf16[352,256]{1,0:T(8,128)(2,1)S(1)}, u32[]{:S(2)}, u32[]{:S(2)}) %collective-permute-start.31) | collective-permute-done | bytes 180256 | tf_op jit(solution)/shard_map/ppermute | solution.py:607
  267.1 15.6 %collective-permute-start.40 = (bf16[352,256]{1,0:T(8,128)(2,1)S(1)}, bf16[352,256]{1,0:T(8,128)(2,1)S(1)}, u32[]{:S(2)}, u32[]{:S(2)}) collective-permute-start(bf16[352,256]{1,0:T(8,128)(2,1)S(1)} %get-tuple-element.166), channel_id=1, source_target_pairs={{0,1},{1,2},{2,3},{3,0},{4,5},{5,6},{6,7},{7,4},{8,9},{9,10},{10,1... | collective-permute-start | bytes 540680 | tf_op jit(solution)/shard_map/ppermute | solution.py:607
  282.7 3.6 collective-permute-done.30
  290.8 3.9 collective-permute-done.33
  298.9 5.2 collective-permute-start.3
  313.4 2.6 fusion.43
  316.0 1.9 reshape.296
  318.0 2.8 multiply_reduce_fusion.1
  322.4 2.9 pad_maximum_fusion.2
  325.3 3.4 multiply_convert_fusion.7
  328.8 2.4 fusion.29
  336.3 11.7 %collective-permute-done.5 = bf16[4,2,256,128]{3,2,1,0:T(8,128)(2,1)S(1)} collective-permute-done((bf16[4,2,256,128]{3,2,1,0:T(8,128)(2,1)S(1)}, bf16[4,2,256,128]{3,2,1,0:T(8,128)(2,1)S(1)}, u32[]{:S(2)}, u32[]{:S(2)}) %collective-permute-start.5) | collective-permute-done | bytes 524320 | tf_op jit(solution)/shard_map/ppermute | solution.py:814
  350.7 2.8 fusion.99
  353.5 9.3 %collective-permute-done.6 = bf16[4,2,256,128]{3,2,1,0:T(8,128)(2,1)S(1)} collective-permute-done((bf16[4,2,256,128]{3,2,1,0:T(8,128)(2,1)S(1)}, bf16[4,2,256,128]{3,2,1,0:T(8,128)(2,1)S(1)}, u32[]{:S(2)}, u32[]{:S(2)}) %collective-permute-start.6) | collective-permute-done | bytes 524320 | tf_op jit(solution)/shard_map/ppermute | solution.py:814
  365.2 2.8 fusion.98
  368.0 4.5 fusion.40
  372.4 5.2 collective-permute-done.7
  378.8 2.3 fusion.45
  383.8 2.1 multiply_add_fusion
  386.3 2.1 multiply_add_fusion.1
  389.5 3.2 multiply_reduce_fusion
  396.2 3.3 fusion.50
  399.5 3.3 fusion.54
  404.2 2.3 convolution_convert_fusion.4
  409.1 2.9 convolution_convert_fusion.5
  413.2 2.4 pad_maximum_fusion.12
  415.6 2.9 stack.69
  418.5 3.1 convolution_convert_fusion.3
  422.8 4.0 stack.70
  430.5 2.4 slice_bitcast_fusion.5
  437.1 4.5 fusion.52
  442.7 4.0 collective-permute-start.58
  446.7 7.2 %psum.7 = f32[128]{0:T(128)S(1)} all-reduce(f32[128]{0:T(128)S(1)} %fusion.83), channel_id=1, replica_groups={{0,8,16,24},{4,12,20,28},{1,9,17,25},{5,13,21,29},{2,10,18,26},{6,14,22..., use_global_device_ids=true, to_apply=%region_6.7 | all-reduce | flops 128 | bytes 1024 | tf_op jit(solution)/shard_map/psum | solution.py:863
  453.9 1.9 collective-permute-start.24
  460.3 4.5 add_add_fusion
  466.2 2.1 broadcast_select_fusion.1
  468.3 19.5 %collective-permute-done.12 = bf16[4,256,640]{1,2,0:T(8,128)(2,1)S(1)} collective-permute-done((bf16[4,256,640]{1,2,0:T(8,128)(2,1)S(1)}, bf16[4,256,640]{1,2,0:T(8,128)(2,1)S(1)}, u32[]{:S(2)}, u32[]{:S(2)}) %collective-permute-start.12) | collective-permute-done | bytes 1310752 | tf_op jit(solution)/shard_map/ppermute | solution.py:601
  487.9 2.4 collective-permute-done.10
  492.2 2.4 collective-permute-start.15
  497.5 2.9 collective-permute-done.15
  500.5 22.1 %collective-permute-done.14 = bf16[256,640]{0,1:T(8,128)(2,1)S(1)} collective-permute-done((bf16[256,640]{0,1:T(8,128)(2,1)S(1)}, bf16[256,640]{0,1:T(8,128)(2,1)S(1)}, u32[]{:S(2)}, u32[]{:S(2)}) %collective-permute-start.14) | collective-permute-done | bytes 327712 | tf_op jit(solution)/shard_map/ppermute | solution.py:607
  523.4 3.7 slice_bitcast_fusion
  527.0 3.3 collective-permute-done.16
  531.7 2.9 collective-permute-done.18
  535.3 4.3 collective-permute-start.20
  (367 shorter events, 109.6 us)
Async XLA Ops:
  3.9 141.2 %collective-permute-start.1 = (bf16[512,1024]{1,0:T(8,128)(2,1)}, bf16[512,1024]{1,0:T(8,128)(2,1)}, u32[]{:S(2)}, u32[]{:S(2)}) collective-permute-start(bf16[512,1024]{1,0:T(8,128)(2,1)} %pad_maximum_fusion.18), channel_id=1, source_target_pairs={{0,4},{4,0},{8,12},{12,8},{16,20},{20,16},{24,28},{28,24},{1,5},{5... | collective-permute-start | bytes 3145736 | tf_op jit(solution)/shard_map/ppermute | solution.py:601
  5.7 121.6 %copy-start.22 = (bf16[512,256]{1,0:T(8,128)(2,1)}, bf16[512,256]{1,0:T(8,128)(2,1)S(1)}, u32[]{:S(2)}) copy-start(bf16[512,256]{1,0:T(8,128)(2,1)S(1)} %get-tuple-element.143) | copy-start | bytes 786436
  5.7 121.6 %copy-start.24 = (bf16[512,256]{1,0:T(8,128)(2,1)}, bf16[512,256]{1,0:T(8,128)(2,1)S(1)}, u32[]{:S(2)}) copy-start(bf16[512,256]{1,0:T(8,128)(2,1)S(1)} %get-tuple-element.144) | copy-start | bytes 786436
  5.7 121.6 %copy-start.26 = (bf16[512,256]{1,0:T(8,128)(2,1)}, bf16[512,256]{1,0:T(8,128)(2,1)S(1)}, u32[]{:S(2)}) copy-start(bf16[512,256]{1,0:T(8,128)(2,1)S(1)} %get-tuple-element.145) | copy-start | bytes 786436
  127.3 12.2 %slice-start.2 = ((s8[8650752]{0:T(1024)(128)(4,1)}), s8[4194304]{0:T(1024)(128)(4,1)S(1)}, s32[]{:S(2)}) async-start(s8[8650752]{0:T(1024)(128)(4,1)} %bitcast.266), calls=%async_computation.2 | async-start | bytes 8388608
  172.9 37.8 %collective-permute-start.2 = (bf16[512,1024]{1,0:T(8,128)(2,1)S(1)}, bf16[512,1024]{1,0:T(8,128)(2,1)S(1)}, u32[]{:S(2)}, u32[]{:S(2)}) collective-permute-start(bf16[512,1024]{1,0:T(8,128)(2,1)S(1)} %slice.721), channel_id=1, source_target_pairs={{0,4},{4,0},{8,12},{12,8},{16,20},{20,16},{24,28},{28,24},{1,5},{5... | collective-permute-start | bytes 3145736 | tf_op jit(solution)/shard_map/ppermute | solution.py:601
  178.4 34.1 %collective-permute-start = (bf16[512,1024]{1,0:T(8,128)(2,1)S(1)}, bf16[512,1024]{1,0:T(8,128)(2,1)S(1)}, u32[]{:S(2)}, u32[]{:S(2)}) collective-permute-start(bf16[512,1024]{1,0:T(8,128)(2,1)S(1)} %slice.722), channel_id=1, source_target_pairs={{0,4},{4,0},{8,12},{12,8},{16,20},{20,16},{24,28},{28,24},{1,5},{5... | collective-permute-start | bytes 3145736 | tf_op jit(solution)/shard_map/ppermute | solution.py:601
  183.9 9.6 %collective-permute-start.47 = (bf16[4,176,256]{2,1,0:T(8,128)(2,1)S(1)}, bf16[4,176,256]{2,1,0:T(8,128)(2,1)S(1)}, u32[]{:S(2)}, u32[]{:S(2)}) collective-permute-start(bf16[4,176,256]{2,1,0:T(8,128)(2,1)S(1)} %get-tuple-element.109), channel_id=1, source_target_pairs={{0,16},{4,20},{8,24},{12,28},{16,0},{20,4},{24,8},{28,12},{1,17},{... | collective-permute-start | bytes 1081352 | tf_op jit(solution)/shard_map/ppermute | solution.py:601
  185.1 9.5 %collective-permute-start.49 = (bf16[4,176,256]{2,1,0:T(8,128)(2,1)S(1)}, bf16[4,176,256]{2,1,0:T(8,128)(2,1)S(1)}, u32[]{:S(2)}, u32[]{:S(2)}) collective-permute-start(bf16[4,176,256]{2,1,0:T(8,128)(2,1)S(1)} %get-tuple-element.110), channel_id=1, source_target_pairs={{0,8},{4,12},{8,0},{12,4},{16,24},{20,28},{24,16},{28,20},{1,9},{5... | collective-permute-start | bytes 1081352 | tf_op jit(solution)/shard_map/ppermute | solution.py:601
  185.5 15.6 %collective-permute-start.36 = (bf16[4,176,256]{2,1,0:T(8,128)(2,1)S(1)}, bf16[4,176,256]{2,1,0:T(8,128)(2,1)S(1)}, u32[]{:S(2)}, u32[]{:S(2)}) collective-permute-start(bf16[4,176,256]{2,1,0:T(8,128)(2,1)S(1)} %get-tuple-element.103), channel_id=1, source_target_pairs={{0,16},{4,20},{8,24},{12,28},{16,0},{20,4},{24,8},{28,12},{1,17},{... | collective-permute-start | bytes 1081352 | tf_op jit(solution)/shard_map/ppermute | solution.py:601
  193.4 8.9 %collective-permute-start.38 = (bf16[4,176,256]{2,1,0:T(8,128)(2,1)S(1)}, bf16[4,176,256]{2,1,0:T(8,128)(2,1)S(1)}, u32[]{:S(2)}, u32[]{:S(2)}) collective-permute-start(bf16[4,176,256]{2,1,0:T(8,128)(2,1)S(1)} %get-tuple-element.104), channel_id=1, source_target_pairs={{0,8},{4,12},{8,0},{12,4},{16,24},{20,28},{24,16},{28,20},{1,9},{5... | collective-permute-start | bytes 1081352 | tf_op jit(solution)/shard_map/ppermute | solution.py:601
  194.6 14.2 %collective-permute-start.25 = (bf16[4,176,256]{2,1,0:T(8,128)(2,1)S(1)}, bf16[4,176,256]{2,1,0:T(8,128)(2,1)S(1)}, u32[]{:S(2)}, u32[]{:S(2)}) collective-permute-start(bf16[4,176,256]{2,1,0:T(8,128)(2,1)S(1)} %get-tuple-element.97), channel_id=1, source_target_pairs={{0,16},{4,20},{8,24},{12,28},{16,0},{20,4},{24,8},{28,12},{1,17},{... | collective-permute-start | bytes 1081352 | tf_op jit(solution)/shard_map/ppermute | solution.py:601
  201.1 8.9 %collective-permute-start.27 = (bf16[4,176,256]{2,1,0:T(8,128)(2,1)S(1)}, bf16[4,176,256]{2,1,0:T(8,128)(2,1)S(1)}, u32[]{:S(2)}, u32[]{:S(2)}) collective-permute-start(bf16[4,176,256]{2,1,0:T(8,128)(2,1)S(1)} %get-tuple-element.98), channel_id=1, source_target_pairs={{0,8},{4,12},{8,0},{12,4},{16,24},{20,28},{24,16},{28,20},{1,9},{5... | collective-permute-start | bytes 1081352 | tf_op jit(solution)/shard_map/ppermute | solution.py:601
  202.4 22.0 %collective-permute-start.50 = (bf16[4,352,256]{2,1,0:T(8,128)(2,1)S(1)}, bf16[4,352,256]{2,1,0:T(8,128)(2,1)S(1)}, u32[]{:S(2)}, u32[]{:S(2)}) collective-permute-start(bf16[4,352,256]{2,1,0:T(8,128)(2,1)S(1)} %pad_maximum_fusion.25), channel_id=1, source_target_pairs={{0,16},{4,20},{8,24},{12,28},{16,0},{20,4},{24,8},{28,12},{1,17},{... | collective-permute-start | bytes 2162696 | tf_op jit(solution)/shard_map/ppermute | solution.py:601
  208.9 16.7 %collective-permute-start.48 = (bf16[4,352,256]{2,1,0:T(8,128)(2,1)S(1)}, bf16[4,352,256]{2,1,0:T(8,128)(2,1)S(1)}, u32[]{:S(2)}, u32[]{:S(2)}) collective-permute-start(bf16[4,352,256]{2,1,0:T(8,128)(2,1)S(1)} %pad_maximum_fusion.24), channel_id=1, source_target_pairs={{0,8},{4,12},{8,0},{12,4},{16,24},{20,28},{24,16},{28,20},{1,9},{5... | collective-permute-start | bytes 2162696 | tf_op jit(solution)/shard_map/ppermute | solution.py:601
  210.1 29.7 %collective-permute-start.39 = (bf16[4,352,256]{2,1,0:T(8,128)(2,1)S(1)}, bf16[4,352,256]{2,1,0:T(8,128)(2,1)S(1)}, u32[]{:S(2)}, u32[]{:S(2)}) collective-permute-start(bf16[4,352,256]{2,1,0:T(8,128)(2,1)S(1)} %pad_maximum_fusion.23), channel_id=1, source_target_pairs={{0,16},{4,20},{8,24},{12,28},{16,0},{20,4},{24,8},{28,12},{1,17},{... | collective-permute-start | bytes 2162696 | tf_op jit(solution)/shard_map/ppermute | solution.py:601
  210.7 29.1 %collective-permute-start.37 = (bf16[4,352,256]{2,1,0:T(8,128)(2,1)S(1)}, bf16[4,352,256]{2,1,0:T(8,128)(2,1)S(1)}, u32[]{:S(2)}, u32[]{:S(2)}) collective-permute-start(bf16[4,352,256]{2,1,0:T(8,128)(2,1)S(1)} %pad_maximum_fusion.22), channel_id=1, source_target_pairs={{0,8},{4,12},{8,0},{12,4},{16,24},{20,28},{24,16},{28,20},{1,9},{5... | collective-permute-start | bytes 2162696 | tf_op jit(solution)/shard_map/ppermute | solution.py:601
  212.5 42.7 %collective-permute-start.28 = (bf16[4,352,256]{2,1,0:T(8,128)(2,1)S(1)}, bf16[4,352,256]{2,1,0:T(8,128)(2,1)S(1)}, u32[]{:S(2)}, u32[]{:S(2)}) collective-permute-start(bf16[4,352,256]{2,1,0:T(8,128)(2,1)S(1)} %pad_maximum_fusion.21), channel_id=1, source_target_pairs={{0,16},{4,20},{8,24},{12,28},{16,0},{20,4},{24,8},{28,12},{1,17},{... | collective-permute-start | bytes 2162696 | tf_op jit(solution)/shard_map/ppermute | solution.py:601
  215.0 97.5 %copy-start.44 = (bf16[512,1024]{1,0:T(8,128)(2,1)}, bf16[512,1024]{1,0:T(8,128)(2,1)S(1)}, u32[]{:S(2)}) copy-start(bf16[512,1024]{1,0:T(8,128)(2,1)S(1)} %get-tuple-element.73) | copy-start | bytes 3145732
  224.3 32.4 %collective-permute-start.26 = (bf16[4,352,256]{2,1,0:T(8,128)(2,1)S(1)}, bf16[4,352,256]{2,1,0:T(8,128)(2,1)S(1)}, u32[]{:S(2)}, u32[]{:S(2)}) collective-permute-start(bf16[4,352,256]{2,1,0:T(8,128)(2,1)S(1)} %pad_maximum_fusion.20), channel_id=1, source_target_pairs={{0,8},{4,12},{8,0},{12,4},{16,24},{20,28},{24,16},{28,20},{1,9},{5... | collective-permute-start | bytes 2162696 | tf_op jit(solution)/shard_map/ppermute | solution.py:601
  226.0 31.2 %collective-permute-start.53 = (bf16[352,256]{1,0:T(8,128)(2,1)S(1)}, bf16[352,256]{1,0:T(8,128)(2,1)S(1)}, u32[]{:S(2)}, u32[]{:S(2)}) collective-permute-start(bf16[352,256]{1,0:T(8,128)(2,1)S(1)} %get-tuple-element.174), channel_id=1, source_target_pairs={{0,3},{1,0},{2,1},{3,2},{4,7},{5,4},{6,5},{7,6},{8,11},{9,8},{10,9... | collective-permute-start | bytes 540680 | tf_op jit(solution)/shard_map/ppermute | solution.py:607
  239.8 19.8 %collective-permute-start.52 = (bf16[352,256]{1,0:T(8,128)(2,1)S(1)}, bf16[352,256]{1,0:T(8,128)(2,1)S(1)}, u32[]{:S(2)}, u32[]{:S(2)}) collective-permute-start(bf16[352,256]{1,0:T(8,128)(2,1)S(1)} %get-tuple-element.175), channel_id=1, source_target_pairs={{0,2},{1,3},{2,0},{3,1},{4,6},{5,7},{6,4},{7,5},{8,10},{9,11},{10,... | collective-permute-start | bytes 540680 | tf_op jit(solution)/shard_map/ppermute | solution.py:607
  239.8 19.9 %collective-permute-start.51 = (bf16[352,256]{1,0:T(8,128)(2,1)S(1)}, bf16[352,256]{1,0:T(8,128)(2,1)S(1)}, u32[]{:S(2)}, u32[]{:S(2)}) collective-permute-start(bf16[352,256]{1,0:T(8,128)(2,1)S(1)} %get-tuple-element.173), channel_id=1, source_target_pairs={{0,1},{1,2},{2,3},{3,0},{4,5},{5,6},{6,7},{7,4},{8,9},{9,10},{10,1... | collective-permute-start | bytes 540680 | tf_op jit(solution)/shard_map/ppermute | solution.py:607
  255.2 32.7 %collective-permute-start.42 = (bf16[352,256]{1,0:T(8,128)(2,1)S(1)}, bf16[352,256]{1,0:T(8,128)(2,1)S(1)}, u32[]{:S(2)}, u32[]{:S(2)}) collective-permute-start(bf16[352,256]{1,0:T(8,128)(2,1)S(1)} %get-tuple-element.167), channel_id=1, source_target_pairs={{0,3},{1,0},{2,1},{3,2},{4,7},{5,4},{6,5},{7,6},{8,11},{9,8},{10,9... | collective-permute-start | bytes 540680 | tf_op jit(solution)/shard_map/ppermute | solution.py:607
  256.8 32.4 %collective-permute-start.41 = (bf16[352,256]{1,0:T(8,128)(2,1)S(1)}, bf16[352,256]{1,0:T(8,128)(2,1)S(1)}, u32[]{:S(2)}, u32[]{:S(2)}) collective-permute-start(bf16[352,256]{1,0:T(8,128)(2,1)S(1)} %get-tuple-element.168), channel_id=1, source_target_pairs={{0,2},{1,3},{2,0},{3,1},{4,6},{5,7},{6,4},{7,5},{8,10},{9,11},{10,... | collective-permute-start | bytes 540680 | tf_op jit(solution)/shard_map/ppermute | solution.py:607
  257.2 9.9 %collective-permute-start.31 = (bf16[352,256]{1,0:T(8,128)(2,1)S(1)}, bf16[352,256]{1,0:T(8,128)(2,1)S(1)}, u32[]{:S(2)}, u32[]{:S(2)}) collective-permute-start(bf16[352,256]{1,0:T(8,128)(2,1)S(1)} %get-tuple-element.160), channel_id=1, source_target_pairs={{0,3},{1,0},{2,1},{3,2},{4,7},{5,4},{6,5},{7,6},{8,11},{9,8},{10,9... | collective-permute-start | bytes 540680 | tf_op jit(solution)/shard_map/ppermute | solution.py:607
  259.6 26.7 %collective-permute-start.30 = (bf16[352,256]{1,0:T(8,128)(2,1)S(1)}, bf16[352,256]{1,0:T(8,128)(2,1)S(1)}, u32[]{:S(2)}, u32[]{:S(2)}) collective-permute-start(bf16[352,256]{1,0:T(8,128)(2,1)S(1)} %get-tuple-element.161), channel_id=1, source_target_pairs={{0,2},{1,3},{2,0},{3,1},{4,6},{5,7},{6,4},{7,5},{8,10},{9,11},{10,... | collective-permute-start | bytes 540680 | tf_op jit(solution)/shard_map/ppermute | solution.py:607
  259.7 27.9 %collective-permute-start.29 = (bf16[352,256]{1,0:T(8,128)(2,1)S(1)}, bf16[352,256]{1,0:T(8,128)(2,1)S(1)}, u32[]{:S(2)}, u32[]{:S(2)}) collective-permute-start(bf16[352,256]{1,0:T(8,128)(2,1)S(1)} %get-tuple-element.159), channel_id=1, source_target_pairs={{0,1},{1,2},{2,3},{3,0},{4,5},{5,6},{6,7},{7,4},{8,9},{9,10},{10,1... | collective-permute-start | bytes 540680 | tf_op jit(solution)/shard_map/ppermute | solution.py:607
  267.1 22.3 %collective-permute-start.40 = (bf16[352,256]{1,0:T(8,128)(2,1)S(1)}, bf16[352,256]{1,0:T(8,128)(2,1)S(1)}, u32[]{:S(2)}, u32[]{:S(2)}) collective-permute-start(bf16[352,256]{1,0:T(8,128)(2,1)S(1)} %get-tuple-element.166), channel_id=1, source_target_pairs={{0,1},{1,2},{2,3},{3,0},{4,5},{5,6},{6,7},{7,4},{8,9},{9,10},{10,1... | collective-permute-start | bytes 540680 | tf_op jit(solution)/shard_map/ppermute | solution.py:607
  286.3 10.1 %collective-permute-start.55 = (bf16[352,256]{1,0:T(8,128)(2,1)S(1)}, bf16[352,256]{1,0:T(8,128)(2,1)S(1)}, u32[]{:S(2)}, u32[]{:S(2)}) collective-permute-start(bf16[352,256]{1,0:T(8,128)(2,1)S(1)} %fusion.65), channel_id=1, source_target_pairs={{0,16},{4,20},{8,24},{12,28},{16,0},{20,4},{24,8},{28,12},{1,17},{... | collective-permute-start | bytes 540680 | tf_op jit(solution)/shard_map/ppermute | solution.py:601
  287.5 11.3 %collective-permute-start.54 = (bf16[352,256]{1,0:T(8,128)(2,1)S(1)}, bf16[352,256]{1,0:T(8,128)(2,1)S(1)}, u32[]{:S(2)}, u32[]{:S(2)}) collective-permute-start(bf16[352,256]{1,0:T(8,128)(2,1)S(1)} %fusion.65), channel_id=1, source_target_pairs={{0,8},{4,12},{8,0},{12,4},{16,24},{20,28},{24,16},{28,20},{1,9},{5... | collective-permute-start | bytes 540680 | tf_op jit(solution)/shard_map/ppermute | solution.py:601
  287.9 6.8 %collective-permute-start.33 = (bf16[352,256]{1,0:T(8,128)(2,1)S(1)}, bf16[352,256]{1,0:T(8,128)(2,1)S(1)}, u32[]{:S(2)}, u32[]{:S(2)}) collective-permute-start(bf16[352,256]{1,0:T(8,128)(2,1)S(1)} %fusion.71), channel_id=1, source_target_pairs={{0,16},{4,20},{8,24},{12,28},{16,0},{20,4},{24,8},{28,12},{1,17},{... | collective-permute-start | bytes 540680 | tf_op jit(solution)/shard_map/ppermute | solution.py:601
  289.2 6.9 %collective-permute-start.32 = (bf16[352,256]{1,0:T(8,128)(2,1)S(1)}, bf16[352,256]{1,0:T(8,128)(2,1)S(1)}, u32[]{:S(2)}, u32[]{:S(2)}) collective-permute-start(bf16[352,256]{1,0:T(8,128)(2,1)S(1)} %fusion.71), channel_id=1, source_target_pairs={{0,8},{4,12},{8,0},{12,4},{16,24},{20,28},{24,16},{28,20},{1,9},{5... | collective-permute-start | bytes 540680 | tf_op jit(solution)/shard_map/ppermute | solution.py:601
  289.5 14.6 %collective-permute-start.44 = (bf16[352,256]{1,0:T(8,128)(2,1)S(1)}, bf16[352,256]{1,0:T(8,128)(2,1)S(1)}, u32[]{:S(2)}, u32[]{:S(2)}) collective-permute-start(bf16[352,256]{1,0:T(8,128)(2,1)S(1)} %fusion.68), channel_id=1, source_target_pairs={{0,16},{4,20},{8,24},{12,28},{16,0},{20,4},{24,8},{28,12},{1,17},{... | collective-permute-start | bytes 540680 | tf_op jit(solution)/shard_map/ppermute | solution.py:601
  294.7 9.7 %collective-permute-start.43 = (bf16[352,256]{1,0:T(8,128)(2,1)S(1)}, bf16[352,256]{1,0:T(8,128)(2,1)S(1)}, u32[]{:S(2)}, u32[]{:S(2)}) collective-permute-start(bf16[352,256]{1,0:T(8,128)(2,1)S(1)} %fusion.68), channel_id=1, source_target_pairs={{0,8},{4,12},{8,0},{12,4},{16,24},{20,28},{24,16},{28,20},{1,9},{5... | collective-permute-start | bytes 540680 | tf_op jit(solution)/shard_map/ppermute | solution.py:601
  296.1 9.6 %collective-permute-start.35 = (bf16[176,256]{1,0:T(8,128)(2,1)S(1)}, bf16[176,256]{1,0:T(8,128)(2,1)S(1)}, u32[]{:S(2)}, u32[]{:S(2)}) collective-permute-start(bf16[176,256]{1,0:T(8,128)(2,1)S(1)} %slice.553), channel_id=1, source_target_pairs={{0,8},{4,12},{8,0},{12,4},{16,24},{20,28},{24,16},{28,20},{1,9},{5... | collective-permute-start | bytes 270344 | tf_op jit(solution)/shard_map/ppermute | solution.py:601
  296.4 9.6 %collective-permute-start.34 = (bf16[176,256]{1,0:T(8,128)(2,1)S(1)}, bf16[176,256]{1,0:T(8,128)(2,1)S(1)}, u32[]{:S(2)}, u32[]{:S(2)}) collective-permute-start(bf16[176,256]{1,0:T(8,128)(2,1)S(1)} %slice.552), channel_id=1, source_target_pairs={{0,16},{4,20},{8,24},{12,28},{16,0},{20,4},{24,8},{28,12},{1,17},{... | collective-permute-start | bytes 270344 | tf_op jit(solution)/shard_map/ppermute | solution.py:601
  298.9 13.6 %collective-permute-start.3 = (bf16[512,1024]{1,0:T(8,128)(2,1)S(1)}, bf16[512,1024]{1,0:T(8,128)(2,1)S(1)}, u32[]{:S(2)}, u32[]{:S(2)}) collective-permute-start(bf16[512,1024]{1,0:T(8,128)(2,1)S(1)} %get-tuple-element.73), channel_id=1, source_target_pairs={{0,4},{4,0},{8,12},{12,8},{16,20},{20,16},{24,28},{28,24},{1,5},{5... | collective-permute-start | bytes 3145736 | tf_op jit(solution)/shard_map/ppermute | solution.py:601
  304.1 4.3 collective-permute-start.57
  304.4 4.0 collective-permute-start.56
  305.7 4.3 collective-permute-start.46
  306.0 4.1 collective-permute-start.45
  320.9 4.4 collective-permute-start.4
  332.6 15.4 %collective-permute-start.5 = (bf16[4,2,256,128]{3,2,1,0:T(8,128)(2,1)S(1)}, bf16[4,2,256,128]{3,2,1,0:T(8,128)(2,1)S(1)}, u32[]{:S(2)}, u32[]{:S(2)}) collective-permute-start(bf16[4,2,256,128]{3,2,1,0:T(8,128)(2,1)S(1)} %pad_maximum_fusion.26), channel_id=1, source_target_pairs={{1,0},{2,1},{3,2},{5,4},{6,5},{7,6},{9,8},{10,9},{11,10},{13,12},{... | collective-permute-start | bytes 1572872 | tf_op jit(solution)/shard_map/ppermute | solution.py:814
  348.3 14.5 %collective-permute-start.6 = (bf16[4,2,256,128]{3,2,1,0:T(8,128)(2,1)S(1)}, bf16[4,2,256,128]{3,2,1,0:T(8,128)(2,1)S(1)}, u32[]{:S(2)}, u32[]{:S(2)}) collective-permute-start(bf16[4,2,256,128]{3,2,1,0:T(8,128)(2,1)S(1)} %pad_maximum_fusion.27), channel_id=1, source_target_pairs={{1,0},{2,1},{3,2},{5,4},{6,5},{7,6},{9,8},{10,9},{11,10},{13,12},{... | collective-permute-start | bytes 1572872 | tf_op jit(solution)/shard_map/ppermute | solution.py:814
  363.9 13.7 %collective-permute-start.7 = (bf16[4,2,256,128]{3,2,1,0:T(8,128)(2,1)}, bf16[4,2,256,128]{3,2,1,0:T(8,128)(2,1)}, u32[]{:S(2)}, u32[]{:S(2)}) collective-permute-start(bf16[4,2,256,128]{3,2,1,0:T(8,128)(2,1)} %pad_maximum_fusion.28), channel_id=1, source_target_pairs={{1,0},{2,1},{3,2},{5,4},{6,5},{7,6},{9,8},{10,9},{11,10},{13,12},{... | collective-permute-start | bytes 1572872 | tf_op jit(solution)/shard_map/ppermute | solution.py:814
  434.2 21.6 %collective-permute-start.11 = (bf16[4,128,640]{1,2,0:T(8,128)(2,1)}, bf16[4,128,640]{1,2,0:T(8,128)(2,1)}, u32[]{:S(2)}, u32[]{:S(2)}) collective-permute-start(bf16[4,128,640]{1,2,0:T(8,128)(2,1)} %get-tuple-element.138), channel_id=1, source_target_pairs={{0,8},{4,12},{8,0},{12,4},{16,24},{20,28},{24,16},{28,20},{1,9},{5... | collective-permute-start | bytes 1966088 | tf_op jit(solution)/shard_map/ppermute | solution.py:601
  435.3 23.2 %collective-permute-start.9 = (bf16[4,128,640]{1,2,0:T(8,128)(2,1)}, bf16[4,128,640]{1,2,0:T(8,128)(2,1)}, u32[]{:S(2)}, u32[]{:S(2)}) collective-permute-start(bf16[4,128,640]{1,2,0:T(8,128)(2,1)} %get-tuple-element.137), channel_id=1, source_target_pairs={{0,16},{4,20},{8,24},{12,28},{16,0},{20,4},{24,8},{28,12},{1,17},{... | collective-permute-start | bytes 1966088 | tf_op jit(solution)/shard_map/ppermute | solution.py:601
  435.7 7.0 %collective-permute-start.23 = (f32[128]{0:T(128)S(1)}, f32[128]{0:T(128)S(1)}, u32[]{:S(2)}, u32[]{:S(2)}) collective-permute-start(f32[128]{0:T(128)S(1)} %get-tuple-element.177), channel_id=1, source_target_pairs={{0,3},{1,0},{2,1},{3,2},{4,7},{5,4},{6,5},{7,6},{8,11},{9,8},{10,9... | collective-permute-start | bytes 1544 | tf_op jit(solution)/shard_map/ppermute | solution.py:607
  435.7 11.0 %collective-permute-start.22 = (f32[128]{0:T(128)S(1)}, f32[128]{0:T(128)S(1)}, u32[]{:S(2)}, u32[]{:S(2)}) collective-permute-start(f32[128]{0:T(128)S(1)} %get-tuple-element.178), channel_id=1, source_target_pairs={{0,2},{1,3},{2,0},{3,1},{4,6},{5,7},{6,4},{7,5},{8,10},{9,11},{10,... | collective-permute-start | bytes 1544 | tf_op jit(solution)/shard_map/ppermute | solution.py:607
  436.1 10.6 %collective-permute-start.21 = (f32[128]{0:T(128)S(1)}, f32[128]{0:T(128)S(1)}, u32[]{:S(2)}, u32[]{:S(2)}) collective-permute-start(f32[128]{0:T(128)S(1)} %get-tuple-element.176), channel_id=1, source_target_pairs={{0,1},{1,2},{2,3},{3,0},{4,5},{5,6},{6,7},{7,4},{8,9},{9,10},{10,1... | collective-permute-start | bytes 1544 | tf_op jit(solution)/shard_map/ppermute | solution.py:607
  442.7 23.5 %collective-permute-start.58 = (bf16[3,352,1024]{2,1,0:T(8,128)(2,1)}, bf16[3,352,1024]{2,1,0:T(8,128)(2,1)}, u32[]{:S(2)}, u32[]{:S(2)}) collective-permute-start(bf16[3,352,1024]{2,1,0:T(8,128)(2,1)} %pad_maximum_fusion.2), channel_id=1, source_target_pairs={{0,4},{4,0},{8,12},{12,8},{16,20},{20,16},{24,28},{28,24},{1,5},{5... | collective-permute-start | bytes 6488072 | tf_op jit(solution)/shard_map/ppermute | solution.py:601
  453.9 11.7 %collective-permute-start.24 = (f32[128]{0:T(128)S(1)}, f32[128]{0:T(128)S(1)}, u32[]{:S(2)}, u32[]{:S(2)}) collective-permute-start(f32[128]{0:T(128)S(1)} %psum.7), channel_id=1, source_target_pairs={{0,4},{4,0},{8,12},{12,8},{16,20},{20,16},{24,28},{28,24},{1,5},{5... | collective-permute-start | bytes 1544 | tf_op jit(solution)/shard_map/ppermute | solution.py:601
  457.4 30.4 %collective-permute-start.12 = (bf16[4,256,640]{1,2,0:T(8,128)(2,1)S(1)}, bf16[4,256,640]{1,2,0:T(8,128)(2,1)S(1)}, u32[]{:S(2)}, u32[]{:S(2)}) collective-permute-start(bf16[4,256,640]{1,2,0:T(8,128)(2,1)S(1)} %pad_maximum_fusion.15), channel_id=1, source_target_pairs={{0,16},{4,20},{8,24},{12,28},{16,0},{20,4},{24,8},{28,12},{1,17},{... | collective-permute-start | bytes 3932168 | tf_op jit(solution)/shard_map/ppermute | solution.py:601
  460.0 30.2 %collective-permute-start.10 = (bf16[4,256,640]{1,2,0:T(8,128)(2,1)S(1)}, bf16[4,256,640]{1,2,0:T(8,128)(2,1)S(1)}, u32[]{:S(2)}, u32[]{:S(2)}) collective-permute-start(bf16[4,256,640]{1,2,0:T(8,128)(2,1)S(1)} %pad_maximum_fusion.14), channel_id=1, source_target_pairs={{0,8},{4,12},{8,0},{12,4},{16,24},{20,28},{24,16},{28,20},{1,9},{5... | collective-permute-start | bytes 3932168 | tf_op jit(solution)/shard_map/ppermute | solution.py:601
  465.0 74.6 %collective-permute-start.8 = (bf16[512,1024]{1,0:T(8,128)(2,1)S(1)}, bf16[512,1024]{1,0:T(8,128)(2,1)S(1)}, u32[]{:S(2)}, u32[]{:S(2)}) collective-permute-start(bf16[512,1024]{1,0:T(8,128)(2,1)S(1)} %slice.720), channel_id=1, source_target_pairs={{0,4},{4,0},{8,12},{12,8},{16,20},{20,16},{24,28},{28,24},{1,5},{5... | collective-permute-start | bytes 3145736 | tf_op jit(solution)/shard_map/ppermute | solution.py:601
  492.2 8.3 %collective-permute-start.15 = (bf16[256,640]{0,1:T(8,128)(2,1)S(1)}, bf16[256,640]{0,1:T(8,128)(2,1)S(1)}, u32[]{:S(2)}, u32[]{:S(2)}) collective-permute-start(bf16[256,640]{0,1:T(8,128)(2,1)S(1)} %get-tuple-element.135), channel_id=1, source_target_pairs={{0,3},{1,0},{2,1},{3,2},{4,7},{5,4},{6,5},{7,6},{8,11},{9,8},{10,9... | collective-permute-start | bytes 983048 | tf_op jit(solution)/shard_map/ppermute | solution.py:607
  494.5 28.1 %collective-permute-start.14 = (bf16[256,640]{0,1:T(8,128)(2,1)S(1)}, bf16[256,640]{0,1:T(8,128)(2,1)S(1)}, u32[]{:S(2)}, u32[]{:S(2)}) collective-permute-start(bf16[256,640]{0,1:T(8,128)(2,1)S(1)} %get-tuple-element.136), channel_id=1, source_target_pairs={{0,2},{1,3},{2,0},{3,1},{4,6},{5,7},{6,4},{7,5},{8,10},{9,11},{10,... | collective-permute-start | bytes 983048 | tf_op jit(solution)/shard_map/ppermute | solution.py:607
  494.7 27.9 %collective-permute-start.13 = (bf16[256,640]{0,1:T(8,128)(2,1)S(1)}, bf16[256,640]{0,1:T(8,128)(2,1)S(1)}, u32[]{:S(2)}, u32[]{:S(2)}) collective-permute-start(bf16[256,640]{0,1:T(8,128)(2,1)S(1)} %get-tuple-element.134), channel_id=1, source_target_pairs={{0,1},{1,2},{2,3},{3,0},{4,5},{5,6},{6,7},{7,4},{8,9},{9,10},{10,1... | collective-permute-start | bytes 983048 | tf_op jit(solution)/shard_map/ppermute | solution.py:607
  522.8 7.5 %collective-permute-start.16 = (bf16[256,640]{0,1:T(8,128)(2,1)S(1)}, bf16[256,640]{0,1:T(8,128)(2,1)S(1)}, u32[]{:S(2)}, u32[]{:S(2)}) collective-permute-start(bf16[256,640]{0,1:T(8,128)(2,1)S(1)} %get-tuple-element.68), channel_id=1, source_target_pairs={{0,8},{4,12},{8,0},{12,4},{16,24},{20,28},{24,16},{28,20},{1,9},{5... | collective-permute-start | bytes 983048 | tf_op jit(solution)/shard_map/ppermute | solution.py:601
  523.1 7.4 %collective-permute-start.17 = (bf16[256,640]{0,1:T(8,128)(2,1)S(1)}, bf16[256,640]{0,1:T(8,128)(2,1)S(1)}, u32[]{:S(2)}, u32[]{:S(2)}) collective-permute-start(bf16[256,640]{0,1:T(8,128)(2,1)S(1)} %get-tuple-element.68), channel_id=1, source_target_pairs={{0,16},{4,20},{8,24},{12,28},{16,0},{20,4},{24,8},{28,12},{1,17},{... | collective-permute-start | bytes 983048 | tf_op jit(solution)/shard_map/ppermute | solution.py:601
  530.3 4.2 collective-permute-start.18
  530.6 4.2 collective-permute-start.19
  535.3 7.4 %collective-permute-start.20 = (bf16[1024,640]{0,1:T(8,128)(2,1)S(1)}, bf16[1024,640]{0,1:T(8,128)(2,1)S(1)}, u32[]{:S(2)}, u32[]{:S(2)}) collective-permute-start(bf16[1024,640]{0,1:T(8,128)(2,1)S(1)} %pad_maximum_fusion.16), channel_id=1, source_target_pairs={{0,4},{4,0},{8,12},{12,8},{16,20},{20,16},{24,28},{28,24},{1,5},{5... | collective-permute-start | bytes 3932168 | tf_op jit(solution)/shard_map/ppermute | solution.py:601
  (65 other events, 258.6 us)

commit v3 on v2

--- a/solution.py
+++ b/solution.py
@@ -62,6 +62,9 @@
         self.up = {"head": lax.rem(self.z + 1, n_head)}
         self.down = {"head": lax.rem(self.z + n_head - 1, n_head)}
 
+    def above(self, step):
+        return {"head": lax.rem(self.z + step, self.n_head)}
+
     def below(self, step):
         return {"head": lax.rem(self.z + self.n_head - step, self.n_head)}
 
@@ -78,6 +81,7 @@
     def __init__(self, sends, receives, locals_):
         self.sends, self.receives, self.locals = sends, receives, locals_
         self.pending = []
+        self.started = {}
         self.n_local = 0
 
     def send(self, src, dst, out, into, device, when=None):
@@ -92,6 +96,8 @@
         if when is None:
             copy.start()
             self.pending.append(copy.wait_send)
+            if isinstance(out, int):
+                self.started[out] = copy.wait_send
         else:
             pl.when(when)(copy.start)
             self.pending.append(lambda: pl.when(when)(copy.wait_send))
@@ -113,6 +119,11 @@
         if later:
             self.pending.append(copy.wait)
         return copy
+
+    def sent(self, out):
+        wait = self.started.pop(out)
+        self.pending.remove(wait)
+        wait()
 
     def finish(self):
         for wait in self.pending:
@@ -169,6 +180,7 @@
 def forward_kernel(
     n_head,
     tokens,
+    out_grad,
     wq,
     wk,
     wv,
@@ -193,6 +205,7 @@
     gated_out,
     hidden_out,
     nm_out,
+    og_out,
     wa_ref,
     wo_ref,
     wf_ref,
@@ -216,6 +229,7 @@
     hidden_ref,
     nm_ref,
     rates_ref,
+    og_ref,
     sends,
     receives,
     locals_,
@@ -251,6 +265,13 @@
         )
         for q in range(4)
     ]
+    grad_loads = [
+        copies.move(
+            out_grad.at[:, columns(place.at[q] * quarter, quarter)],
+            og_ref.at[pl.ds(0, rows), pl.ds(q * quarter, quarter)],
+        )
+        for q in range(4)
+    ]
     place.greet()
 
     def half_rows(half, size):
@@ -301,6 +322,11 @@
         nin_ref[at, :] = norm_rows(x_ref[at, :].astype(F32)).astype(BF)
 
     base += 4
+    for load in grad_loads:
+        load.wait()
+    og_other = og_ref.at[pl.ds(rows, rows)]
+    copies.send(og_ref.at[pl.ds(0, rows)], og_other, base, base, place.across)
+    base += 1
     nin_other = nin_ref.at[pl.ds(rows, rows)]
     copies.send(nin_ref.at[pl.ds(0, rows)], nin_other, base, base, place.across)
     own_loads[0][5].wait()
@@ -309,9 +335,11 @@
         for load in loads:
             load.wait()
     for step in range(1, n_head):
-        copies.receive(rates_ref.at[step], base - 4 + step, place.up)
+        copies.receive(rates_ref.at[step], base - 5 + step, place.up)
     copies.receive(nin_other, base, place.across)
     copies.move(nin_ref, nin_out, later=True)
+    copies.receive(og_other, base - 1, place.across)
+    copies.move(og_ref, og_out, later=True)
 
     def decay_of(head):
         exponent = jnp.full((1, 1), -8.0 / HEADS, F32) * (head + 1).astype(F32)
@@ -547,7 +575,7 @@
     copies.finish()
 
 
-def forward(n_head, tokens, wq, wk, wv, wg, wo, ffn, rates):
+def forward(n_head, tokens, out_grad, wq, wk, wv, wg, wo, ffn, rates):
     rows, width = tokens.shape
     units = ffn.shape[1] // 2
     tall = 2 * rows
@@ -575,13 +603,14 @@
         ((rows, width), F32),
         ((tall, width), BF),
         ((n_head, 8, HEAD_DIM), F32),
+        ((tall, width), BF),
     ]
-    out_of = [0, 1, 2, 4, 5, 6, 7, 8, 9, 10, 11, 12, 13, 16, 17, 20, 21]
-    n_sems = 3 * PER_GATHER + 4 + 1 + 2 * n_head + 2 + 2
+    out_of = [0, 1, 2, 4, 5, 6, 7, 8, 9, 10, 11, 12, 13, 16, 17, 20, 21, 23]
+    n_sems = 3 * PER_GATHER + 4 + 1 + 1 + 2 * n_head + 2 + 2
     return pl.pallas_call(
         functools.partial(forward_kernel, n_head),
         out_shape=[jax.ShapeDtypeStruct(*buffers[i]) for i in out_of],
-        in_specs=[ANY] * 7 + [IN_VMEM],
+        in_specs=[ANY] * 8 + [IN_VMEM],
         out_specs=[ANY] * len(out_of),
         scratch_shapes=[pltpu.VMEM(*b) for b in buffers]
         + [
@@ -593,7 +622,527 @@
             collective_id=0, has_side_effects=True, vmem_limit_bytes=62 << 20
         ),
         name="forward",
-    )(tokens, wq, wk, wv, wg, wo, ffn, rates)
+    )(tokens, out_grad, wq, wk, wv, wg, wo, ffn, rates)
+
+
+class Scatter:
+    def __init__(self, place, copies, view, far_x, far_y, near_x, near_y, high, base):
+        self.place, self.copies, self.view, self.base = place, copies, view, base
+        self.far_x, self.far_y, self.near_x, self.near_y, self.high = far_x, far_y, near_x, near_y, high
+
+    def begin(self, slot):
+        place, at = self.place, self.base + 4 * slot
+        self.copies.send(self.view(slot, 3, 0), self.far_y.at[slot], at, at, place.by_y)
+        self.copies.send(self.view(slot, 3, 1), self.far_x.at[slot], at + 1, at + 1, place.by_x)
+
+    def middle(self, slot):
+        place, copies, at = self.place, self.copies, self.base + 4 * slot
+        copies.receive(self.far_y.at[slot], at, place.by_y)
+        add_to(self.view(slot, 1, 0), self.far_y.at[slot])
+        copies.send(self.view(slot, 1, None), self.near_x.at[slot], at + 2, at + 2, place.by_x)
+        copies.receive(self.far_x.at[slot], at + 1, place.by_x)
+        add_to(self.view(slot, 2, 1), self.far_x.at[slot])
+        copies.send(self.view(slot, 2, None), self.near_y.at[slot], at + 3, at + 3, place.by_y)
+
+    def end(self, slot):
+        place, copies, at = self.place, self.copies, self.base + 4 * slot
+        copies.receive(self.near_x.at[slot], at + 2, place.by_x)
+        copies.receive(self.near_y.at[slot], at + 3, place.by_y)
+        add_to(self.view(slot, 0, None), self.near_x.at[slot], self.near_y.at[slot])
+        if slot:
+            at = self.base + 4 * place.n_head + slot
+            into = self.high.at[slot - 1]
+            copies.send(self.view(slot, 0, None), into, at, at, place.above(slot))
+
+    def total(self):
+        place = self.place
+        high = [self.high.at[slot - 1] for slot in range(1, place.n_head)]
+        for slot, part in enumerate(high, 1):
+            self.copies.receive(part, self.base + 4 * place.n_head + slot, place.up)
+        add_to(self.view(0, 0, None), *high)
+
+
+PER_SCATTER = 20
+
+
+def add_to(ref, *others):
+    def add(*refs):
+        total = refs[0][...].astype(F32)
+        for other in refs[1:]:
+            total += other[...].astype(F32)
+        refs[0][...] = total.astype(BF)
+
+    if len(ref.shape) == 2:
+        add(ref, *others)
+    else:
+        for i in range(ref.shape[0]):
+            add(ref.at[i], *(other.at[i] for other in others))
+
+
+def dot(left, right):
+    return jnp.dot(left, right, preferred_element_type=F32)
+
+
+def iota(shape, axis):
+    return lax.broadcasted_iota(jnp.int32, shape, axis).astype(F32)
+
+
+def decay_of(head):
+    exponent = jnp.full((1, 1), -8.0 / HEADS, F32) * (head + 1).astype(F32)
+    return jnp.exp2(exponent)
+
+
+def middle_kernel(
+    n_head,
+    wf,
+    nm,
+    og,
+    hidden,
+    wo,
+    pre,
+    query,
+    keys,
+    values,
+    attn,
+    cosines,
+    sines,
+    fresh,
+    carry,
+    scale,
+    feed_out,
+    block_out,
+    hidden_grad_out,
+    branch_out,
+    pre_out,
+    rates_out,
+    wf_ref,
+    t_ref,
+    g_ref,
+    far_x,
+    far_y,
+    near_x,
+    near_y,
+    high,
+    nm_ref,
+    og_ref,
+    hidden_ref,
+    mid_ref,
+    send_ref,
+    got_ref,
+    block_ref,
+    wo_ref,
+    gate_ref,
+    attn_ref,
+    ga_ref,
+    qk_pre_ref,
+    cos_ref,
+    sin_ref,
+    fresh_ref,
+    carry_ref,
+    late_ref,
+    pending_ref,
+    message_ref,
+    scale_ref,
+    sum_ref,
+    other_sum_ref,
+    rates_ref,
+    sends,
+    receives,
+    locals_,
+):
+    rows, width = hidden.shape
+    quarter = width // 4
+    units = wf.shape[1] // n_head
+    spans = rows // SPAN
+    tiles = 2 * spans
+    last = n_head - 1
+    place = Place(n_head)
+    z, core = place.z, place.core
+    copies = Copies(sends, receives, locals_)
+    own, other = pl.ds(0, rows), pl.ds(rows, rows)
+
+    order = (2, 1, 3, 0)
+    load_nm = copies.move(nm, nm_ref)
+    load_og = copies.move(og, og_ref)
+    load_wf = {}
+    for slot in order:
+        at = pl.ds(slot * units, units)
+        load_wf[slot] = copies.move(wf.at[:, at, :], wf_ref.at[:, at, :])
+    early_loads = [
+        copies.move(hidden, hidden_ref),
+        copies.move(wo, wo_ref),
+        copies.move(scale, scale_ref),
+        copies.move(attn, attn_ref),
+        copies.move(pre.at[:, :, pl.ds(3 * HEAD_DIM, HEAD_DIM)], gate_ref),
+        copies.move(carry, carry_ref),
+    ]
+    for seq in range(2):
+        for slot in range(n_head):
+            early_loads.append(copies.move(fresh.at[slot, seq * spans], fresh_ref.at[slot, seq]))
+    place.greet()
+
+    def tile(i):
+        return pl.ds(pl.multiple_of(i * SPAN, SPAN), SPAN)
+
+    def dot_last(left, right):
+        return lax.dot_general(left, right, (((1,), (1,)), ((), ())), preferred_element_type=F32)
+
+    def dot_first(left, right):
+        return lax.dot_general(left, right, (((0,), (0,)), ((), ())), preferred_element_type=F32)
+
+    def g_view(slot, q, half):
+        size = units if half is None else units // 2
+        start = slot * units + (half or 0) * size
+        return g_ref.at[:, pl.ds(start, size), pl.ds(q * quarter, quarter)]
+
+    feed = Scatter(place, copies, g_view, far_x, far_y, near_x, near_y, high, 0)
+    base = PER_SCATTER
+
+    def feed_slot(slot):
+        at = pl.ds(slot * units, units)
+
+        @pl.loop(0, tiles)
+        def _(i):
+            rows_at = tile(i)
+            left = dot_last(wf_ref[0, at, :], nm_ref[rows_at, :])
+            right = dot_last(wf_ref[1, at, :], nm_ref[rows_at, :])
+            grad = dot_last(wf_ref[2, at, :], og_ref[rows_at, :])
+            t_ref[0, at, rows_at] = (grad * right).astype(BF)
+            t_ref[1, at, rows_at] = (grad * left).astype(BF)
+            t_ref[2, at, rows_at] = (left * right).astype(BF)
+
+        @pl.loop(0, width // SPAN)
+        def _(i):
+            columns = tile(i)
+            for m, right in enumerate((nm_ref, nm_ref, og_ref)):
+                g_ref[m, at, columns] = dot(t_ref[m, at, :], right[:, columns]).astype(BF)
+
+    load_nm.wait()
+    load_og.wait()
+    for i, slot in enumerate(order):
+        load_wf[slot].wait()
+        feed_slot(slot)
+        feed.begin(slot)
+        if i == 2:
+            feed.middle(order[0])
+    feed.middle(order[1])
+    for load in early_loads:
+        load.wait()
+
+    @pl.loop(0, spans)
+    def _(i):
+        at = tile(spans + i)
+        total = dot_first(t_ref[0, :, at], wf_ref[0]) + dot_first(t_ref[1, :, at], wf_ref[1])
+        send_ref[tile(i), :] = total.astype(BF)
+
+    copies.send(send_ref, got_ref, base, base, place.across)
+
+    @pl.loop(0, spans)
+    def _(i):
+        at = tile(i)
+        total = dot_first(t_ref[0, :, at], wf_ref[0]) + dot_first(t_ref[1, :, at], wf_ref[1])
+        mid_ref[at, :] = total
+
+    feed.end(order[0])
+    copies.receive(got_ref, base, place.across)
+
+    @pl.loop(0, rows // 128)
+    def _(i):
+        at = pl.ds(pl.multiple_of(i * 128, 128), 128)
+        grad = mid_ref[at, :] + got_ref[at, :].astype(F32)
+        values = hidden_ref[at, :]
+        norm = lax.rsqrt(jnp.mean(values * values, axis=-1, keepdims=True) + EPSILON)
+        normed = values * norm
+        mean = jnp.mean(grad * normed, axis=-1, keepdims=True)
+        grad = og_ref[at, :].astype(F32) + norm * (grad - normed * mean)
+        mid_ref[at, :] = grad
+        nm_ref[at, :] = grad.astype(BF)
+
+    copies.send(nm_ref.at[own], nm_ref.at[other], base + 1, base + 1, place.across)
+    copies.move(mid_ref, hidden_grad_out, later=True)
+    copies.sent(base)
+
+    @pl.loop(0, spans)
+    def _(i):
+        send_ref[tile(i), :] = dot_first(t_ref[2, :, tile(spans + i)], wf_ref[2]).astype(BF)
+
+    copies.receive(nm_ref.at[other], base + 1, place.across)
+    copies.move(nm_ref, branch_out, later=True)
+    copies.send(send_ref, got_ref, base + 2, base + 2, place.across)
+
+    @pl.loop(0, spans)
+    def _(i):
+        at = tile(i)
+        hidden_ref[at, :] += dot_first(t_ref[2, :, at], wf_ref[2])
+
+    loads = []
+    for slot in range(n_head):
+        lanes = pl.ds(slot * 2 * HEAD_DIM, 2 * HEAD_DIM)
+        loads.append(copies.move(query.at[slot], t_ref.at[0, pl.ds(0, 2 * rows), lanes]))
+        loads.append(copies.move(keys.at[slot], t_ref.at[1, pl.ds(0, 2 * rows), lanes]))
+        lanes = pl.ds(slot * HEAD_DIM, HEAD_DIM)
+        loads.append(copies.move(values.at[slot], wf_ref.at[1, pl.ds(0, 2 * rows), lanes]))
+
+    def late_loads(slot):
+        turn = slot % 2
+        return [
+            copies.move(pre.at[slot, :, pl.ds(0, 2 * HEAD_DIM)], qk_pre_ref.at[turn]),
+            copies.move(cosines.at[slot], cos_ref.at[turn]),
+            copies.move(sines.at[slot], sin_ref.at[turn]),
+        ]
+
+    slot_loads = {slot: late_loads(slot) for slot in range(2)}
+
+    def q_at(slot, at):
+        return t_ref[0, at, pl.ds(slot * 2 * HEAD_DIM, 2 * HEAD_DIM)]
+
+    def k_at(slot, at):
+        return t_ref[1, at, pl.ds(slot * 2 * HEAD_DIM, 2 * HEAD_DIM)]
+
+    def v_at(slot, at):
+        return wf_ref[1, at, pl.ds(slot * HEAD_DIM, HEAD_DIM)]
+
+    def pre_at(slot, at, part):
+        start = (slot % 2) * 4 * HEAD_DIM + part * HEAD_DIM
+        holder = t_ref.at[2] if slot < 2 else wf_ref.at[0]
+        return holder.at[at, pl.ds(start, HEAD_DIM)]
+
+    @pl.loop(0, tiles)
+    def _(i):
+        at = tile(i)
+        grad = dot_last(nm_ref[at, :], wo_ref[...])
+        norm = scale_ref[at, :]
+        total = jnp.zeros((SPAN, 1), F32)
+        for slot in range(n_head):
+            part = grad[:, slot * HEAD_DIM : (slot + 1) * HEAD_DIM]
+            normed = attn_ref[slot, at, :] * norm
+            pre_at(slot, at, 3)[...] = (part * normed).astype(BF)
+            part = part * gate_ref[slot, at, :]
+            gate_ref[slot, at, :] = part
+            total += jnp.sum(part * normed, axis=-1, keepdims=True)
+        sum_ref[at, :] = jnp.broadcast_to(total, (SPAN, HEAD_DIM))
+
+    base += 3
+    copies.send(sum_ref.at[own], other_sum_ref.at[other], base, base, place.across)
+    copies.send(sum_ref.at[other], other_sum_ref.at[own], base + 1, base + 1, place.across)
+    feed.middle(order[2])
+    copies.receive(got_ref, base - 1, place.across)
+
+    @pl.loop(0, rows // 128)
+    def _(i):
+        at = pl.ds(pl.multiple_of(i * 128, 128), 128)
+        block_ref[at, :] = (hidden_ref[at, :] + got_ref[at, :].astype(F32)).astype(BF)
+
+    for q in range(4):
+        far = pl.ds(pl.multiple_of(place.at[q] * quarter, quarter), quarter)
+        src = block_ref.at[:, pl.ds(q * quarter, quarter)]
+        copies.move(src, block_out.at[:, far], later=True)
+    copies.receive(other_sum_ref.at[other], base, place.across)
+    copies.receive(other_sum_ref.at[own], base + 1, place.across)
+    base += 2
+    for load in loads:
+        load.wait()
+
+    def slot_decay(slot):
+        return decay_of(2 * lax.rem(z + slot, n_head) + core)
+
+    for slot in range(n_head):
+        decay = slot_decay(slot)
+        early = jnp.exp(-decay * (iota((SPAN, HEAD_DIM), 0) + 1.0))
+
+        @pl.loop(0, tiles)
+        def _(i):
+            at = tile(i)
+            norm = scale_ref[at, :]
+            mean = (sum_ref[at, :] + other_sum_ref[at, :]) / width
+            grad = norm * (gate_ref[slot, at, :] - attn_ref[slot, at, :] * norm * mean)
+            grad = grad.astype(BF)
+            ga_ref[slot, at, :] = grad
+            both = dot_first(
+                q_at(slot, at), jnp.concatenate(split(grad.astype(F32) * early), axis=1)
+            )
+            late_ref[slot, i] = both[:, :HEAD_DIM] + both[:, HEAD_DIM:]
+
+    n_chain = 2 * n_head
+    chain_base = base
+
+    def chain_at(index):
+        group, seq = lax.div(index, 2), lax.rem(index, 2)
+        return lax.rem(group - z + n_head, n_head), seq, decay_of(2 * group + core)
+
+    def chain_copy(index, slot, seq):
+        return pltpu.make_async_remote_copy(
+            src_ref=message_ref.at[slot, seq],
+            dst_ref=pending_ref.at[lax.rem(slot + 1, n_head), seq],
+            send_sem=sends.at[chain_base + index],
+            recv_sem=receives.at[chain_base + index],
+            device_id=place.down,
+            device_id_type=MESH,
+        )
+
+    @pl.loop(0, n_chain)
+    def _(index):
+        slot, seq, decay = chain_at(index)
+
+        @pl.when(z < last)
+        def _():
+            copies.receive(pending_ref.at[slot, seq], chain_base + index, place.up)
+
+        @pl.when(z == last)
+        def _():
+            pending_ref[slot, seq] = jnp.zeros(pending_ref.shape[2:], BF)
+
+        @pl.when(z > 0)
+        def _():
+            total = jnp.exp(-decay * rows) * pending_ref[slot, seq].astype(F32)
+            for n in range(spans):
+                total += jnp.exp(-decay * (n * SPAN)) * late_ref[slot, seq * spans + n]
+            message_ref[slot, seq] = total.astype(BF)
+            chain_copy(index, slot, seq).start()
+
+    feed.end(order[1])
+    feed.middle(order[3])
+
+    offsets = iota((SPAN, SPAN), 0) - iota((SPAN, SPAN), 1)
+
+    def back_slot(slot):
+        turn = slot % 2
+        decay = slot_decay(slot)
+        mask = jnp.where(offsets >= 0.0, jnp.exp(-decay * jnp.maximum(offsets, 0.0)), 0.0)
+        places = iota((SPAN, 1), 0)
+        early = jnp.exp(-decay * (places + 1.0))
+        late = jnp.exp(-decay * (SPAN - 1.0 - places))
+        span_decay = jnp.exp(-decay * SPAN)
+        rates_ref[slot] = jnp.zeros((8, HEAD_DIM), F32)
+
+        @pl.loop(0, 2)
+        def _(seq):
+            for n in range(spans):
+                i = seq * spans + n
+                at, here = tile(i), pl.ds(n * SPAN, SPAN)
+                state = carry_ref[slot, seq].astype(F32)
+                if n == 1:
+                    state = span_decay * state + fresh_ref[slot, seq]
+                later = pending_ref[slot, seq].astype(F32)
+                if n == 0:
+                    later = span_decay * later + late_ref[slot, seq * spans + 1]
+                q, k, v, grad = q_at(slot, at), k_at(slot, at), v_at(slot, at), ga_ref[slot, at, :]
+                weights = (dot_last(q, k) * mask).astype(BF)
+                scores = (dot_last(grad, v) * mask).astype(BF)
+                state_high, state_low = split(state)
+                grad_query = dot(scores, k)
+                grad_query += early * (dot_last(grad, state_high) + dot_last(grad, state_low))
+                later_high, later_low = split(later)
+                grad_keys = dot_first(scores, q)
+                grad_keys += late * (dot_last(v, later_high) + dot_last(v, later_low))
+                both = dot(k, jnp.concatenate([later_high, later_low], axis=1))
+                grad_values = dot_first(weights, grad)
+                grad_values += late * (both[:, :HEAD_DIM] + both[:, HEAD_DIM:])
+                pre_at(slot, at, 2)[...] = grad_values.astype(BF)
+                cosine, sine = cos_ref[turn, here, :], sin_ref[turn, here, :]
+                angles = jnp.zeros((SPAN, HEAD_DIM), F32)
+                for part, turned in enumerate((grad_query, grad_keys)):
+                    value = qk_pre_ref[turn, at, pl.ds(part * HEAD_DIM, HEAD_DIM)]
+                    by_cos, by_sin = turned[:, :HEAD_DIM], turned[:, HEAD_DIM:]
+                    gate = 1.0 / (1.0 + jnp.exp(-value))
+                    act = by_cos * cosine + by_sin * sine
+                    angles += value * gate * (by_sin * cosine - by_cos * sine)
+                    act = act * gate * (1.0 + value * (1.0 - gate))
+                    pre_at(slot, at, part)[...] = act.astype(BF)
+                steps = (z * rows + n * SPAN).astype(F32) + places
+                rates_ref[slot, pl.ds(0, 1), :] += jnp.sum(steps * angles, axis=0, keepdims=True)
+
+    for slot in range(n_head):
+        for load in slot_loads[slot]:
+            load.wait()
+        back_slot(slot)
+        if slot + 2 < n_head:
+            slot_loads[slot + 2] = late_loads(slot + 2)
+        lanes = pl.ds((slot % 2) * 4 * HEAD_DIM, 4 * HEAD_DIM)
+        holder = t_ref.at[2] if slot < 2 else wf_ref.at[0]
+        copies.move(holder.at[pl.ds(0, 2 * rows), lanes], pre_out.at[slot], later=True)
+        if slot == 1:
+            feed.end(order[2])
+    feed.end(order[3])
+    feed.total()
+    copies.move(g_view(0, 0, None), feed_out, later=True)
+    copies.move(rates_ref, rates_out, later=True)
+
+    @pl.when(z > 0)
+    def _():
+        @pl.loop(0, n_chain)
+        def _(index):
+            slot, seq, _ = chain_at(index)
+            chain_copy(index, slot, seq).wait_send()
+
+    copies.finish()
+
+
+def middle(n_head, wf, nm, og, hidden, wo, pre, query, keys, values, attn, cos, sin, fresh, carry, scale):
+    rows, width = hidden.shape
+    units = wf.shape[1] // n_head
+    quarter = width // 4
+    tall = 2 * rows
+    halves = (n_head, 3, units // 2, quarter)
+    wholes = (n_head, 3, units, quarter)
+    buffers = [
+        (wf.shape, BF),
+        (wf.shape, BF),
+        (wf.shape, BF),
+        (halves, BF),
+        (halves, BF),
+        (wholes, BF),
+        (wholes, BF),
+        ((n_head - 1,) + wholes[1:], BF),
+        ((tall, width), BF),
+        ((tall, width), BF),
+        ((rows, width), F32),
+        ((rows, width), F32),
+        ((rows, width), BF),
+        ((rows, width), BF),
+        ((rows, width), BF),
+        (wo.shape, BF),
+        ((n_head, tall, HEAD_DIM), F32),
+        ((n_head, tall, HEAD_DIM), F32),
+        ((n_head, tall, HEAD_DIM), BF),
+        ((2, tall, 2 * HEAD_DIM), F32),
+        ((2, rows, HEAD_DIM), F32),
+        ((2, rows, HEAD_DIM), F32),
+        ((n_head, 2, 2 * HEAD_DIM, HEAD_DIM), F32),
+        ((n_head, 2, 2 * HEAD_DIM, HEAD_DIM), BF),
+        ((n_head, tall // SPAN, 2 * HEAD_DIM, HEAD_DIM), F32),
+        ((n_head, 2, 2 * HEAD_DIM, HEAD_DIM), BF),
+        ((n_head, 2, 2 * HEAD_DIM, HEAD_DIM), BF),
+        ((tall, HEAD_DIM), F32),
+        ((tall, HEAD_DIM), F32),
+        ((tall, HEAD_DIM), F32),
+        ((n_head, 8, HEAD_DIM), F32),
+    ]
+    outs = [
+        (wholes[1:], BF),
+        ((rows, width), BF),
+        ((rows, width), F32),
+        ((tall, width), BF),
+        ((n_head, tall, 4 * HEAD_DIM), BF),
+        ((n_head, 8, HEAD_DIM), F32),
+    ]
+    n_sems = PER_SCATTER + 3 + 2 + 2 * n_head
+    return pl.pallas_call(
+        functools.partial(middle_kernel, n_head),
+        out_shape=[jax.ShapeDtypeStruct(*out) for out in outs],
+        in_specs=[ANY] * 15,
+        out_specs=[ANY] * len(outs),
+        scratch_shapes=[pltpu.VMEM(*b) for b in buffers]
+        + [
+            pltpu.SemaphoreType.DMA((n_sems,)),
+            pltpu.SemaphoreType.DMA((n_sems,)),
+            pltpu.SemaphoreType.DMA((64,)),
+        ],
+        compiler_params=pltpu.CompilerParams(
+            collective_id=1, has_side_effects=True, vmem_limit_bytes=63 << 20
+        ),
+        name="middle",
+    )(wf, nm, og, hidden, wo, pre, query, keys, values, attn, cos, sin, fresh, carry, scale)
 
 
 def make(n_dp, n_head):
@@ -693,9 +1242,11 @@
             gated,
             hidden,
             gathered_mid,
+            grad_rows,
         ) = forward(
             n_head,
             tokens,
+            out_grad,
             attn_query,
             attn_key,
             attn_value,
@@ -704,144 +1255,33 @@
             ffn,
             rates_in,
         )
-        left_w, right_w, down_w = ffn_all[0], ffn_all[1], ffn_all[2]
-        out_w = out_w.T
-
+        feed_piece, block_out, grad_hidden, branch_rows, grad_pre, rates_grad = middle(
+            n_head,
+            ffn_all,
+            gathered_mid,
+            grad_rows,
+            hidden,
+            out_w,
+            pre,
+            query,
+            keys,
+            values,
+            attn,
+            cosines,
+            sines,
+            fresh,
+            carry,
+            scale_attn,
+        )
+        rates_grad = rates_grad[:, 0]
+        left_grad, right_grad, down_grad = jnp.concatenate(share(feed_piece, 1), axis=2)
         inputs = relative(tokens, 1).astype(F32)
         normed_one, scale_one = norm_parts(inputs)
-        out_grad = relative(out_grad, 1)
-        grad_rows = jnp.concatenate([out_grad, swap(out_grad, 1)], axis=0)
-        positions = (place * rows + jnp.arange(rows)).astype(F32)
-        cosines, sines = cosines[:, None], sines[:, None]
-        pre = pre.reshape(n_head, 2, rows, 4 * HEAD_DIM)
-        query_pre, key_pre, value_pre, gate_pre = (
-            pre[..., i * HEAD_DIM : (i + 1) * HEAD_DIM] for i in range(4)
-        )
-
-        def blocks(array):
-            return array.reshape(n_head, 2, spans, SPAN, array.shape[-1])
-
-        query, keys, values = blocks(query), blocks(keys), blocks(values)
-        head_ids = 2 * ((place + jnp.arange(n_head)) % n_head) + core
-        decay_rates = jnp.exp2(-8.0 * (head_ids.astype(F32) + 1.0) / HEADS)
-        places = jnp.arange(SPAN, dtype=F32)
-        offsets = places[:, None] - places[None, :]
-        decay_mask = jnp.where(
-            offsets[None] >= 0.0,
-            jnp.exp(-decay_rates[:, None, None] * jnp.maximum(offsets[None], 0.0)),
-            0.0,
-        )[:, None, None]
-        query_decay = jnp.exp(-decay_rates[:, None] * (places[None] + 1.0))[:, None, None, :, None]
-        key_decay = jnp.exp(-decay_rates[:, None] * (SPAN - 1.0 - places[None]))[
-            :, None, None, :, None
-        ]
-        span_decay = jnp.exp(-decay_rates * SPAN)[:, None, None, None]
-        rows_decay = jnp.exp(-decay_rates * rows)[:, None, None, None]
-
-        def ein(spec, left, right):
-            return jnp.einsum(spec, left, right, preferred_element_type=F32)
-
-        def exact(spec, left, right):
-            left, right = left.astype(F32), right.astype(F32)
-            return jnp.einsum(spec, left, right, precision=lax.Precision.HIGHEST)
-
-        def roll(array, step):
-            return jnp.roll(array, step, axis=0)
-
-        scores = ein("hsnid,hsnjd->hsnij", query, keys)
-        weights = (scores * decay_mask).astype(BF)
-        fresh = fresh.reshape(n_head, 2, spans, 2 * HEAD_DIM, HEAD_DIM)
-        state = carry.astype(F32)
-        states = []
-        for n in range(spans):
-            states.append(state)
-            state = span_decay * state + fresh[:, :, n]
-        states = jnp.stack(states, axis=2)
-        attn = attn.reshape(n_head, 2, rows, HEAD_DIM)
-        scale_attn = scale_attn[:, :1].reshape(1, 2, rows, 1)
-        attn_normed = attn * scale_attn
-
-        def core_sum(array):
-            return array + swap(array[::-1], 1)
+        out_grads = first_dot(branch_rows, gated)
 
         def core_scatter(array):
             return array[:rows] + swap(array[rows:].astype(BF), 1).astype(F32)
 
-        normed_two, scale_two = norm_parts(hidden)
-        left = second_dot(gathered_mid, left_w)
-        right = second_dot(gathered_mid, right_w)
-        product = (left * right).astype(BF)
-        down_grad = first_dot(product, grad_rows).astype(BF)
-        grad_product = second_dot(grad_rows, down_w)
-        grad_left = (grad_product * right).astype(BF)
-        grad_right = (grad_product * left).astype(BF)
-        left_grad = first_dot(grad_left, gathered_mid).astype(BF)
-        right_grad = first_dot(grad_right, gathered_mid).astype(BF)
-        grad_mid = core_scatter(plain_dot(grad_left, left_w) + plain_dot(grad_right, right_w))
-        grad_hidden = out_grad.astype(F32) + norm_back(normed_two, scale_two, grad_mid)
-
-        def ffn_total(grad):
-            grad = grad.reshape(n_head, units, width)
-            piece = collect([grad[:, :, q * quarter : (q + 1) * quarter] for q in range(4)], 1)
-            return jnp.concatenate(share(piece, 0), axis=1)
-
-        down_grad, left_grad, right_grad = (ffn_total(g) for g in (down_grad, left_grad, right_grad))
-        block_out = (hidden + core_scatter(plain_dot(product, down_w))).astype(BF)
-
-        branch_low = grad_hidden.astype(BF)
-        branch_rows = jnp.concatenate([branch_low, swap(branch_low, 1)], axis=0)
-        out_grads = first_dot(branch_rows, gated)
-        grad_gated = plain_dot(branch_rows, out_w)
-        grad_gated = grad_gated.reshape(2, rows, n_head, HEAD_DIM).transpose(2, 0, 1, 3)
-        grad_normed = grad_gated * gate_pre
-        grad_gate_pre = (grad_gated * attn_normed).astype(BF)
-        products = core_sum(jnp.sum(grad_normed * attn_normed, axis=(0, 3)))[None, :, :, None]
-        grad_attn = (scale_attn * (grad_normed - attn_normed * (products / width))).astype(BF)
-        grad_blocks = blocks(grad_attn)
-        grad_scores = (ein("hsnie,hsnje->hsnij", grad_blocks, values) * decay_mask).astype(BF)
-        grad_values = ein("hsnij,hsnie->hsnje", weights, grad_blocks)
-        grad_query = ein("hsnij,hsnjd->hsnid", grad_scores, keys)
-        grad_keys = ein("hsnij,hsnid->hsnjd", grad_scores, query)
-        grad_query = grad_query + query_decay * exact("hsnie,hsnde->hsnid", grad_blocks, states)
-        grad_early = grad_blocks.astype(F32) * query_decay
-        grad_states = exact("hsnid,hsnie->hsnde", query, grad_early)
-        local_pending = jnp.zeros(grad_states.shape[:2] + grad_states.shape[3:], F32)
-        for n in reversed(range(spans)):
-            local_pending = span_decay * local_pending + grad_states[:, :, n]
-        pending = jnp.zeros_like(local_pending)
-        for hop in range(n_head - 1):
-            message = roll((local_pending + rows_decay * pending).astype(BF), 1)
-            pending = lax.ppermute(message, "head", [(i + 1, i) for i in range(n_head - 1)]).astype(
-                F32
-            )
-        later = []
-        for n in reversed(range(spans)):
-            later.insert(0, pending)
-            pending = span_decay * pending + grad_states[:, :, n]
-        later = jnp.stack(later, axis=2)
-        grad_keys = grad_keys + key_decay * exact("hsnje,hsnde->hsnjd", values, later)
-        grad_values = grad_values + key_decay * exact("hsnjd,hsnde->hsnje", keys, later)
-
-        def unrotate(grad_rotated, pre_values):
-            shaped = grad_rotated.reshape(n_head, 2, rows, 2 * HEAD_DIM)
-            grad_cos = shaped[..., :HEAD_DIM]
-            grad_sin = shaped[..., HEAD_DIM:]
-            grad_act = grad_cos * cosines + grad_sin * sines
-            sigmoid_pre = jax.nn.sigmoid(pre_values)
-            activated = pre_values * sigmoid_pre
-            grad_angle = activated * (grad_sin * cosines - grad_cos * sines)
-            grad_pre = grad_act * sigmoid_pre * (1.0 + pre_values * (1.0 - sigmoid_pre))
-            return (grad_pre.astype(BF), grad_angle)
-
-        grad_query_pre, angle_query = unrotate(grad_query, query_pre)
-        grad_key_pre, angle_key = unrotate(grad_keys, key_pre)
-        grad_value_pre = grad_values.reshape(n_head, 2, rows, HEAD_DIM).astype(BF)
-        rates_grad = jnp.sum(
-            positions[None, None, :, None] * (angle_query + angle_key), axis=(1, 2)
-        )
-        grad_pre = jnp.concatenate(
-            [grad_query_pre, grad_key_pre, grad_value_pre, grad_gate_pre], axis=-1
-        ).reshape(n_head, 2 * rows, 4 * HEAD_DIM)
         attn_grads = []
         grad_in = None
         for r in range(n_head):
@@ -879,7 +1319,7 @@
         ffn_grads = jnp.stack([relative(g, 1) for g in (left_grad, right_grad, down_grad)])
         ffn_grads = jnp.concatenate(both(ffn_grads, 1), axis=1).astype(F32)
         return (
-            relative(block_out, 1),
+            block_out,
             relative(input_grad, 1),
             query_grad,
             key_grad,

time: 560 us -> 425 us (0.76)
  the two profiles are of different devices: /device:TPU:1 before, /device:TPU:9 now
where the time goes in v3:
time: 425 us; the launch traced here: 420 us
  Pallas kernels  213 us (50%)
  waiting for transfers between devices  61.6 us (14%)
  local copies, waits for them, and re-layouts  39.5 us (9%)
  starting transfers between devices  38.7 us (9%)
  matrix products  29.3 us (7%)
  other arithmetic  24.1 us (6%)
  blocking collectives  12.6 us (3%)
    pallas_call x1, Pallas kernels, middle(): pl.pallas_call(functools.partial(middle_kernel, n_head), out_shape=[jax.S...  108 us
    pallas_call x1, Pallas kernels, forward(): pl.pallas_call(functools.partial(forward_kernel, n_head), out_shape=[jax....  105 us
    ppermute x16, waiting for transfers between devices, swap(): return lax.ppermute(array, 'dp', [(i, i ^ bit) for i in range(n_dp)])  33.2 us
    ppermute x6, waiting for transfers between devices, to_above(): lax.ppermute(array, 'head', [(i, (i + step) % n_head) for i in range(n_he...  28.5 us
    ppermute x16, starting transfers between devices, swap(): return lax.ppermute(array, 'dp', [(i, i ^ bit) for i in range(n_dp)])  21.9 us
    dot_general x4, matrix products, second_dot(): lax.dot_general(left, right, (((1,), (1,)), ((), ())), preferred_element_...  18.8 us
    ppermute x6, starting transfers between devices, to_above(): lax.ppermute(array, 'head', [(i, (i + step) % n_head) for i in range(n_he...  16.8 us
    unnamed x39, local copies, waits for them, and re-layouts  14 us
  transfers between devices with their start and end apart: 22, of which 9 were waited for; matrix products, arithmetic and copies ran while one was open for 19% of the time, Pallas kernels for 0%

profile of v3, /device:TPU:9, one launch (start us, length us, event | category | flops | bytes accessed | tf_op | source)
XLA Modules:
  0.0 419.7 jit_solution(5204200807386115531)
XLA Ops:
  0.6 1.3 pad.4.rates
  1.9 3.8 pad_maximum_fusion.ffn
  5.7 104.5 %forward.1 = (bf16[4,1024,512]{2,1,0:T(8,128)(2,1)}, bf16[512,1024]{1,0:T(8,128)(2,1)}, bf16[3,1408,1024]{2,1,0:T(8,128)(2,1)}, bf16[1024,1024]{1,0:T(8,128)(2,1...) custom-call(bf16[512,1024]{1,0:T(8,128)(2,1)} %tokens.1, ...), custom_call_target="tpu_custom_call" | custom-call | tf_op jit(solution)/shard_map/forward/pallas_call | solution.py:610
  110.3 108.1 %middle.1 = (bf16[3,352,256]{2,1,0:T(8,128)(2,1)}, bf16[512,1024]{1,0:T(8,128)(2,1)}, f32[512,1024]{1,0:T(8,128)}, bf16[1024,1024]{1,0:T(8,128)(2,1)}, bf16[4,10...) custom-call(bf16[3,1408,1024]{2,1,0:T(8,128)(2,1)} %get-tuple-element.35.wf, bf16[1024,1024]{1,0:T(8,128)(2,1)} %get-tuple-element.36.nm, ...), custom_call_target="tpu_custom_call" | custom-call | tf_op jit(solution)/shard_map/middle/pallas_call | solution.py:1130
  218.7 1.1 collective-permute-start.18
  219.8 0.7 slice_bitcast_fusion.13
  220.5 13.0 %collective-permute-start.14 = (f32[128]{0:T(128)S(1)}, f32[128]{0:T(128)S(1)}, u32[]{:S(2)}, u32[]{:S(2)}) collective-permute-start(f32[128]{0:T(128)S(1)} %get-tuple-element.130), channel_id=1, source_target_pairs={{0,2},{1,3},{2,0},{3,1},{4,6},{5,7},{6,4},{7,5},{8,10},{9,11},{10,... | collective-permute-start | bytes 1544 | tf_op jit(solution)/shard_map/ppermute | solution.py:1156
  233.5 1.5 collective-permute-start.15
  235.0 3.3 convolution_convert_fusion
  238.8 1.3 convolution_convert_fusion.1
  240.1 2.3 convolution_convert_fusion.2
  242.4 2.3 convolution_convert_fusion.4
  244.7 3.4 fusion.16
  248.1 3.3 fusion.20
  251.4 3.4 fusion.12
  254.8 1.3 convolution_convert_fusion.3
  256.4 2.0 stack.45
  258.5 2.9 pad_maximum_fusion.3
  261.3 3.8 stack.43
  265.1 2.6 copy_dynamic-update-slice_fusion.3
  267.7 1.8 stack.44
  269.5 1.8 stack.46
  271.4 2.6 copy_dynamic-update-slice_fusion.2
  274.0 1.2 copy_dynamic-update-slice_fusion.1
  275.2 1.3 copy_dynamic-update-slice_fusion
  276.5 2.4 slice_bitcast_fusion.5
  278.9 1.3 fusion.45
  280.2 8.7 %add_add_fusion = f32[1024,1024]{1,0:T(8,128)} fusion(f32[1024,1024]{1,0:T(8,128)} %fusion.12, f32[1024,1024]{1,0:T(8,128)} %fusion.20, f32[1024,1024]{1,0:T(8,128)} %fusion.16, bf16[4,1024,512]{2,1,0:T(8,128)(2,1)} %get-tuple-element.53, bf16[4,1024,512]{2,1,0:T(8,128)(2,1)} %get-tuple-element.52), kind=kOutput, calls=%fused_computation.2 | convolution fusion | flops 1076887552 | bytes 18874368 | tf_op jit(solution)/shard_map/dot_general | solution.py:36
  289.0 0.7 copy-done.4
  290.4 1.2 collective-permute-start.3
  291.6 0.7 fusion.40
  292.3 12.6 %psum.7 = f32[128]{0:T(128)S(1)} all-reduce(f32[128]{0:T(128)S(1)} %fusion.40), channel_id=1, replica_groups={{0,8,16,24},{4,12,20,28},{1,9,17,25},{5,13,21,29},{2,10,18,26},{6,14,22..., use_global_device_ids=true, to_apply=%region_2.3 | all-reduce | flops 128 | bytes 1024 | tf_op jit(solution)/shard_map/psum | solution.py:1303
  304.9 7.2 %collective-permute-start.16 = (f32[128]{0:T(128)S(1)}, f32[128]{0:T(128)S(1)}, u32[]{:S(2)}, u32[]{:S(2)}) collective-permute-start(f32[128]{0:T(128)S(1)} %psum.7), channel_id=1, source_target_pairs={{0,4},{4,0},{8,12},{12,8},{16,20},{20,16},{24,28},{28,24},{1,5},{5... | collective-permute-start | bytes 1544 | tf_op jit(solution)/shard_map/ppermute | solution.py:1150
  312.3 1.7 slice.326
  314.7 1.0 slice.246
  316.1 1.0 slice.247
  317.3 1.3 add_convert_fusion.1
  318.8 1.3 collective-permute-start.2
  320.1 1.3 add_convert_fusion
  321.5 1.2 collective-permute-start.4
  323.3 1.0 collective-permute-done.20
  324.4 3.3 maximum_maximum_fusion
  328.7 3.0 collective-permute-start.21
  331.6 20.8 %collective-permute-done.2 = bf16[4,256,640]{1,2,0:T(8,128)(2,1)S(1)} collective-permute-done((bf16[4,256,640]{1,2,0:T(8,128)(2,1)S(1)}, bf16[4,256,640]{1,2,0:T(8,128)(2,1)S(1)}, u32[]{:S(2)}, u32[]{:S(2)}) %collective-permute-start.2) | collective-permute-done | bytes 1310752 | tf_op jit(solution)/shard_map/ppermute | solution.py:1150
  352.5 2.0 fusion.1
  354.6 2.1 collective-permute-start.6
  357.5 4.6 %collective-permute-done.5 = bf16[256,640]{0,1:T(8,128)(2,1)S(1)} collective-permute-done((bf16[256,640]{0,1:T(8,128)(2,1)S(1)}, bf16[256,640]{0,1:T(8,128)(2,1)S(1)}, u32[]{:S(2)}, u32[]{:S(2)}) %collective-permute-start.5) | collective-permute-done | bytes 327712 | tf_op jit(solution)/shard_map/ppermute | solution.py:1156
  362.2 18.9 %collective-permute-done.6 = bf16[256,640]{0,1:T(8,128)(2,1)S(1)} collective-permute-done((bf16[256,640]{0,1:T(8,128)(2,1)S(1)}, bf16[256,640]{0,1:T(8,128)(2,1)S(1)}, u32[]{:S(2)}, u32[]{:S(2)}) %collective-permute-start.6) | collective-permute-done | bytes 327712 | tf_op jit(solution)/shard_map/ppermute | solution.py:1156
  381.0 4.9 %collective-permute-done.7 = bf16[256,640]{0,1:T(8,128)(2,1)S(1)} collective-permute-done((bf16[256,640]{0,1:T(8,128)(2,1)S(1)}, bf16[256,640]{0,1:T(8,128)(2,1)S(1)}, u32[]{:S(2)}, u32[]{:S(2)}) %collective-permute-start.7) | collective-permute-done | bytes 327712 | tf_op jit(solution)/shard_map/ppermute | solution.py:1156
  386.4 1.1 collective-permute-start.9
  388.5 6.6 %collective-permute-done.8 = bf16[256,640]{0,1:T(8,128)(2,1)S(1)} collective-permute-done((bf16[256,640]{0,1:T(8,128)(2,1)S(1)}, bf16[256,640]{0,1:T(8,128)(2,1)S(1)}, u32[]{:S(2)}, u32[]{:S(2)}) %collective-permute-start.8) | collective-permute-done | bytes 327712 | tf_op jit(solution)/shard_map/ppermute | solution.py:1150
  395.0 1.2 collective-permute-start.10
  396.6 2.7 collective-permute-done.10
  399.3 1.5 collective-permute-done.11
  401.2 2.5 collective-permute-start.12
  403.8 1.6 pad_maximum_fusion.2
  406.0 1.1 maximum_convert_fusion
  407.1 3.7 slice_bitcast_fusion
  411.8 1.3 copy.33
  413.3 1.3 copy.32
  414.7 1.3 copy.31
  416.1 1.3 copy.30
  417.4 1.1 convert_bitcast_fusion
  418.5 1.0 copy.50
  (91 shorter events, 10.4 us)
Async XLA Ops:
  218.3 96.4 %collective-permute-start.17 = (bf16[3,352,256]{2,1,0:T(8,128)(2,1)}, bf16[3,352,256]{2,1,0:T(8,128)(2,1)}, u32[]{:S(2)}, u32[]{:S(2)}) collective-permute-start(bf16[3,352,256]{2,1,0:T(8,128)(2,1)} %get-tuple-element.58), channel_id=1, source_target_pairs={{0,8},{4,12},{8,0},{12,4},{16,24},{20,28},{24,16},{28,20},{1,9},{5... | collective-permute-start | bytes 1622024 | tf_op jit(solution)/shard_map/ppermute | solution.py:1150
  218.7 97.4 %collective-permute-start.18 = (bf16[3,352,256]{2,1,0:T(8,128)(2,1)}, bf16[3,352,256]{2,1,0:T(8,128)(2,1)}, u32[]{:S(2)}, u32[]{:S(2)}) collective-permute-start(bf16[3,352,256]{2,1,0:T(8,128)(2,1)} %get-tuple-element.58), channel_id=1, source_target_pairs={{0,16},{4,20},{8,24},{12,28},{16,0},{20,4},{24,8},{28,12},{1,17},{... | collective-permute-start | bytes 1622024 | tf_op jit(solution)/shard_map/ppermute | solution.py:1150
  220.5 69.5 %collective-permute-start.13 = (f32[128]{0:T(128)S(1)}, f32[128]{0:T(128)S(1)}, u32[]{:S(2)}, u32[]{:S(2)}) collective-permute-start(f32[128]{0:T(128)S(1)} %get-tuple-element.128), channel_id=1, source_target_pairs={{0,1},{1,2},{2,3},{3,0},{4,5},{5,6},{6,7},{7,4},{8,9},{9,10},{10,1... | collective-permute-start | bytes 1544 | tf_op jit(solution)/shard_map/ppermute | solution.py:1156
  220.5 69.9 %collective-permute-start.14 = (f32[128]{0:T(128)S(1)}, f32[128]{0:T(128)S(1)}, u32[]{:S(2)}, u32[]{:S(2)}) collective-permute-start(f32[128]{0:T(128)S(1)} %get-tuple-element.130), channel_id=1, source_target_pairs={{0,2},{1,3},{2,0},{3,1},{4,6},{5,7},{6,4},{7,5},{8,10},{9,11},{10,... | collective-permute-start | bytes 1544 | tf_op jit(solution)/shard_map/ppermute | solution.py:1156
  233.5 58.1 %collective-permute-start.15 = (f32[128]{0:T(128)S(1)}, f32[128]{0:T(128)S(1)}, u32[]{:S(2)}, u32[]{:S(2)}) collective-permute-start(f32[128]{0:T(128)S(1)} %get-tuple-element.129), channel_id=1, source_target_pairs={{0,3},{1,0},{2,1},{3,2},{4,7},{5,4},{6,5},{7,6},{8,11},{9,8},{10,9... | collective-permute-start | bytes 1544 | tf_op jit(solution)/shard_map/ppermute | solution.py:1156
  235.0 3.3 copy-start.10
  235.0 3.8 copy-start.12
  242.4 2.3 copy-start.9
  251.4 3.4 copy-start.11
  251.4 3.4 copy-start.13
  269.5 4.5 %copy-start.1 = (bf16[1,4,256,640]{2,1,3,0:T(4,128)(2,1)S(1)}, bf16[1,4,256,640]{2,1,3,0:T(4,128)(2,1)}, u32[]{:S(2)}) copy-start(bf16[1,4,256,640]{2,1,3,0:T(4,128)(2,1)} %stack.45) | copy-start | bytes 3932164
  271.4 3.9 copy-start.2
  280.2 8.7 %copy-start.3 = (bf16[512,1024]{1,0:T(8,128)(2,1)S(1)}, bf16[512,1024]{1,0:T(8,128)(2,1)}, u32[]{:S(2)}) copy-start(bf16[512,1024]{1,0:T(8,128)(2,1)} %tokens.1) | copy-start | bytes 3145732
  289.0 0.7 copy-start.4
  290.0 27.3 %collective-permute-start.1 = (bf16[4,128,640]{1,2,0:T(8,128)(2,1)}, bf16[4,128,640]{1,2,0:T(8,128)(2,1)}, u32[]{:S(2)}, u32[]{:S(2)}) collective-permute-start(bf16[4,128,640]{1,2,0:T(8,128)(2,1)} %get-tuple-element.106), channel_id=1, source_target_pairs={{0,16},{4,20},{8,24},{12,28},{16,0},{20,4},{24,8},{28,12},{1,17},{... | collective-permute-start | bytes 1966088 | tf_op jit(solution)/shard_map/ppermute | solution.py:1150
  290.4 29.6 %collective-permute-start.3 = (bf16[4,128,640]{1,2,0:T(8,128)(2,1)}, bf16[4,128,640]{1,2,0:T(8,128)(2,1)}, u32[]{:S(2)}, u32[]{:S(2)}) collective-permute-start(bf16[4,128,640]{1,2,0:T(8,128)(2,1)} %get-tuple-element.107), channel_id=1, source_target_pairs={{0,8},{4,12},{8,0},{12,4},{16,24},{20,28},{24,16},{28,20},{1,9},{5... | collective-permute-start | bytes 1966088 | tf_op jit(solution)/shard_map/ppermute | solution.py:1150
  304.9 9.2 %collective-permute-start.16 = (f32[128]{0:T(128)S(1)}, f32[128]{0:T(128)S(1)}, u32[]{:S(2)}, u32[]{:S(2)}) collective-permute-start(f32[128]{0:T(128)S(1)} %psum.7), channel_id=1, source_target_pairs={{0,4},{4,0},{8,12},{12,8},{16,20},{20,16},{24,28},{28,24},{1,5},{5... | collective-permute-start | bytes 1544 | tf_op jit(solution)/shard_map/ppermute | solution.py:1150
  314.1 42.9 %collective-permute-start = (bf16[512,1024]{1,0:T(8,128)(2,1)S(1)}, bf16[512,1024]{1,0:T(8,128)(2,1)S(1)}, u32[]{:S(2)}, u32[]{:S(2)}) collective-permute-start(bf16[512,1024]{1,0:T(8,128)(2,1)S(1)} %slice.326), channel_id=1, source_target_pairs={{0,4},{4,0},{8,12},{12,8},{16,20},{20,16},{24,28},{28,24},{1,5},{5... | collective-permute-start | bytes 3145736 | tf_op jit(solution)/shard_map/ppermute | solution.py:1150
  315.7 7.6 %collective-permute-start.19 = (bf16[3,176,256]{2,1,0:T(8,128)(2,1)S(1)}, bf16[3,176,256]{2,1,0:T(8,128)(2,1)S(1)}, u32[]{:S(2)}, u32[]{:S(2)}) collective-permute-start(bf16[3,176,256]{2,1,0:T(8,128)(2,1)S(1)} %slice.246), channel_id=1, source_target_pairs={{0,16},{4,20},{8,24},{12,28},{16,0},{20,4},{24,8},{28,12},{1,17},{... | collective-permute-start | bytes 811016 | tf_op jit(solution)/shard_map/ppermute | solution.py:1150
  317.0 7.3 %collective-permute-start.20 = (bf16[3,176,256]{2,1,0:T(8,128)(2,1)S(1)}, bf16[3,176,256]{2,1,0:T(8,128)(2,1)S(1)}, u32[]{:S(2)}, u32[]{:S(2)}) collective-permute-start(bf16[3,176,256]{2,1,0:T(8,128)(2,1)S(1)} %slice.247), channel_id=1, source_target_pairs={{0,8},{4,12},{8,0},{12,4},{16,24},{20,28},{24,16},{28,20},{1,9},{5... | collective-permute-start | bytes 811016 | tf_op jit(solution)/shard_map/ppermute | solution.py:1150
  318.7 5.6 %copy-start.8 = (bf16[3,352,256]{2,1,0:T(8,128)(2,1)S(1)}, bf16[3,352,256]{2,1,0:T(8,128)(2,1)}, u32[]{:S(2)}) copy-start(bf16[3,352,256]{2,1,0:T(8,128)(2,1)} %get-tuple-element.58) | copy-start | bytes 1622020
  318.8 33.7 %collective-permute-start.2 = (bf16[4,256,640]{1,2,0:T(8,128)(2,1)S(1)}, bf16[4,256,640]{1,2,0:T(8,128)(2,1)S(1)}, u32[]{:S(2)}, u32[]{:S(2)}) collective-permute-start(bf16[4,256,640]{1,2,0:T(8,128)(2,1)S(1)} %pad_maximum_fusion.7), channel_id=1, source_target_pairs={{0,8},{4,12},{8,0},{12,4},{16,24},{20,28},{24,16},{28,20},{1,9},{5... | collective-permute-start | bytes 3932168 | tf_op jit(solution)/shard_map/ppermute | solution.py:1150
  321.5 31.0 %collective-permute-start.4 = (bf16[4,256,640]{1,2,0:T(8,128)(2,1)S(1)}, bf16[4,256,640]{1,2,0:T(8,128)(2,1)S(1)}, u32[]{:S(2)}, u32[]{:S(2)}) collective-permute-start(bf16[4,256,640]{1,2,0:T(8,128)(2,1)S(1)} %pad_maximum_fusion.8), channel_id=1, source_target_pairs={{0,16},{4,20},{8,24},{12,28},{16,0},{20,4},{24,8},{28,12},{1,17},{... | collective-permute-start | bytes 3932168 | tf_op jit(solution)/shard_map/ppermute | solution.py:1150
  328.7 76.7 %collective-permute-start.21 = (bf16[3,352,1024]{2,1,0:T(8,128)(2,1)S(1)}, bf16[3,352,1024]{2,1,0:T(8,128)(2,1)S(1)}, u32[]{:S(2)}, u32[]{:S(2)}) collective-permute-start(bf16[3,352,1024]{2,1,0:T(8,128)(2,1)S(1)} %pad_maximum_fusion.1), channel_id=1, source_target_pairs={{0,4},{4,0},{8,12},{12,8},{16,20},{20,16},{24,28},{28,24},{1,5},{5... | collective-permute-start | bytes 6488072 | tf_op jit(solution)/shard_map/ppermute | solution.py:1150
  352.5 4.5 %copy-start = (f32[1024,1024]{1,0:T(8,128)S(1)}, f32[1024,1024]{1,0:T(8,128)}, u32[]{:S(2)}) copy-start(f32[1024,1024]{1,0:T(8,128)} %add_add_fusion) | copy-start | bytes 12582916
  354.5 2.5 copy-start.5
  354.6 7.6 %collective-permute-start.5 = (bf16[256,640]{0,1:T(8,128)(2,1)S(1)}, bf16[256,640]{0,1:T(8,128)(2,1)S(1)}, u32[]{:S(2)}, u32[]{:S(2)}) collective-permute-start(bf16[256,640]{0,1:T(8,128)(2,1)S(1)} %get-tuple-element.103), channel_id=1, source_target_pairs={{0,1},{1,2},{2,3},{3,0},{4,5},{5,6},{6,7},{7,4},{8,9},{9,10},{10,1... | collective-permute-start | bytes 983048 | tf_op jit(solution)/shard_map/ppermute | solution.py:1156
  354.6 26.4 %collective-permute-start.6 = (bf16[256,640]{0,1:T(8,128)(2,1)S(1)}, bf16[256,640]{0,1:T(8,128)(2,1)S(1)}, u32[]{:S(2)}, u32[]{:S(2)}) collective-permute-start(bf16[256,640]{0,1:T(8,128)(2,1)S(1)} %get-tuple-element.105), channel_id=1, source_target_pairs={{0,2},{1,3},{2,0},{3,1},{4,6},{5,7},{6,4},{7,5},{8,10},{9,11},{10,... | collective-permute-start | bytes 983048 | tf_op jit(solution)/shard_map/ppermute | solution.py:1156
  356.7 30.9 %copy-start.6 = (f32[512,1024]{1,0:T(8,128)S(1)}, f32[512,1024]{1,0:T(8,128)}, u32[]{:S(2)}) copy-start(f32[512,1024]{1,0:T(8,128)} %get-tuple-element.51) | copy-start | bytes 6291460
  356.7 29.3 %collective-permute-start.7 = (bf16[256,640]{0,1:T(8,128)(2,1)S(1)}, bf16[256,640]{0,1:T(8,128)(2,1)S(1)}, u32[]{:S(2)}, u32[]{:S(2)}) collective-permute-start(bf16[256,640]{0,1:T(8,128)(2,1)S(1)} %get-tuple-element.104), channel_id=1, source_target_pairs={{0,3},{1,0},{2,1},{3,2},{4,7},{5,4},{6,5},{7,6},{8,11},{9,8},{10,9... | collective-permute-start | bytes 983048 | tf_op jit(solution)/shard_map/ppermute | solution.py:1156
  386.2 8.9 %collective-permute-start.8 = (bf16[256,640]{0,1:T(8,128)(2,1)S(1)}, bf16[256,640]{0,1:T(8,128)(2,1)S(1)}, u32[]{:S(2)}, u32[]{:S(2)}) collective-permute-start(bf16[256,640]{0,1:T(8,128)(2,1)S(1)} %get-tuple-element.71), channel_id=1, source_target_pairs={{0,8},{4,12},{8,0},{12,4},{16,24},{20,28},{24,16},{28,20},{1,9},{5... | collective-permute-start | bytes 983048 | tf_op jit(solution)/shard_map/ppermute | solution.py:1150
  386.4 9.8 %collective-permute-start.9 = (bf16[256,640]{0,1:T(8,128)(2,1)S(1)}, bf16[256,640]{0,1:T(8,128)(2,1)S(1)}, u32[]{:S(2)}, u32[]{:S(2)}) collective-permute-start(bf16[256,640]{0,1:T(8,128)(2,1)S(1)} %get-tuple-element.71), channel_id=1, source_target_pairs={{0,16},{4,20},{8,24},{12,28},{16,0},{20,4},{24,8},{28,12},{1,17},{... | collective-permute-start | bytes 983048 | tf_op jit(solution)/shard_map/ppermute | solution.py:1150
  395.0 4.2 %collective-permute-start.10 = (bf16[128,640]{0,1:T(8,128)(2,1)S(1)}, bf16[128,640]{0,1:T(8,128)(2,1)S(1)}, u32[]{:S(2)}, u32[]{:S(2)}) collective-permute-start(bf16[128,640]{0,1:T(8,128)(2,1)S(1)} %slice.234), channel_id=1, source_target_pairs={{0,16},{4,20},{8,24},{12,28},{16,0},{20,4},{24,8},{28,12},{1,17},{... | collective-permute-start | bytes 491528 | tf_op jit(solution)/shard_map/ppermute | solution.py:1150
  396.3 4.5 %collective-permute-start.11 = (bf16[128,640]{0,1:T(8,128)(2,1)S(1)}, bf16[128,640]{0,1:T(8,128)(2,1)S(1)}, u32[]{:S(2)}, u32[]{:S(2)}) collective-permute-start(bf16[128,640]{0,1:T(8,128)(2,1)S(1)} %slice.235), channel_id=1, source_target_pairs={{0,8},{4,12},{8,0},{12,4},{16,24},{20,28},{24,16},{28,20},{1,9},{5... | collective-permute-start | bytes 491528 | tf_op jit(solution)/shard_map/ppermute | solution.py:1150
  401.2 9.6 %collective-permute-start.12 = (bf16[1024,640]{0,1:T(8,128)(2,1)S(1)}, bf16[1024,640]{0,1:T(8,128)(2,1)S(1)}, u32[]{:S(2)}, u32[]{:S(2)}) collective-permute-start(bf16[1024,640]{0,1:T(8,128)(2,1)S(1)} %pad_maximum_fusion.9), channel_id=1, source_target_pairs={{0,4},{4,0},{8,12},{12,8},{16,20},{20,16},{24,28},{28,24},{1,5},{5... | collective-permute-start | bytes 3932168 | tf_op jit(solution)/shard_map/ppermute | solution.py:1150
  416.1 2.4 copy-start.7

commit v4 on v3

--- a/solution.py
+++ b/solution.py
@@ -13,27 +13,6 @@
 EPSILON = 1e-06
 BF = jnp.bfloat16
 F32 = jnp.float32
-
-
-def norm_parts(values):
-    scale = lax.rsqrt(jnp.mean(values * values, axis=-1, keepdims=True) + EPSILON)
-    return (values * scale, scale)
-
-
-def norm_back(normed, scale, grad):
-    return scale * (grad - normed * jnp.mean(grad * normed, axis=-1, keepdims=True))
-
-
-def plain_dot(left, right):
-    return jnp.dot(left, right, preferred_element_type=F32)
-
-
-def first_dot(left, right):
-    return lax.dot_general(left, right, (((0,), (0,)), ((), ())), preferred_element_type=F32)
-
-
-def second_dot(left, right):
-    return lax.dot_general(left, right, (((1,), (1,)), ((), ())), preferred_element_type=F32)
 
 
 MESH = pl.DeviceIdType.MESH
@@ -654,29 +633,30 @@
             into = self.high.at[slot - 1]
             copies.send(self.view(slot, 0, None), into, at, at, place.above(slot))
 
-    def total(self):
+    def total(self, into=None):
         place = self.place
         high = [self.high.at[slot - 1] for slot in range(1, place.n_head)]
         for slot, part in enumerate(high, 1):
             self.copies.receive(part, self.base + 4 * place.n_head + slot, place.up)
-        add_to(self.view(0, 0, None), *high)
+        add_to(self.view(0, 0, None), *high, into=into)
 
 
 PER_SCATTER = 20
 
 
-def add_to(ref, *others):
-    def add(*refs):
+def add_to(ref, *others, into=None):
+    def add(into, *refs):
         total = refs[0][...].astype(F32)
         for other in refs[1:]:
             total += other[...].astype(F32)
-        refs[0][...] = total.astype(BF)
-
+        into[...] = total.astype(BF)
+
+    refs = (ref if into is None else into, ref) + others
     if len(ref.shape) == 2:
-        add(ref, *others)
+        add(*refs)
     else:
         for i in range(ref.shape[0]):
-            add(ref.at[i], *(other.at[i] for other in others))
+            add(*(one.at[i] for one in refs))
 
 
 def dot(left, right):
@@ -1145,47 +1125,349 @@
     )(wf, nm, og, hidden, wo, pre, query, keys, values, attn, cos, sin, fresh, carry, scale)
 
 
+class Share:
+    def __init__(self, place, copies, view, base):
+        self.place, self.copies, self.view, self.base = place, copies, view, base
+
+    def hand_over(self, q):
+        at = self.base + 4 + q
+        self.copies.send(self.view(0, q, None), self.view(1, q, None), at, at, self.place.across)
+
+    def begin(self):
+        place, copies, at = self.place, self.copies, self.base
+        copies.send(self.view(0, 0, None), self.view(0, 1, None), at, at, place.by_x)
+        copies.send(self.view(0, 0, None), self.view(0, 2, None), at + 1, at + 1, place.by_y)
+        self.hand_over(0)
+
+    def spread(self):
+        place, copies, at = self.place, self.copies, self.base
+        copies.receive(self.view(0, 1, None), at, place.by_x)
+        copies.send(self.view(0, 1, 0), self.view(0, 3, 0), at + 2, at + 2, place.by_y)
+        copies.receive(self.view(0, 2, None), at + 1, place.by_y)
+        copies.send(self.view(0, 2, 1), self.view(0, 3, 1), at + 3, at + 3, place.by_x)
+        self.hand_over(1)
+        self.hand_over(2)
+
+    def complete(self):
+        place, copies, at = self.place, self.copies, self.base
+        copies.receive(self.view(0, 3, 0), at + 2, place.by_y)
+        copies.receive(self.view(0, 3, 1), at + 3, place.by_x)
+        self.hand_over(3)
+
+    def other_side(self):
+        for q in range(4):
+            self.copies.receive(self.view(1, q, None), self.base + 4 + q, self.place.across)
+
+
+PER_SHARE = 8
+
+
+def last_kernel(
+    n_head,
+    feed_piece,
+    tokens,
+    nin,
+    branch,
+    gated,
+    pre,
+    wa,
+    hidden_grad,
+    rates,
+    input_out,
+    feed_out,
+    attn_out,
+    down_out,
+    rates_out,
+    feed_ref,
+    attn_ref,
+    down_ref,
+    ga_ref,
+    a_far_x,
+    a_far_y,
+    a_near_x,
+    a_near_y,
+    a_high,
+    gd_ref,
+    d_far_x,
+    d_far_y,
+    d_near_x,
+    d_near_y,
+    d_high,
+    nin_ref,
+    branch_ref,
+    gated_ref,
+    pre_ref,
+    wa_ref,
+    x_ref,
+    grad_ref,
+    send_ref,
+    got_ref,
+    rates_high,
+    rates_sum,
+    rates_got,
+    rates_both,
+    sends,
+    receives,
+    locals_,
+):
+    rows, width = tokens.shape
+    quarter = width // 4
+    units = feed_piece.shape[1]
+    spans = rows // SPAN
+    place = Place(n_head)
+    copies = Copies(sends, receives, locals_)
+    order = (2, 1, 3, 0)
+
+    load_feed = copies.move(feed_piece, feed_ref.at[0, :, :, pl.ds(0, quarter)])
+    load_nin = copies.move(nin, nin_ref)
+    load_pre = {slot: copies.move(pre.at[slot], pre_ref.at[slot]) for slot in order}
+    load_gated = copies.move(gated, gated_ref)
+    load_branch = copies.move(branch, branch_ref)
+    late_loads = [copies.move(wa, wa_ref), copies.move(hidden_grad, grad_ref)]
+    for q in range(4):
+        far = pl.ds(pl.multiple_of(place.at[q] * quarter, quarter), quarter)
+        late_loads.append(copies.move(tokens.at[:, far], x_ref.at[:, pl.ds(q * quarter, quarter)]))
+    place.greet()
+
+    def tile(i):
+        return pl.ds(pl.multiple_of(i * SPAN, SPAN), SPAN)
+
+    def dot_last(left, right):
+        return lax.dot_general(left, right, (((1,), (1,)), ((), ())), preferred_element_type=F32)
+
+    def dot_first(left, right):
+        return lax.dot_general(left, right, (((0,), (0,)), ((), ())), preferred_element_type=F32)
+
+    def part(start, half, size):
+        if half is None:
+            return pl.ds(start, size)
+        return pl.ds(start + half * (size // 2), size // 2)
+
+    def feed_view(side, q, half):
+        return feed_ref.at[side, :, part(0, half, units), pl.ds(q * quarter, quarter)]
+
+    def attn_view(side, q, half):
+        return attn_ref.at[side, part(q * quarter, half, quarter), :]
+
+    def down_view(side, q, half):
+        return down_ref.at[side, part(0, half, HEAD_DIM), pl.ds(q * quarter, quarter)]
+
+    def ga_view(slot, q, half):
+        return ga_ref.at[slot, part(q * quarter, half, quarter), :]
+
+    def gd_view(slot, q, half):
+        return gd_ref.at[slot, part(0, half, HEAD_DIM), pl.ds(q * quarter, quarter)]
+
+    attn = Scatter(place, copies, ga_view, a_far_x, a_far_y, a_near_x, a_near_y, a_high, 0)
+    down = Scatter(place, copies, gd_view, d_far_x, d_far_y, d_near_x, d_near_y, d_high, PER_SCATTER)
+    base = 2 * PER_SCATTER
+    feed_share = Share(place, copies, feed_view, base)
+    attn_share = Share(place, copies, attn_view, base + PER_SHARE)
+    down_share = Share(place, copies, down_view, base + 2 * PER_SHARE)
+    base += 3 * PER_SHARE
+
+    load_feed.wait()
+    feed_share.begin()
+    for slot in range(1, n_head):
+        into = rates_high.at[slot - 1]
+        copies.send(rates.at[slot], into, base + slot, base + slot, place.above(slot))
+    load_nin.wait()
+
+    def slot_grads(slot):
+        load_pre[slot].wait()
+
+        @pl.loop(0, 4)
+        def _(i):
+            at = tile(3 - i)
+            ga_ref[slot, at, :] = dot_first(nin_ref[:, at], pre_ref[slot]).astype(BF)
+
+        lanes = pl.ds(slot * HEAD_DIM, HEAD_DIM)
+        gd_ref[slot] = dot_first(gated_ref[:, lanes], branch_ref[...]).astype(BF)
+
+    def begin(slot):
+        attn.begin(slot)
+        down.begin(slot)
+
+    def middle_step(slot):
+        attn.middle(slot)
+        down.middle(slot)
+
+    def end(slot):
+        attn.end(slot)
+        down.end(slot)
+
+    load_gated.wait()
+    load_branch.wait()
+    slot_grads(order[0])
+    begin(order[0])
+    slot_grads(order[1])
+    begin(order[1])
+    slot_grads(order[2])
+    begin(order[2])
+    middle_step(order[0])
+    slot_grads(order[3])
+    begin(order[3])
+    for load in late_loads:
+        load.wait()
+
+    def grad_in(at):
+        total = dot_last(pre_ref[0, at, :], wa_ref[0])
+        for slot in range(1, n_head):
+            total += dot_last(pre_ref[slot, at, :], wa_ref[slot])
+        return total
+
+    @pl.loop(0, spans)
+    def _(i):
+        send_ref[tile(i), :] = grad_in(tile(spans + i)).astype(BF)
+
+    copies.send(send_ref, got_ref, base, base, place.across)
+    middle_step(order[1])
+
+    total = rates[0]
+    for slot in range(1, n_head):
+        copies.receive(rates_high.at[slot - 1], base + slot, place.up)
+        total += rates_high[slot - 1]
+    base += n_head
+    rates_sum[0] = total
+    copies.send(rates_sum.at[0], rates_got.at[0], base, base, place.by_x)
+
+    end(order[0])
+    middle_step(order[2])
+    copies.receive(rates_got.at[0], base, place.by_x)
+    rates_sum[1] = total + rates_got[0]
+    copies.send(rates_sum.at[1], rates_got.at[1], base + 1, base + 1, place.by_y)
+
+    copies.receive(got_ref, base - n_head, place.across)
+
+    @pl.loop(0, spans)
+    def _(i):
+        at = tile(i)
+        values = x_ref[at, :].astype(F32)
+        norm = lax.rsqrt(jnp.mean(values * values, axis=-1, keepdims=True) + EPSILON)
+        normed = values * norm
+        grad = grad_in(at) + got_ref[at, :].astype(F32)
+        mean = jnp.mean(grad * normed, axis=-1, keepdims=True)
+        grad_ref[at, :] += norm * (grad - normed * mean)
+
+    for q in range(4):
+        far = pl.ds(pl.multiple_of(place.at[q] * quarter, quarter), quarter)
+        src = grad_ref.at[:, pl.ds(q * quarter, quarter)]
+        copies.move(src, input_out.at[:, far], later=True)
+    end(order[1])
+    middle_step(order[3])
+    copies.receive(rates_got.at[1], base + 1, place.by_y)
+    rates_both[0] = rates_sum[1] + rates_got[1]
+    copies.send(rates_both.at[0], rates_both.at[1], base + 2, base + 2, place.across)
+    feed_share.spread()
+    end(order[2])
+    end(order[3])
+    attn.total(attn_view(0, 0, None))
+    attn_share.begin()
+    down.total(down_view(0, 0, None))
+    down_share.begin()
+    copies.receive(rates_both.at[1], base + 2, place.across)
+    sides = (place.core, 1 - place.core)
+    for side in range(2):
+        copies.move(rates_both.at[side], rates_out.at[sides[side]], later=True)
+
+    def write(ref, out, side, q):
+        far = pl.ds(pl.multiple_of(place.at[q] * quarter, quarter), quarter)
+        near = pl.ds(q * quarter, quarter)
+        if ref is attn_ref:
+            src, dst = ref.at[side, near], out.at[sides[side], far]
+        elif ref is down_ref:
+            src, dst = ref.at[side, :, near], out.at[sides[side], :, far]
+        else:
+            src, dst = ref.at[side, :, :, near], out.at[sides[side], :, :, far]
+        copies.move(src, dst, later=True)
+
+    feed_share.complete()
+    for q in range(4):
+        write(feed_ref, feed_out, 0, q)
+    feed_share.other_side()
+    for q in range(4):
+        write(feed_ref, feed_out, 1, q)
+    attn_share.spread()
+    down_share.spread()
+    for q in range(3):
+        write(attn_ref, attn_out, 0, q)
+        write(down_ref, down_out, 0, q)
+    attn_share.complete()
+    down_share.complete()
+    write(attn_ref, attn_out, 0, 3)
+    write(down_ref, down_out, 0, 3)
+    attn_share.other_side()
+    down_share.other_side()
+    for q in range(4):
+        write(attn_ref, attn_out, 1, q)
+        write(down_ref, down_out, 1, q)
+    copies.finish()
+
+
+def last(n_head, feed_piece, tokens, nin, branch, gated, pre, wa, hidden_grad, rates):
+    rows, width = tokens.shape
+    _, units, quarter = feed_piece.shape
+    tall = 2 * rows
+
+    def scatter_buffers(shape, halved):
+        half = tuple(n // 2 if i == halved else n for i, n in enumerate(shape))
+        return [
+            ((n_head,) + half, BF),
+            ((n_head,) + half, BF),
+            ((n_head,) + shape, BF),
+            ((n_head,) + shape, BF),
+            ((n_head - 1,) + shape, BF),
+        ]
+
+    outs = [
+        ((rows, width), F32),
+        ((2, 3, units, width), BF),
+        ((2, width, 4 * HEAD_DIM), BF),
+        ((2, HEAD_DIM, width), BF),
+        ((2, 8, HEAD_DIM), F32),
+    ]
+    buffers = [
+        outs[1],
+        outs[2],
+        outs[3],
+        ((n_head, width, 4 * HEAD_DIM), BF),
+        *scatter_buffers((quarter, 4 * HEAD_DIM), 0),
+        ((n_head, HEAD_DIM, width), BF),
+        *scatter_buffers((HEAD_DIM, quarter), 0),
+        ((tall, width), BF),
+        ((tall, width), BF),
+        (gated.shape, BF),
+        (pre.shape, BF),
+        (wa.shape, BF),
+        ((rows, width), BF),
+        ((rows, width), F32),
+        ((rows, width), BF),
+        ((rows, width), BF),
+        ((n_head - 1, 8, HEAD_DIM), F32),
+        ((2, 8, HEAD_DIM), F32),
+        ((2, 8, HEAD_DIM), F32),
+        ((2, 8, HEAD_DIM), F32),
+    ]
+    n_sems = 2 * PER_SCATTER + 3 * PER_SHARE + n_head + 3
+    return pl.pallas_call(
+        functools.partial(last_kernel, n_head),
+        out_shape=[jax.ShapeDtypeStruct(*out) for out in outs],
+        in_specs=[ANY] * 8 + [IN_VMEM],
+        out_specs=[ANY] * len(outs),
+        scratch_shapes=[pltpu.VMEM(*b) for b in buffers]
+        + [
+            pltpu.SemaphoreType.DMA((n_sems,)),
+            pltpu.SemaphoreType.DMA((n_sems,)),
+            pltpu.SemaphoreType.DMA((64,)),
+        ],
+        compiler_params=pltpu.CompilerParams(
+            collective_id=2, has_side_effects=True, vmem_limit_bytes=60 << 20
+        ),
+        name="last",
+    )(feed_piece, tokens, nin, branch, gated, pre, wa, hidden_grad, rates)
+
+
 def make(n_dp, n_head):
-    def swap(array, bit):
-        return lax.ppermute(array, "dp", [(i, i ^ bit) for i in range(n_dp)])
-
-    def from_above(array, step):
-        return lax.ppermute(array, "head", [((i + step) % n_head, i) for i in range(n_head)])
-
-    def to_above(array, step):
-        return lax.ppermute(array, "head", [(i, (i + step) % n_head) for i in range(n_head)])
-
-    def share(pieces, axis):
-        half = pieces.shape[axis] // 2
-        by_x = swap(pieces, 2)
-        by_y = swap(pieces, 4)
-        low = swap(lax.slice_in_dim(by_x, 0, half, axis=axis), 4)
-        high = swap(lax.slice_in_dim(by_y, half, 2 * half, axis=axis), 2)
-        return [pieces, by_x, by_y, jnp.concatenate([low, high], axis=axis)]
-
-    def collect(parts, axis):
-        own, for_x, for_y, for_far = parts
-        half = own.shape[axis] // 2
-
-        def cut(array, which):
-            return lax.slice_in_dim(array, which * half, (which + 1) * half, axis=axis)
-
-        def add(left, right):
-            return (left.astype(F32) + right.astype(F32)).astype(BF)
-
-        low = swap(cut(for_far, 0), 4)
-        high = swap(cut(for_far, 1), 2)
-        by_x = swap(jnp.concatenate([add(cut(for_x, 0), low), cut(for_x, 1)], axis=axis), 2)
-        by_y = swap(jnp.concatenate([cut(for_y, 0), add(cut(for_y, 1), high)], axis=axis), 4)
-        plane = (own.astype(F32) + by_x.astype(F32) + by_y.astype(F32)).astype(BF)
-        total = plane[0].astype(F32)
-        for step in range(1, n_head):
-            total = total + to_above(plane[step], step).astype(F32)
-        if n_dp > 8:
-            groups = [[i + 8 * j for j in range(n_dp // 8)] for i in range(8)]
-            total = lax.psum(total, "dp", axis_index_groups=groups)
-        return total.astype(BF)
-
     def on_device(
         tokens,
         attn_query,
@@ -1199,29 +1481,6 @@
         ffn_down,
         out_grad,
     ):
-        width = tokens.shape[1]
-        quarter = width // 4
-        rows = tokens.shape[0]
-        spans = rows // SPAN
-        units = ffn_left.shape[1] // 2
-        dp = lax.axis_index("dp")
-        place = lax.axis_index("head")
-        core = dp & 1
-        plane = (dp >> 1) & 3
-
-        def relative(array, axis):
-            return jnp.concatenate(
-                [
-                    lax.dynamic_slice_in_dim(array, (plane ^ q) * quarter, quarter, axis=axis)
-                    for q in range(4)
-                ],
-                axis=axis,
-            )
-
-        def half_of(array, axis):
-            size = array.shape[axis] // 2
-            return lax.dynamic_slice_in_dim(array, core * size, size, axis=axis)
-
         ffn = jnp.stack([ffn_left.T, ffn_right.T, ffn_down])
         rates_in = jnp.pad(rotation_rates.reshape(2, HEAD_DIM), ((0, 6), (0, 0)))
         (
@@ -1273,63 +1532,44 @@
             carry,
             scale_attn,
         )
-        rates_grad = rates_grad[:, 0]
-        left_grad, right_grad, down_grad = jnp.concatenate(share(feed_piece, 1), axis=2)
-        inputs = relative(tokens, 1).astype(F32)
-        normed_one, scale_one = norm_parts(inputs)
-        out_grads = first_dot(branch_rows, gated)
-
-        def core_scatter(array):
-            return array[:rows] + swap(array[rows:].astype(BF), 1).astype(F32)
-
-        attn_grads = []
-        grad_in = None
-        for r in range(n_head):
-            main = first_dot(gathered_in, grad_pre[r]).astype(BF)
-            outs = out_grads[:, r * HEAD_DIM : (r + 1) * HEAD_DIM].astype(BF)
-            attn_grads.append(jnp.concatenate([main, outs], axis=1))
-            term = second_dot(grad_pre[r], attn_weights[r])
-            grad_in = term if grad_in is None else grad_in + term
-        grad_in = core_scatter(grad_in)
-        input_grad = grad_hidden + norm_back(normed_one, scale_one, grad_in)
-
-        attn_grads = jnp.stack(attn_grads).reshape(n_head, 4, quarter, 5 * HEAD_DIM)
-        piece = collect([attn_grads[:, q] for q in range(4)], 1)
-        attn_total = jnp.concatenate(share(piece, 0), axis=0)
-        rates_piece = rates_grad[0]
-        for step in range(1, n_head):
-            rates_piece = rates_piece + to_above(rates_grad[step], step)
-        groups = [list(range(0, n_dp, 2)), list(range(1, n_dp, 2))]
-        rates_piece = lax.psum(rates_piece, "dp", axis_index_groups=groups)
-
-        def both(array, axis):
-            other = swap(array, 1)
-            first = jnp.where(core == 0, array, other)
-            second = jnp.where(core == 0, other, array)
-            return first, second
-
-        first, second = both(relative(attn_total, 0), 0)
-        matrices = []
-        for i in range(5):
-            pair = [part[:, i * HEAD_DIM : (i + 1) * HEAD_DIM] for part in (first, second)]
-            matrices.append(jnp.concatenate(pair, axis=1).astype(F32))
-        query_grad, key_grad, value_grad, gate_grad, out_proj_grad = matrices
-        out_proj_grad = out_proj_grad.T
-        rates_grad = jnp.concatenate(both(rates_piece, 0), axis=0)
-        ffn_grads = jnp.stack([relative(g, 1) for g in (left_grad, right_grad, down_grad)])
-        ffn_grads = jnp.concatenate(both(ffn_grads, 1), axis=1).astype(F32)
+        input_grad, feed_grads, attn_grads, down_grads, rates_grad = last(
+            n_head,
+            feed_piece,
+            tokens,
+            gathered_in,
+            branch_rows,
+            gated,
+            grad_pre,
+            attn_weights,
+            grad_hidden,
+            rates_grad,
+        )
+
+        def over_rest(grad):
+            if n_dp == 8:
+                return grad
+            groups = [[i + 8 * j for j in range(n_dp // 8)] for i in range(8)]
+            return lax.psum(grad, "dp", axis_index_groups=groups)
+
+        def projection(i):
+            halves = attn_grads[:, :, i * HEAD_DIM : (i + 1) * HEAD_DIM].astype(F32)
+            return over_rest(jnp.concatenate([halves[0], halves[1]], axis=1))
+
+        def feed(i):
+            return feed_grads[:, i].astype(F32).reshape(-1, tokens.shape[1])
+
         return (
             block_out,
-            relative(input_grad, 1),
-            query_grad,
-            key_grad,
-            value_grad,
-            gate_grad,
-            out_proj_grad,
-            rates_grad,
-            ffn_grads[0].T,
-            ffn_grads[1].T,
-            ffn_grads[2],
+            input_grad,
+            projection(0),
+            projection(1),
+            projection(2),
+            projection(3),
+            over_rest(down_grads.astype(F32).reshape(-1, tokens.shape[1])),
+            over_rest(rates_grad[:, 0].reshape(-1)),
+            over_rest(feed(0).T),
+            over_rest(feed(1).T),
+            over_rest(feed(2)),
         )
 
     return on_device

time: 425 us -> 330 us (0.78)
  the two profiles are of different devices: /device:TPU:9 before, /device:TPU:1 now
where the time goes in v4:
time: 330 us
  Pallas kernels  305 us (92%)
  other arithmetic  17.3 us (5%)
  local copies, waits for them, and re-layouts  6.98 us (2%)
    pallas_call x1, Pallas kernels, forward(): pl.pallas_call(functools.partial(forward_kernel, n_head), out_shape=[jax....  113 us
    pallas_call x1, Pallas kernels, middle(): pl.pallas_call(functools.partial(middle_kernel, n_head), out_shape=[jax.S...  110 us
    pallas_call x1, Pallas kernels, last(): pl.pallas_call(functools.partial(last_kernel, n_head), out_shape=[jax.Sha...  82.3 us

profile of v4, /device:TPU:1, one launch (start us, length us, event | category | flops | bytes accessed | tf_op | source)
XLA Modules:
  0.0 329.7 jit_solution(5499320941729603841)
XLA Ops:
  0.6 1.3 pad.4.rates
  1.9 3.7 %pad_maximum_fusion.ffn = bf16[3,704,1024]{2,1,0:T(8,128)(2,1)} fusion(bf16[1,704,1024]{2,1,0:T(8,128)(2,1)} %bitcast.43, bf16[1,704,1024]{2,1,0:T(8,128)(2,1)} %bitcast.44, bf16[1,704,1024]{2,1,0:T(8,128)(2,1)} %bitcast.45), kind=kLoop, calls=%fused_computation | loop fusion | flops 4325376 | bytes 8650752 | tf_op jit(solution)/shard_map/stack | solution.py:1484
  5.7 112.7 %forward.1 = (bf16[4,1024,512]{2,1,0:T(8,128)(2,1)}, bf16[512,1024]{1,0:T(8,128)(2,1)}, bf16[3,1408,1024]{2,1,0:T(8,128)(2,1)}, bf16[1024,1024]{1,0:T(8,128)(2,1...) custom-call(bf16[512,1024]{1,0:T(8,128)(2,1)} %tokens.3, ...), custom_call_target="tpu_custom_call" | custom-call | tf_op jit(solution)/shard_map/forward/pallas_call | solution.py:589
  118.4 109.7 %middle.1 = (bf16[3,352,256]{2,1,0:T(8,128)(2,1)}, bf16[512,1024]{1,0:T(8,128)(2,1)}, f32[512,1024]{1,0:T(8,128)}, bf16[1024,1024]{1,0:T(8,128)(2,1)}, bf16[4,10...) custom-call(bf16[3,1408,1024]{2,1,0:T(8,128)(2,1)} %get-tuple-element.40.wf, bf16[1024,1024]{1,0:T(8,128)(2,1)} %get-tuple-element.41.nm, ...), custom_call_target="tpu_custom_call" | custom-call | tf_op jit(solution)/shard_map/middle/pallas_call | solution.py:1110
  228.1 82.3 %last.1 = (f32[512,1024]{1,0:T(8,128)}, bf16[2,3,352,1024]{3,2,1,0:T(8,128)(2,1)}, bf16[2,1024,512]{2,1,0:T(8,128)(2,1)}, bf16[2,128,1024]{2,1,0:T(8,128)(2,1)}, f32[2,8,128]{2,1,0:T(8,128)}) custom-call(bf16[3,352,256]{2,1,0:T(8,128)(2,1)} %get-tuple-element.56.feed_piece, bf16[512,1024]{1,0:T(8,128)(2,1)} %tokens.3, ...), custom_call_target="tpu_custom_call" | custom-call | tf_op jit(solution)/shard_map/last/pallas_call | solution.py:1452
  310.4 1.3 slice.60
  311.6 2.1 bitcast_convert_fusion.1
  313.8 1.8 slice_convert_fusion
  315.6 0.1 slice_bitcast_fusion.1
  315.8 1.0 pad_maximum_fusion.4
  316.8 0.0 slice-start
  316.8 1.0 pad_maximum_fusion.3
  317.8 0.0 slice-start.1
  317.8 0.1 slice_bitcast_fusion.5
  318.0 1.0 pad_maximum_fusion.2
  319.0 1.0 pad_maximum_fusion.1
  320.1 0.0 slice-done
  320.1 0.0 slice-done.1
  320.1 0.9 fusion
  320.9 2.0 bitcast_convert_fusion
  323.0 0.0 copy-start.1
  323.0 3.4 %convert_bitcast_fusion = (f32[1024,704]{0,1:T(8,128)}, f32[1024,704]{0,1:T(8,128)}) fusion(bf16[2,1,352,1024]{3,2,1,0:T(8,128)(2,1)S(1)} %get-tuple-element.70, bf16[2,1,352,1024]{3,2,1,0:T(8,128)(2,1)S(1)} %get-tuple-element.71), kind=kLoop, calls=%fused_computation.1 | loop fusion | flops 1441792 | bytes 8650752 | tf_op jit(solution)/shard_map/transpose | solution.py:1571
  326.4 0.0 copy-start
  326.4 0.0 copy-done.1
  326.4 1.0 copy.24
  327.4 1.0 copy-done
  328.4 1.3 copy.25
  (1 shorter events, 0.0 us)
Async XLA Ops:
  316.8 3.3 slice-start
  317.8 2.2 slice-start.1
  323.0 3.4 %copy-start.1 = (bf16[512,1024]{1,0:T(8,128)(2,1)S(1)}, bf16[512,1024]{1,0:T(8,128)(2,1)}, u32[]{:S(2)}) copy-start(bf16[512,1024]{1,0:T(8,128)(2,1)} %get-tuple-element.101) | copy-start | bytes 3145732
  326.4 2.0 copy-start

commit v5 on v4

--- a/solution.py
+++ b/solution.py
@@ -122,21 +122,26 @@
         )
         self.copies.send(own, self.view(1, 0, None), self.base + 1, self.base + 1, place.down, when=z > 0)
 
-    def arrived(self, slot):
+    def arrived(self, slot, when=True):
         place, copies, z, base = self.place, self.copies, self.place.z, self.base
         last = place.n_head - 1
-        copies.receive(self.view(slot, 0, None), base + slot, place.up)
+        if when is True:
+            copies.receive(self.view(slot, 0, None), base + slot, place.up)
+        else:
+            pl.when(when)(lambda: copies.receive(self.view(slot, 0, None), base + slot, place.up))
         from_up = z + slot <= last
         piece = self.view(slot, 0, None)
-        down = jnp.logical_and(from_up, z > 0)
+        down = jnp.logical_and(jnp.logical_and(from_up, z > 0), when)
         up = jnp.logical_and(jnp.logical_not(from_up), z < last)
+        up = jnp.logical_and(up, when)
+        always = None if when is True else when
         after = jnp.minimum(slot + 1, last)
         before = jnp.maximum(slot - 1, 1)
         copies.send(piece, self.view(after, 0, None), base + 1 + slot, base + after, place.down, when=down)
         copies.send(piece, self.view(before, 0, None), base + 1 + slot, base + before, place.up, when=up)
         at = base + 4 * slot + 4
-        copies.send(piece, self.view(slot, 1, None), at, at, place.by_x)
-        copies.send(piece, self.view(slot, 2, None), at + 1, at + 1, place.by_y)
+        copies.send(piece, self.view(slot, 1, None), at, at, place.by_x, when=always)
+        copies.send(piece, self.view(slot, 2, None), at + 1, at + 1, place.by_y, when=always)
 
     def spread(self, slot):
         place, copies = self.place, self.copies
@@ -165,7 +170,9 @@
     wv,
     wg,
     wo,
-    ffn,
+    ffn_left,
+    ffn_right,
+    ffn_down,
     rates,
     wa_out,
     wo_out,
@@ -215,7 +222,7 @@
 ):
     rows, width = tokens.shape
     quarter = width // 4
-    units = ffn.shape[1] // 2
+    units = ffn_down.shape[0] // 2
     tiles = 2 * rows // SPAN
     place = Place(n_head)
     z, core = place.z, place.core
@@ -234,8 +241,9 @@
             loads.append(copies.move(src, wa_ref.at[0, near, pl.ds(i * HEAD_DIM, HEAD_DIM)]))
         src = wo.at[columns(core * HEAD_DIM, HEAD_DIM), far]
         loads.append(copies.move(src, wo_ref.at[pl.ds(0, HEAD_DIM), near]))
-        src = ffn.at[:, pl.ds(pl.multiple_of(core * units, 16), units), far]
-        loads.append(copies.move(src, wf_ref.at[:, pl.ds(0, units), near]))
+        for i, w in enumerate((ffn_left, ffn_right, ffn_down)):
+            src = w.at[pl.ds(pl.multiple_of(core * units, 16), units), far]
+            loads.append(copies.move(src, wf_ref.at[i, pl.ds(0, units), near]))
         own_loads.append(loads)
     token_loads = [
         copies.move(
@@ -308,10 +316,8 @@
     base += 1
     nin_other = nin_ref.at[pl.ds(rows, rows)]
     copies.send(nin_ref.at[pl.ds(0, rows)], nin_other, base, base, place.across)
-    own_loads[0][5].wait()
-    feed.begin()
-    for loads in own_loads[1:]:
-        for load in loads:
+    for q, loads in enumerate(own_loads):
+        for load in loads[5:] if q == 0 else loads:
             load.wait()
     for step in range(1, n_head):
         copies.receive(rates_ref.at[step], base - 5 + step, place.up)
@@ -336,7 +342,7 @@
     def slot_compute(slot):
         head = 2 * lax.rem(z + slot, n_head) + core
         decay = decay_of(head)
-        rate = rates_ref[slot, pl.ds(core, 1), :]
+        rate = rates_ref[slot, :, columns(core * HEAD_DIM, HEAD_DIM)]
         coarse = (z * rows).astype(F32) + 32.0 * iota((rows // 32, HEAD_DIM), 0)
         coarse = coarse * rate
         fine = iota((32, HEAD_DIM), 0) * rate
@@ -409,22 +415,20 @@
     attn_down.spread(first)
     attn_in.arrived(third)
     attn_down.arrived(third)
+    feed.begin()
     attn_in.spread(second)
     attn_down.spread(second)
     attn_in.complete(first)
     slot_compute(first)
-    feed.arrived(first)
     attn_in.spread(third)
     attn_down.spread(third)
+    feed.arrived(first)
     attn_in.complete(second)
     slot_compute(second)
-    feed.arrived(second)
-    feed.spread(first)
+    inner = jnp.logical_and(z > 0, z < last)
+    feed.arrived(second, inner)
     attn_in.complete(third)
     slot_compute(third)
-    feed.arrived(third)
-    feed.spread(second)
-
     base += 1
     chain_base = base
     n_chain = 2 * n_head
@@ -444,42 +448,49 @@
             device_id_type=MESH,
         )
 
-    @pl.loop(0, n_chain)
-    def _(index):
-        slot, seq, decay = chain_at(index)
-
-        @pl.when(z > 0)
-        def _():
+    def hand_on(index, slot, seq, decay):
+        total = jnp.exp(-decay * rows) * carry_ref[slot, seq].astype(F32)
+        for n in range(rows // SPAN):
+            left = rows - (n + 1) * SPAN
+            total += jnp.exp(-decay * left) * fresh_ref[slot, seq * (rows // SPAN) + n]
+        message_ref[slot, seq] = total.astype(BF)
+        chain_copy(index, slot, seq).start()
+
+    @pl.when(z == 0)
+    def _():
+        @pl.loop(0, n_chain)
+        def _(index):
+            slot, seq, decay = chain_at(index)
+            carry_ref[slot, seq] = jnp.zeros(carry_ref.shape[2:], BF)
+            hand_on(index, slot, seq, decay)
+
+    feed.arrived(second, jnp.logical_not(inner))
+    feed.spread(first)
+    feed.arrived(third)
+
+    @pl.when(z > 0)
+    def _():
+        @pl.loop(0, n_chain)
+        def _(index):
+            slot, seq, decay = chain_at(index)
             copies.receive(carry_ref.at[slot, seq], chain_base + index, place.down)
-
-        @pl.when(z == 0)
-        def _():
-            carry_ref[slot, seq] = jnp.zeros(carry_ref.shape[2:], BF)
-
-        @pl.when(z < last)
-        def _():
-            total = jnp.exp(-decay * rows) * carry_ref[slot, seq].astype(F32)
-            for n in range(rows // SPAN):
-                left = rows - (n + 1) * SPAN
-                total += jnp.exp(-decay * left) * fresh_ref[slot, seq * (rows // SPAN) + n]
-            message_ref[slot, seq] = total.astype(BF)
-            chain_copy(index, slot, seq).start()
+            pl.when(z < last)(lambda: hand_on(index, slot, seq, decay))
 
     copies.move(carry_ref, carry_out, later=True)
-
-    squares_ref[...] = jnp.zeros_like(squares_ref)
-
-    @pl.loop(0, n_head)
-    def _(slot):
-        decay = decay_of(2 * lax.rem(z + slot, n_head) + core)
-        early = jnp.exp(-decay * (iota((SPAN, HEAD_DIM), 0) + 1.0))
-
-        @pl.loop(0, 2)
-        def _(seq):
+    feed.spread(second)
+
+    def apply(seq):
+        mine = pl.ds(seq * rows, rows)
+        squares_ref[mine, :] = jnp.zeros((rows, HEAD_DIM), F32)
+
+        @pl.loop(0, n_head)
+        def _(slot):
+            decay = decay_of(2 * lax.rem(z + slot, n_head) + core)
+            early = jnp.exp(-decay * (iota((SPAN, HEAD_DIM), 0) + 1.0))
             state = carry_ref[slot, seq].astype(F32)
             for n in range(rows // SPAN):
                 i = seq * (rows // SPAN) + n
-                at = tile(i)
+                at = pl.ds(i * SPAN, SPAN)
                 both = dot(q_ref[slot, at, :], jnp.concatenate(split(state), axis=1))
                 attn = attn_ref[slot, at, :]
                 attn += early * (both[:, :HEAD_DIM] + both[:, HEAD_DIM:])
@@ -488,39 +499,39 @@
                 if n + 1 < rows // SPAN:
                     state = jnp.exp(-decay * SPAN) * state + fresh_ref[slot, i]
 
-    copies.move(attn_ref, attn_out, later=True)
+    def gating(seq):
+        for n in range(rows // SPAN):
+            at = pl.ds(seq * rows + n * SPAN, SPAN)
+            total = squares_ref[at, :] + other_squares_ref[at, :]
+            scale = lax.rsqrt(total / width + EPSILON)
+            other_squares_ref[at, :] = scale
+            for slot in range(n_head):
+                gate = pre_ref[slot, at, pl.ds(3 * HEAD_DIM, HEAD_DIM)]
+                gated = (attn_ref[slot, at, :] * scale * gate).astype(BF)
+                gated_ref[at, pl.ds(slot * HEAD_DIM, HEAD_DIM)] = gated
+
     base += n_chain
     own, other = pl.ds(0, rows), pl.ds(rows, rows)
-    copies.send(squares_ref.at[own], other_squares_ref.at[other], base, base, place.across)
-    copies.send(squares_ref.at[other], other_squares_ref.at[own], base + 1, base + 1, place.across)
-    feed.spread(third)
+    apply(1)
+    copies.send(squares_ref.at[other], other_squares_ref.at[own], base, base, place.across)
+    apply(0)
+    copies.send(squares_ref.at[own], other_squares_ref.at[other], base + 1, base + 1, place.across)
+    copies.move(attn_ref, attn_out, later=True)
     for slot in (first, second, third):
         attn_down.complete(slot)
-    copies.receive(other_squares_ref.at[other], base, place.across)
-    copies.receive(other_squares_ref.at[own], base + 1, place.across)
-
-    @pl.loop(0, tiles)
-    def _(i):
-        at = tile(i)
-        total = squares_ref[at, :] + other_squares_ref[at, :]
-        scale = lax.rsqrt(total / width + EPSILON)
-        other_squares_ref[at, :] = scale
-        for slot in range(n_head):
-            gate = pre_ref[slot, at, pl.ds(3 * HEAD_DIM, HEAD_DIM)]
-            gated = (attn_ref[slot, at, :] * scale * gate).astype(BF)
-            gated_ref[at, pl.ds(slot * HEAD_DIM, HEAD_DIM)] = gated
-
+    copies.receive(other_squares_ref.at[other], base + 1, place.across)
+    gating(1)
+    base += 2
+    for n in range(rows // SPAN):
+        gated = gated_ref[pl.ds(rows + n * SPAN, SPAN), :]
+        branch_ref[pl.ds(n * SPAN, SPAN), :] = dot(gated, wo_ref[...]).astype(BF)
+    copies.send(branch_ref, other_branch_ref, base, base, place.across)
+    copies.receive(other_squares_ref.at[own], base - 2, place.across)
+    gating(0)
     copies.move(other_squares_ref, scale_out, later=True)
     copies.move(gated_ref, gated_out, later=True)
     copies.move(wo_ref, wo_out, later=True)
-    base += 2
-
-    @pl.loop(0, rows // SPAN)
-    def _(i):
-        gated = gated_ref[pl.ds(pl.multiple_of(rows + i * SPAN, SPAN), SPAN), :]
-        branch_ref[tile(i), :] = dot(gated, wo_ref[...]).astype(BF)
-
-    copies.send(branch_ref, other_branch_ref, base, base, place.across)
+    feed.spread(third)
 
     @pl.loop(0, rows // SPAN)
     def _(i):
@@ -554,9 +565,9 @@
     copies.finish()
 
 
-def forward(n_head, tokens, out_grad, wq, wk, wv, wg, wo, ffn, rates):
+def forward(n_head, tokens, out_grad, wq, wk, wv, wg, wo, ffn_left, ffn_right, ffn_down, rates):
     rows, width = tokens.shape
-    units = ffn.shape[1] // 2
+    units = ffn_down.shape[0] // 2
     tall = 2 * rows
     buffers = [
         ((n_head, width, 4 * HEAD_DIM), BF),
@@ -581,7 +592,7 @@
         ((rows, width), BF),
         ((rows, width), F32),
         ((tall, width), BF),
-        ((n_head, 8, HEAD_DIM), F32),
+        ((n_head, 1, 2 * HEAD_DIM), F32),
         ((tall, width), BF),
     ]
     out_of = [0, 1, 2, 4, 5, 6, 7, 8, 9, 10, 11, 12, 13, 16, 17, 20, 21, 23]
@@ -589,19 +600,19 @@
     return pl.pallas_call(
         functools.partial(forward_kernel, n_head),
         out_shape=[jax.ShapeDtypeStruct(*buffers[i]) for i in out_of],
-        in_specs=[ANY] * 8 + [IN_VMEM],
+        in_specs=[ANY] * 10 + [IN_VMEM],
         out_specs=[ANY] * len(out_of),
         scratch_shapes=[pltpu.VMEM(*b) for b in buffers]
         + [
             pltpu.SemaphoreType.DMA((n_sems,)),
             pltpu.SemaphoreType.DMA((n_sems,)),
-            pltpu.SemaphoreType.DMA((80,)),
+            pltpu.SemaphoreType.DMA((96,)),
         ],
         compiler_params=pltpu.CompilerParams(
             collective_id=0, has_side_effects=True, vmem_limit_bytes=62 << 20
         ),
         name="forward",
-    )(tokens, out_grad, wq, wk, wv, wg, wo, ffn, rates)
+    )(tokens, out_grad, wq, wk, wv, wg, wo, ffn_left, ffn_right, ffn_down, rates)
 
 
 class Scatter:
@@ -623,20 +634,23 @@
         add_to(self.view(slot, 2, 1), self.far_x.at[slot])
         copies.send(self.view(slot, 2, None), self.near_y.at[slot], at + 3, at + 3, place.by_y)
 
-    def end(self, slot):
+    def end(self, slot, onward=True):
         place, copies, at = self.place, self.copies, self.base + 4 * slot
         copies.receive(self.near_x.at[slot], at + 2, place.by_x)
         copies.receive(self.near_y.at[slot], at + 3, place.by_y)
         add_to(self.view(slot, 0, None), self.near_x.at[slot], self.near_y.at[slot])
-        if slot:
-            at = self.base + 4 * place.n_head + slot
-            into = self.high.at[slot - 1]
-            copies.send(self.view(slot, 0, None), into, at, at, place.above(slot))
-
-    def total(self, into=None):
+        if slot and onward:
+            self.go_up(slot)
+
+    def go_up(self, slot):
+        at = self.base + 4 * self.place.n_head + slot
+        into = self.high.at[slot - 1]
+        self.copies.send(self.view(slot, 0, None), into, at, at, self.place.above(slot))
+
+    def total(self, into=None, slots=(1, 2, 3)):
         place = self.place
-        high = [self.high.at[slot - 1] for slot in range(1, place.n_head)]
-        for slot, part in enumerate(high, 1):
+        high = [self.high.at[slot - 1] for slot in slots]
+        for slot, part in zip(slots, high):
             self.copies.receive(part, self.base + 4 * place.n_head + slot, place.up)
         add_to(self.view(0, 0, None), *high, into=into)
 
@@ -791,19 +805,23 @@
             t_ref[1, at, rows_at] = (grad * left).astype(BF)
             t_ref[2, at, rows_at] = (left * right).astype(BF)
 
-        @pl.loop(0, width // SPAN)
-        def _(i):
-            columns = tile(i)
+        def gradient(columns):
             for m, right in enumerate((nm_ref, nm_ref, og_ref)):
                 g_ref[m, at, columns] = dot(t_ref[m, at, :], right[:, columns]).astype(BF)
+
+        gradient(pl.ds(3 * quarter, quarter))
+        feed.begin(slot)
+
+        @pl.loop(0, 3)
+        def _(q):
+            gradient(pl.ds(pl.multiple_of(q * quarter, quarter), quarter))
 
     load_nm.wait()
     load_og.wait()
     for i, slot in enumerate(order):
         load_wf[slot].wait()
         feed_slot(slot)
-        feed.begin(slot)
-        if i == 2:
+        if i == 1:
             feed.middle(order[0])
     feed.middle(order[1])
     for load in early_loads:
@@ -816,6 +834,7 @@
         send_ref[tile(i), :] = total.astype(BF)
 
     copies.send(send_ref, got_ref, base, base, place.across)
+    feed.end(order[0])
 
     @pl.loop(0, spans)
     def _(i):
@@ -823,7 +842,6 @@
         total = dot_first(t_ref[0, :, at], wf_ref[0]) + dot_first(t_ref[1, :, at], wf_ref[1])
         mid_ref[at, :] = total
 
-    feed.end(order[0])
     copies.receive(got_ref, base, place.across)
 
     @pl.loop(0, rows // 128)
@@ -840,21 +858,6 @@
 
     copies.send(nm_ref.at[own], nm_ref.at[other], base + 1, base + 1, place.across)
     copies.move(mid_ref, hidden_grad_out, later=True)
-    copies.sent(base)
-
-    @pl.loop(0, spans)
-    def _(i):
-        send_ref[tile(i), :] = dot_first(t_ref[2, :, tile(spans + i)], wf_ref[2]).astype(BF)
-
-    copies.receive(nm_ref.at[other], base + 1, place.across)
-    copies.move(nm_ref, branch_out, later=True)
-    copies.send(send_ref, got_ref, base + 2, base + 2, place.across)
-
-    @pl.loop(0, spans)
-    def _(i):
-        at = tile(i)
-        hidden_ref[at, :] += dot_first(t_ref[2, :, at], wf_ref[2])
-
     loads = []
     for slot in range(n_head):
         lanes = pl.ds(slot * 2 * HEAD_DIM, 2 * HEAD_DIM)
@@ -882,46 +885,44 @@
     def v_at(slot, at):
         return wf_ref[1, at, pl.ds(slot * HEAD_DIM, HEAD_DIM)]
 
+    def pre_of(slot):
+        holder, start = ((wf_ref.at[0], 0), (wf_ref.at[0], 1), (wf_ref.at[1], 1), (og_ref, 0))[slot]
+        return holder, start * 4 * HEAD_DIM
+
     def pre_at(slot, at, part):
-        start = (slot % 2) * 4 * HEAD_DIM + part * HEAD_DIM
-        holder = t_ref.at[2] if slot < 2 else wf_ref.at[0]
-        return holder.at[at, pl.ds(start, HEAD_DIM)]
-
-    @pl.loop(0, tiles)
-    def _(i):
-        at = tile(i)
-        grad = dot_last(nm_ref[at, :], wo_ref[...])
-        norm = scale_ref[at, :]
-        total = jnp.zeros((SPAN, 1), F32)
-        for slot in range(n_head):
-            part = grad[:, slot * HEAD_DIM : (slot + 1) * HEAD_DIM]
-            normed = attn_ref[slot, at, :] * norm
-            pre_at(slot, at, 3)[...] = (part * normed).astype(BF)
-            part = part * gate_ref[slot, at, :]
-            gate_ref[slot, at, :] = part
-            total += jnp.sum(part * normed, axis=-1, keepdims=True)
-        sum_ref[at, :] = jnp.broadcast_to(total, (SPAN, HEAD_DIM))
-
-    base += 3
+        holder, start = pre_of(slot)
+        return holder.at[at, pl.ds(start + part * HEAD_DIM, HEAD_DIM)]
+
+    def gate_back(seq):
+        for n in range(spans):
+            at = pl.ds(seq * rows + n * SPAN, SPAN)
+            grad = dot_last(nm_ref[at, :], wo_ref[...])
+            norm = scale_ref[at, :]
+            total = jnp.zeros((SPAN, 1), F32)
+            for slot in range(n_head):
+                part = grad[:, slot * HEAD_DIM : (slot + 1) * HEAD_DIM]
+                normed = attn_ref[slot, at, :] * norm
+                pre_at(slot, at, 3)[...] = (part * normed).astype(BF)
+                part = part * gate_ref[slot, at, :]
+                gate_ref[slot, at, :] = part
+                total += jnp.sum(part * normed, axis=-1, keepdims=True)
+            sum_ref[at, :] = jnp.broadcast_to(total, (SPAN, HEAD_DIM))
+
+    gate_back(0)
+    base += 2
     copies.send(sum_ref.at[own], other_sum_ref.at[other], base, base, place.across)
+    copies.receive(nm_ref.at[other], base - 1, place.across)
+    copies.move(nm_ref, branch_out, later=True)
+    feed.middle(order[2])
+    gate_back(1)
     copies.send(sum_ref.at[other], other_sum_ref.at[own], base + 1, base + 1, place.across)
-    feed.middle(order[2])
-    copies.receive(got_ref, base - 1, place.across)
-
-    @pl.loop(0, rows // 128)
-    def _(i):
-        at = pl.ds(pl.multiple_of(i * 128, 128), 128)
-        block_ref[at, :] = (hidden_ref[at, :] + got_ref[at, :].astype(F32)).astype(BF)
-
-    for q in range(4):
-        far = pl.ds(pl.multiple_of(place.at[q] * quarter, quarter), quarter)
-        src = block_ref.at[:, pl.ds(q * quarter, quarter)]
-        copies.move(src, block_out.at[:, far], later=True)
+    copies.sent(base - 2)
+    feed.middle(order[3])
+    for load in loads:
+        load.wait()
     copies.receive(other_sum_ref.at[other], base, place.across)
     copies.receive(other_sum_ref.at[own], base + 1, place.across)
     base += 2
-    for load in loads:
-        load.wait()
 
     def slot_decay(slot):
         return decay_of(2 * lax.rem(z + slot, n_head) + core)
@@ -960,8 +961,7 @@
             device_id_type=MESH,
         )
 
-    @pl.loop(0, n_chain)
-    def _(index):
+    def chain_step(index):
         slot, seq, decay = chain_at(index)
 
         @pl.when(z < last)
@@ -980,8 +980,29 @@
             message_ref[slot, seq] = total.astype(BF)
             chain_copy(index, slot, seq).start()
 
-    feed.end(order[1])
-    feed.middle(order[3])
+    base += n_chain
+    for i in range(n_chain):
+        chain_step(i)
+        if i < spans:
+            at = pl.ds(rows + i * SPAN, SPAN)
+            send_ref[pl.ds(i * SPAN, SPAN), :] = dot_first(t_ref[2, :, at], wf_ref[2]).astype(BF)
+            if i + 1 == spans:
+                copies.send(send_ref, got_ref, base, base, place.across)
+        elif i < tiles:
+            at = pl.ds((i - spans) * SPAN, SPAN)
+            hidden_ref[at, :] += dot_first(t_ref[2, :, at], wf_ref[2])
+    copies.receive(got_ref, base, place.across)
+
+    @pl.loop(0, rows // 128)
+    def _(i):
+        at = pl.ds(pl.multiple_of(i * 128, 128), 128)
+        block_ref[at, :] = (hidden_ref[at, :] + got_ref[at, :].astype(F32)).astype(BF)
+
+    for q in range(4):
+        far = pl.ds(pl.multiple_of(place.at[q] * quarter, quarter), quarter)
+        src = block_ref.at[:, pl.ds(q * quarter, quarter)]
+        copies.move(src, block_out.at[:, far], later=True)
+    feed.end(order[1], False)
 
     offsets = iota((SPAN, SPAN), 0) - iota((SPAN, SPAN), 1)
 
@@ -1038,14 +1059,15 @@
         back_slot(slot)
         if slot + 2 < n_head:
             slot_loads[slot + 2] = late_loads(slot + 2)
-        lanes = pl.ds((slot % 2) * 4 * HEAD_DIM, 4 * HEAD_DIM)
-        holder = t_ref.at[2] if slot < 2 else wf_ref.at[0]
-        copies.move(holder.at[pl.ds(0, 2 * rows), lanes], pre_out.at[slot], later=True)
-        if slot == 1:
-            feed.end(order[2])
+        holder, start = pre_of(slot)
+        src = holder.at[pl.ds(0, 2 * rows), pl.ds(start, 4 * HEAD_DIM)]
+        copies.move(src, pre_out.at[slot], later=True)
+    feed.end(order[2], False)
+    for i, slot in enumerate(order[1:3], 1):
+        copies.move(g_view(slot, 0, None), feed_out.at[i], later=True)
     feed.end(order[3])
-    feed.total()
-    copies.move(g_view(0, 0, None), feed_out, later=True)
+    feed.total(slots=order[:1])
+    copies.move(g_view(0, 0, None), feed_out.at[0], later=True)
     copies.move(rates_ref, rates_out, later=True)
 
     @pl.when(z > 0)
@@ -1099,14 +1121,14 @@
         ((n_head, 8, HEAD_DIM), F32),
     ]
     outs = [
-        (wholes[1:], BF),
+        ((3,) + wholes[1:], BF),
         ((rows, width), BF),
         ((rows, width), F32),
         ((tall, width), BF),
         ((n_head, tall, 4 * HEAD_DIM), BF),
         ((n_head, 8, HEAD_DIM), F32),
     ]
-    n_sems = PER_SCATTER + 3 + 2 + 2 * n_head
+    n_sems = PER_SCATTER + 2 + 2 + 2 * n_head + 1
     return pl.pallas_call(
         functools.partial(middle_kernel, n_head),
         out_shape=[jax.ShapeDtypeStruct(*out) for out in outs],
@@ -1178,6 +1200,8 @@
     attn_out,
     down_out,
     rates_out,
+    piece_ref,
+    piece_high,
     feed_ref,
     attn_ref,
     down_ref,
@@ -1212,13 +1236,13 @@
 ):
     rows, width = tokens.shape
     quarter = width // 4
-    units = feed_piece.shape[1]
+    units = feed_piece.shape[2]
     spans = rows // SPAN
     place = Place(n_head)
     copies = Copies(sends, receives, locals_)
     order = (2, 1, 3, 0)
 
-    load_feed = copies.move(feed_piece, feed_ref.at[0, :, :, pl.ds(0, quarter)])
+    load_feed = [copies.move(feed_piece.at[i], piece_ref.at[i]) for i in range(3)]
     load_nin = copies.move(nin, nin_ref)
     load_pre = {slot: copies.move(pre.at[slot], pre_ref.at[slot]) for slot in order}
     load_gated = copies.move(gated, gated_ref)
@@ -1266,8 +1290,10 @@
     down_share = Share(place, copies, down_view, base + 2 * PER_SHARE)
     base += 3 * PER_SHARE
 
-    load_feed.wait()
-    feed_share.begin()
+    for i, slot in enumerate(order[1:3], 1):
+        load_feed[i].wait()
+        at = base + n_head + 3 + i - 1
+        copies.send(piece_ref.at[i], piece_high.at[i - 1], at, at, place.above(slot))
     for slot in range(1, n_head):
         into = rates_high.at[slot - 1]
         copies.send(rates.at[slot], into, base + slot, base + slot, place.above(slot))
@@ -1322,6 +1348,12 @@
 
     copies.send(send_ref, got_ref, base, base, place.across)
     middle_step(order[1])
+    middle_step(order[2])
+    load_feed[0].wait()
+    for i in range(2):
+        copies.receive(piece_high.at[i], base + n_head + 3 + i, place.up)
+    add_to(piece_ref.at[0], piece_high.at[0], piece_high.at[1], into=feed_view(0, 0, None))
+    feed_share.begin()
 
     total = rates[0]
     for slot in range(1, n_head):
@@ -1332,7 +1364,6 @@
     copies.send(rates_sum.at[0], rates_got.at[0], base, base, place.by_x)
 
     end(order[0])
-    middle_step(order[2])
     copies.receive(rates_got.at[0], base, place.by_x)
     rates_sum[1] = total + rates_got[0]
     copies.send(rates_sum.at[1], rates_got.at[1], base + 1, base + 1, place.by_y)
@@ -1406,7 +1437,7 @@
 
 def last(n_head, feed_piece, tokens, nin, branch, gated, pre, wa, hidden_grad, rates):
     rows, width = tokens.shape
-    _, units, quarter = feed_piece.shape
+    _, _, units, quarter = feed_piece.shape
     tall = 2 * rows
 
     def scatter_buffers(shape, halved):
@@ -1427,6 +1458,8 @@
         ((2, 8, HEAD_DIM), F32),
     ]
     buffers = [
+        (feed_piece.shape, BF),
+        ((2,) + feed_piece.shape[1:], BF),
         outs[1],
         outs[2],
         outs[3],
@@ -1448,7 +1481,7 @@
         ((2, 8, HEAD_DIM), F32),
         ((2, 8, HEAD_DIM), F32),
     ]
-    n_sems = 2 * PER_SCATTER + 3 * PER_SHARE + n_head + 3
+    n_sems = 2 * PER_SCATTER + 3 * PER_SHARE + n_head + 3 + 2
     return pl.pallas_call(
         functools.partial(last_kernel, n_head),
         out_shape=[jax.ShapeDtypeStruct(*out) for out in outs],
@@ -1467,6 +1500,64 @@
     )(feed_piece, tokens, nin, branch, gated, pre, wa, hidden_grad, rates)
 
 
+def finish_kernel(block, grad, feed, attn, down, rates, *refs):
+    outs, (block_ref, grad_ref, feed_ref, attn_ref, down_ref) = refs[:11], refs[11:16]
+    results, locals_ = refs[16:-1], refs[-1]
+    copies = Copies(None, None, locals_)
+    (block_out, grad_out, q_out, k_out, v_out, g_out, o_out, rates_out, l_out, r_out, d_out) = outs
+    units = feed.shape[2]
+    loads = [
+        copies.move(feed.at[side, i], feed_ref.at[side, i]) for i in range(3) for side in range(2)
+    ]
+    loads += [copies.move(attn, attn_ref), copies.move(down, down_ref)]
+    loads += [copies.move(grad, grad_ref), copies.move(block, block_ref)]
+    l_ref, r_ref, d_ref, q_ref, k_ref, v_ref, g_ref, o_ref, rates_ref = results
+    for side in range(2):
+        rates_ref[:, pl.ds(side * HEAD_DIM, HEAD_DIM)] = rates[side, pl.ds(0, 1), :]
+    copies.move(rates_ref, rates_out, later=True)
+    for i, (ref, out) in enumerate(((l_ref, l_out), (r_ref, r_out), (d_ref, d_out))):
+        for side in range(2):
+            at = pl.ds(side * units, units)
+            loads.pop(0).wait()
+            ref[at, :] = feed_ref[side, i].astype(F32)
+            copies.move(ref.at[at], out.at[at], later=True)
+    loads.pop(0).wait()
+    for i, (ref, out) in enumerate(((q_ref, q_out), (k_ref, k_out), (v_ref, v_out), (g_ref, g_out))):
+        lanes = pl.ds(i * HEAD_DIM, HEAD_DIM)
+        for side in range(2):
+            ref[:, pl.ds(side * HEAD_DIM, HEAD_DIM)] = attn_ref[side, :, lanes].astype(F32)
+        copies.move(ref, out, later=True)
+    loads.pop(0).wait()
+    for side in range(2):
+        o_ref[pl.ds(side * HEAD_DIM, HEAD_DIM), :] = down_ref[side].astype(F32)
+    copies.move(o_ref, o_out, later=True)
+    loads.pop(0).wait()
+    copies.move(grad_ref, grad_out, later=True)
+    loads.pop(0).wait()
+    copies.move(block_ref, block_out, later=True)
+    copies.finish()
+
+
+def finish(block, grad, feed, attn, down, rates):
+    _, _, units, width = feed.shape
+    projection = ((width, 2 * HEAD_DIM), F32)
+    back = ((2 * HEAD_DIM, width), F32)
+    results = [((2 * units, width), F32)] * 3 + [projection] * 4 + [back]
+    results.append(((1, 2 * HEAD_DIM), F32))
+    outs = [(block.shape, BF), (grad.shape, F32)] + results[3:] + results[:3]
+    buffers = [(block.shape, BF), (grad.shape, F32)]
+    buffers += [(a.shape, BF) for a in (feed, attn, down)] + results
+    return pl.pallas_call(
+        finish_kernel,
+        out_shape=[jax.ShapeDtypeStruct(*out) for out in outs],
+        in_specs=[ANY] * 5 + [IN_VMEM],
+        out_specs=[ANY] * len(outs),
+        scratch_shapes=[pltpu.VMEM(*b) for b in buffers] + [pltpu.SemaphoreType.DMA((48,))],
+        compiler_params=pltpu.CompilerParams(vmem_limit_bytes=62 << 20),
+        name="finish",
+    )(block, grad, feed, attn, down, rates)
+
+
 def make(n_dp, n_head):
     def on_device(
         tokens,
@@ -1481,8 +1572,7 @@
         ffn_down,
         out_grad,
     ):
-        ffn = jnp.stack([ffn_left.T, ffn_right.T, ffn_down])
-        rates_in = jnp.pad(rotation_rates.reshape(2, HEAD_DIM), ((0, 6), (0, 0)))
+        rates_in = rotation_rates.reshape(1, -1)
         (
             attn_weights,
             out_w,
@@ -1511,7 +1601,9 @@
             attn_value,
             attn_gate,
             attn_out,
-            ffn,
+            ffn_left.T,
+            ffn_right.T,
+            ffn_down,
             rates_in,
         )
         feed_piece, block_out, grad_hidden, branch_rows, grad_pre, rates_grad = middle(
@@ -1532,7 +1624,7 @@
             carry,
             scale_attn,
         )
-        input_grad, feed_grads, attn_grads, down_grads, rates_grad = last(
+        input_grad, *grads = last(
             n_head,
             feed_piece,
             tokens,
@@ -1545,32 +1637,14 @@
             rates_grad,
         )
 
-        def over_rest(grad):
-            if n_dp == 8:
-                return grad
+        results = finish(block_out, input_grad, *grads)
+        rates_grad, left_grad, right_grad = results[7][0], results[8].T, results[9].T
+        results = list(results[:7]) + [rates_grad, left_grad, right_grad, results[10]]
+        if n_dp > 8:
             groups = [[i + 8 * j for j in range(n_dp // 8)] for i in range(8)]
-            return lax.psum(grad, "dp", axis_index_groups=groups)
-
-        def projection(i):
-            halves = attn_grads[:, :, i * HEAD_DIM : (i + 1) * HEAD_DIM].astype(F32)
-            return over_rest(jnp.concatenate([halves[0], halves[1]], axis=1))
-
-        def feed(i):
-            return feed_grads[:, i].astype(F32).reshape(-1, tokens.shape[1])
-
-        return (
-            block_out,
-            input_grad,
-            projection(0),
-            projection(1),
-            projection(2),
-            projection(3),
-            over_rest(down_grads.astype(F32).reshape(-1, tokens.shape[1])),
-            over_rest(rates_grad[:, 0].reshape(-1)),
-            over_rest(feed(0).T),
-            over_rest(feed(1).T),
-            over_rest(feed(2)),
-        )
+            grads = [lax.psum(grad, "dp", axis_index_groups=groups) for grad in results[2:]]
+            results = results[:2] + grads
+        return tuple(results)
 
     return on_device
 

time: 330 us -> 290 us (0.88); the launches traced: 330 us -> 284 us
  Pallas kernels: 305 us -> 283 us
  other arithmetic: 17.3 us -> 0 us
  local copies, waits for them, and re-layouts: 6.98 us -> 0 us
    pallas_call x1, Pallas kernels: 110 us -> 81.9 us  [middle(): pl.pallas_call(functools.partial(middle_kernel, n_head), out_shape=[jax.S...]
    pallas_call x0 -> x1, Pallas kernels: none -> 10.1 us  [finish(): pl.pallas_call(finish_kernel, out_shape=[jax.ShapeDtypeStruct(*out) for o...]
    pallas_call x1, Pallas kernels: 113 us -> 103 us  [forward(): pl.pallas_call(functools.partial(forward_kernel, n_head), out_shape=[jax....]
    pallas_call x1, Pallas kernels: 82.3 us -> 87.6 us  [last(): pl.pallas_call(functools.partial(last_kernel, n_head), out_shape=[jax.Sha...]
    concatenate x4 -> x0, other arithmetic: 4.15 us -> none  [projection(): return over_rest(jnp.concatenate([halves[0], halves[1]], axis=1))]
    convert_element_type x2 -> x0, other arithmetic: 3.88 us -> none  [the longest x1 2.04 us: feed(): return feed_grads[:, i].astype(F32).reshape(-1, tokens.shape[1])]
    another operation x1 -> x0, other arithmetic: 3.75 us -> none  [on_device(): ffn = jnp.stack([ffn_left.T, ffn_right.T, ffn_down])]
    transpose x1 -> x0, other arithmetic: 3.42 us -> none  [on_device(): feed(1)]
where the time goes in v5:
time: 290 us; the launch traced here: 284 us
  Pallas kernels  283 us (98%)
    pallas_call x1, Pallas kernels, forward(): pl.pallas_call(functools.partial(forward_kernel, n_head), out_shape=[jax....  103 us
    pallas_call x1, Pallas kernels, last(): pl.pallas_call(functools.partial(last_kernel, n_head), out_shape=[jax.Sha...  87.6 us
    pallas_call x1, Pallas kernels, middle(): pl.pallas_call(functools.partial(middle_kernel, n_head), out_shape=[jax.S...  81.9 us
    pallas_call x1, Pallas kernels, finish(): pl.pallas_call(finish_kernel, out_shape=[jax.ShapeDtypeStruct(*out) for o...  10.1 us

profile of v5, /device:TPU:1, one launch (start us, length us, event | category | flops | bytes accessed | tf_op | source)
XLA Modules:
  0.0 284.0 jit_solution(2202532437576106569)
XLA Ops:
  0.6 103.2 %forward.1 = (bf16[4,1024,512]{2,1,0:T(8,128)(2,1)}, bf16[512,1024]{1,0:T(8,128)(2,1)}, bf16[3,1408,1024]{2,1,0:T(8,128)(2,1)}, bf16[1024,1024]{1,0:T(8,128)(2,1...) custom-call(bf16[512,1024]{1,0:T(8,128)(2,1)} %tokens.3, ...), custom_call_target="tpu_custom_call" | custom-call | tf_op jit(solution)/shard_map/forward/pallas_call | solution.py:600
  103.9 81.9 %middle.1 = (bf16[3,3,352,256]{3,2,1,0:T(8,128)(2,1)}, bf16[512,1024]{1,0:T(8,128)(2,1)}, f32[512,1024]{1,0:T(8,128)}, bf16[1024,1024]{1,0:T(8,128)(2,1)}, bf16[...) custom-call(bf16[3,1408,1024]{2,1,0:T(8,128)(2,1)} %get-tuple-element.51.wf, bf16[1024,1024]{1,0:T(8,128)(2,1)} %get-tuple-element.52.nm, ...), custom_call_target="tpu_custom_call" | custom-call | tf_op jit(solution)/shard_map/middle/pallas_call | solution.py:1132
  185.8 87.6 %last.1 = (f32[512,1024]{1,0:T(8,128)}, bf16[2,3,352,1024]{3,2,1,0:T(8,128)(2,1)}, bf16[2,1024,512]{2,1,0:T(8,128)(2,1)}, bf16[2,128,1024]{2,1,0:T(8,128)(2,1)}, f32[2,8,128]{2,1,0:T(8,128)}) custom-call(bf16[3,3,352,256]{3,2,1,0:T(8,128)(2,1)} %get-tuple-element.67.feed_piece, bf16[512,1024]{1,0:T(8,128)(2,1)} %tokens.3, ...), custom_call_target="tpu_custom_call" | custom-call | tf_op jit(solution)/shard_map/last/pallas_call | solution.py:1485
  273.4 10.1 %finish.1 = (bf16[512,1024]{1,0:T(8,128)(2,1)}, f32[512,1024]{1,0:T(8,128)}, f32[1024,256]{1,0:T(8,128)}, f32[1024,256]{1,0:T(8,128)}, f32[1024,256]{1,0:T(8,128...) custom-call(bf16[512,1024]{1,0:T(8,128)(2,1)} %get-tuple-element.66., ...), custom_call_target="tpu_custom_call" | custom-call | tf_op jit(solution)/shard_map/finish/pallas_call | solution.py:1550
